TPU v7x, 512 devices: a whole 4x8x8 slice. The times are simulated.
512 devices in a mesh: gx: 8 (over y), gy: 8 (over x, core), gz: 8 (over z).
Axes of the slice: x: 4, y: 8, z: 8, core: 2. Of those that a mesh axis runs over, the one named last changes fastest.
Arguments:
- right_side: float32 [64, 128, 1024], P('gx', 'gy', 'gz'), may hold values from -12 to 12
- face_coefficients: bfloat16 [3, 64, 128, 1024], P(None, 'gx', 'gy', 'gz'), may hold values from 0.25 to 4
- solid: int32 [64, 128, 1024], P('gx', 'gy', 'gz'), may hold values 0 or 1
Outputs:
- solution_field: float32 [64, 128, 1024], P('gx', 'gy', 'gz')
- residual: float32 [64, 128, 1024], P('gx', 'gy', 'gz')
- direction: float32 [64, 128, 1024], P('gx', 'gy', 'gz')
All inputs are finite; a program needn't handle non-finite values. No bound on the sum of `solid` on one device may be relied on, other than what follows from the above.
Results may differ from a plain program's by a relative error of at most 0.0003.
Values may be sent and summed in bfloat16 or wider, within the bound.
No kernel may reach another device: no remote copies, remote signals or barrier semaphores. Data moves between devices by JAX's collectives and lax.ppermute only.
A program may use at most 64 MiB of HBM per device.

v0:
```python
import jax
import jax.numpy as jnp
from jax import lax
from jax.sharding import PartitionSpec as P

LEVELS = 4
SWEEPS = 6


absorption = 0.001
relaxation = 0.8


def extended(shard, sides, width):
    for axis, dim in sides:
        peers, length = (lax.axis_size(axis), shard.shape[dim])
        up = [(i, (i + 1) % peers) for i in range(peers - 1)]
        down = [(j, i) for i, j in up]
        last = lax.slice_in_dim(shard, length - width, length, axis=dim)
        first = lax.slice_in_dim(shard, 0, width, axis=dim)
        before = lax.ppermute(last, axis, up)
        after = lax.ppermute(first, axis, down)
        shard = jnp.concatenate([before, shard, after], axis=dim)
    return shard


def stencil(padded, grid_level):
    low_faces, high_faces, diagonal = grid_level
    centre = padded[1:-1, 1:-1, 1:-1]
    result = diagonal * centre
    result = (
        result - low_faces[0] * padded[:-2, 1:-1, 1:-1] - high_faces[0] * padded[2:, 1:-1, 1:-1]
    )
    result = (
        result - low_faces[1] * padded[1:-1, :-2, 1:-1] - high_faces[1] * padded[1:-1, 2:, 1:-1]
    )
    result = (
        result - low_faces[2] * padded[1:-1, 1:-1, :-2] - high_faces[2] * padded[1:-1, 1:-1, 2:]
    )
    return result


def operate(estimate, grid_level):
    padded = extended(estimate, (("gx", 0), ("gy", 1), ("gz", 2)), 1)
    return stencil(padded, grid_level)


def keep_field(values):
    return values


def fine_faces(rimmed, starts):
    low_list = []
    high_list = []
    for dimension in range(3):
        channel = rimmed[dimension]
        centre = channel[1:-1, 1:-1, 1:-1]
        previous = channel[
            tuple((slice(0, -2) if other == dimension else slice(1, -1) for other in range(3)))
        ]
        following = channel[
            tuple((slice(2, None) if other == dimension else slice(1, -1) for other in range(3)))
        ]
        position = lax.broadcasted_iota(jnp.int32, centre.shape, dimension) + starts[dimension]
        high_list.append(jnp.sqrt(centre * following))
        low_list.append(jnp.sqrt(centre * previous) + jnp.where(position == 0, centre, 0.0))
    return (jnp.stack(low_list), jnp.stack(high_list))


def diagonal_of(low_faces, high_faces, absorb_level):
    return (
        absorb_level
        + low_faces[0]
        + high_faces[0]
        + low_faces[1]
        + high_faces[1]
        + low_faces[2]
        + high_faces[2]
    )


def blocked(values):
    size_x, size_y, size_z = values.shape
    return values.reshape(size_x // 2, 2, size_y // 2, 2, size_z // 2, 2)


def coarsen(low_faces, high_faces):
    coarse_low = jnp.stack(
        [
            0.25 * jnp.sum(blocked(low_faces[0])[:, 0], axis=(2, 4)),
            0.25 * jnp.sum(blocked(low_faces[1])[:, :, :, 0], axis=(1, 4)),
            0.25 * jnp.sum(blocked(low_faces[2])[:, :, :, :, :, 0], axis=(1, 3)),
        ]
    )
    coarse_high = jnp.stack(
        [
            0.25 * jnp.sum(blocked(high_faces[0])[:, 1], axis=(2, 4)),
            0.25 * jnp.sum(blocked(high_faces[1])[:, :, :, 1], axis=(1, 4)),
            0.25 * jnp.sum(blocked(high_faces[2])[:, :, :, :, :, 1], axis=(1, 3)),
        ]
    )
    return (coarse_low, coarse_high)


def build_levels(rimmed, starts):
    low_faces, high_faces = fine_faces(rimmed, starts)
    levels = [(low_faces, high_faces, diagonal_of(low_faces, high_faces, absorption))]
    for depth_index in range(1, LEVELS):
        low_faces, high_faces = coarsen(low_faces, high_faces)
        levels.append(
            (
                low_faces,
                high_faces,
                diagonal_of(low_faces, high_faces, absorption * 4.0**depth_index),
            )
        )
    return levels


def restrict(values):
    return 0.5 * jnp.sum(blocked(values), axis=(1, 3, 5))


def prolong(values):
    return jnp.repeat(jnp.repeat(jnp.repeat(values, 2, axis=0), 2, axis=1), 2, axis=2)


def sweeps(source, grid_level, apply_fn):
    diagonal = grid_level[2]
    estimate = relaxation * source / diagonal
    for sweep_index in range(SWEEPS - 1):
        estimate = estimate + relaxation * (source - apply_fn(estimate, grid_level)) / diagonal
    return estimate


def cycle(levels, source, depth_index, plan):
    operators, descend, ascend, coarse_plan = plan
    grid_level = levels[depth_index]
    if depth_index == len(levels) - 1:
        return coarse_plan(source)
    apply_fn = operators[depth_index]
    diagonal = grid_level[2]
    smoothed = relaxation * source / diagonal
    leftover = source - apply_fn(smoothed, grid_level)
    coarse = cycle(levels, descend[depth_index + 1](restrict(leftover)), depth_index + 1, plan)
    corrected = smoothed + prolong(ascend[depth_index + 1](coarse))
    return corrected + relaxation * (source - apply_fn(corrected, grid_level)) / diagonal


def local(right_side, face_coefficients, solid):
    weight = 1.0 - 0.75 * solid.astype(jnp.float32)
    conductance = (face_coefficients.astype(jnp.float32) * weight[None]).astype(jnp.bfloat16)
    rimmed = extended(conductance, (("gx", 1), ("gy", 2), ("gz", 3)), 1)
    rimmed = rimmed.astype(jnp.float32)
    size_x, size_y, size_z = right_side.shape
    starts = (
        lax.axis_index("gx") * size_x,
        lax.axis_index("gy") * size_y,
        lax.axis_index("gz") * size_z,
    )
    levels = build_levels(rimmed, starts)
    plain_ops = [operate] * LEVELS
    plain_moves = [keep_field] * LEVELS

    def coarse_plan(source):
        return sweeps(source, levels[-1], operate)

    plan = (plain_ops, plain_moves, plain_moves, coarse_plan)
    first_pre = cycle(levels, right_side, 0, plan)
    projected = lax.psum(jnp.sum(right_side * first_pre), ("gx", "gy", "gz"))
    image_field = operate(first_pre, levels[0])
    curvature = lax.psum(jnp.sum(first_pre * image_field), ("gx", "gy", "gz"))
    step_size = projected / curvature
    solution_field = step_size * first_pre
    residual = right_side - step_size * image_field
    next_pre = cycle(levels, residual, 0, plan)
    momentum = lax.psum(jnp.sum(residual * next_pre), ("gx", "gy", "gz")) / projected
    direction = next_pre + momentum * first_pre
    return (solution_field, residual, direction)


def solution(mesh):
    placed = (P("gx", "gy", "gz"), P(None, "gx", "gy", "gz"), P("gx", "gy", "gz"))
    return jax.shard_map(
        local,
        mesh=mesh,
        in_specs=placed,
        out_specs=(P("gx", "gy", "gz"), P("gx", "gy", "gz"), P("gx", "gy", "gz")),
        check_vma=False,
    )
```

profile of v0, /device:TPU:1, one launch (start us, length us, event | category | flops | bytes accessed | tf_op | source)
XLA Modules:
  0.0 874.8 jit_solution(2869606260574111170)
XLA Ops:
  9.3 9.2 %collective-permute-start.3 = (bf16[3,10,1,128]{3,0,2,1:T(4,128)(2,1)S(1)}, bf16[3,10,1,128]{3,0,2,1:T(4,128)(2,1)S(1)}, u32[]{:S(2)}, u32[]{:S(2)}) collective-permute-start(bf16[3,10,1,128]{3,0,2,1:T(4,128)(2,1)S(1)} %copy.385), channel_id=1, source_target_pairs={{8,0},{16,8},{24,16},{32,24},{40,32},{48,40},{56,48},{9,1},{17,9},... | collective-permute-start | bytes 23048 | tf_op jit(solution)/shard_map/ppermute | solution.py:22
  166.8 5.9 collective-permute-start.28
  183.0 5.9 collective-permute-start.32
  191.0 5.7 collective-permute-start.34
  207.0 5.9 collective-permute-start.38
  222.6 5.8 collective-permute-start.42
  231.0 5.9 collective-permute-start.44
  239.0 5.8 collective-permute-start.46
  255.3 5.9 collective-permute-start.50
  263.3 5.7 collective-permute-start.52
  271.4 5.7 collective-permute-start.54
  279.7 5.9 collective-permute-start.56
  287.7 5.7 collective-permute-start.58
  296.0 5.7 collective-permute-start.60
  302.5 5.9 collective-permute-start.62
  341.8 5.8 collective-permute-start.70
  359.5 5.7 collective-permute-start.74
  367.4 5.8 collective-permute-start.76
  375.8 111.4 %all-reduce = (f32[]{:T(128)}, f32[]{:T(128)}) all-reduce(f32[]{:T(128)} %get-tuple-element.16, f32[]{:T(128)} %get-tuple-element.15), channel_id=1, replica_groups=mesh['gx'=8,'gy'=8,'gz'=8] {'gx','gy','gz'}, use_global_device_ids=true, to_apply=%region_23.24 | all-reduce | flops 2 | bytes 16 | tf_op jit(solution)/shard_map/psum | solution.py:170
  595.9 5.9 collective-permute-start.104
  618.7 5.9 collective-permute-start.110
  642.6 5.9 collective-permute-start.116
  650.6 5.8 collective-permute-start.118
  658.5 5.7 collective-permute-start.120
  666.9 5.9 collective-permute-start.122
  674.8 5.7 collective-permute-start.124
  691.3 5.9 collective-permute-start.128
  699.3 5.7 collective-permute-start.130
  707.6 5.7 collective-permute-start.132
  714.0 5.9 collective-permute-start.134
  753.3 5.8 collective-permute-start.142
  761.8 110.9 %psum.23 = f32[]{:T(128)} all-reduce(f32[]{:T(128)} %get-tuple-element.19), channel_id=1, replica_groups=mesh['gx'=8,'gy'=8,'gz'=8] {'gx','gy','gz'}, use_global_device_ids=true, to_apply=%region_31.32 | all-reduce | flops 1 | bytes 8 | tf_op jit(solution)/shard_map/psum | solution.py:177
  (498 shorter events, 468.8 us)
Async XLA Ops:
  9.3 11.2 %collective-permute-start.3 = (bf16[3,10,1,128]{3,0,2,1:T(4,128)(2,1)S(1)}, bf16[3,10,1,128]{3,0,2,1:T(4,128)(2,1)S(1)}, u32[]{:S(2)}, u32[]{:S(2)}) collective-permute-start(bf16[3,10,1,128]{3,0,2,1:T(4,128)(2,1)S(1)} %copy.385), channel_id=1, source_target_pairs={{8,0},{16,8},{24,16},{32,24},{40,32},{48,40},{56,48},{9,1},{17,9},... | collective-permute-start | bytes 23048 | tf_op jit(solution)/shard_map/ppermute | solution.py:22
  21.9 8.0 collective-permute-start.5
  23.2 7.5 collective-permute-start.4
  42.4 22.1 %collective-permute-start.7 = (f32[1,16,128]{2,1,0:T(8,128)S(1)}, f32[1,16,128]{2,1,0:T(8,128)S(1)}, u32[]{:S(2)}, u32[]{:S(2)}) collective-permute-start(f32[1,16,128]{2,1,0:T(8,128)S(1)} %get-tuple-element.73), channel_id=1, source_target_pairs={{64,0},{128,64},{192,128},{256,192},{320,256},{384,320},{448,384},... | collective-permute-start | bytes 24584 | tf_op jit(solution)/shard_map/ppermute | solution.py:22
  43.7 20.8 %collective-permute-start.6 = (f32[1,16,128]{2,1,0:T(8,128)S(1)}, f32[1,16,128]{2,1,0:T(8,128)S(1)}, u32[]{:S(2)}, u32[]{:S(2)}) collective-permute-start(f32[1,16,128]{2,1,0:T(8,128)S(1)} %get-tuple-element.72), channel_id=1, source_target_pairs={{0,64},{64,128},{128,192},{192,256},{256,320},{320,384},{384,448},... | collective-permute-start | bytes 24584 | tf_op jit(solution)/shard_map/ppermute | solution.py:21
  64.5 20.0 %collective-permute-start.9 = (f32[10,1,128]{2,1,0:T(1,128)S(1)}, f32[10,1,128]{2,1,0:T(1,128)S(1)}, u32[]{:S(2)}, u32[]{:S(2)}) collective-permute-start(f32[10,1,128]{2,1,0:T(1,128)S(1)} %get-tuple-element.61), channel_id=1, source_target_pairs={{8,0},{16,8},{24,16},{32,24},{40,32},{48,40},{56,48},{9,1},{17,9},... | collective-permute-start | bytes 15368 | tf_op jit(solution)/shard_map/ppermute | solution.py:22
  68.0 16.5 %collective-permute-start.8 = (f32[10,1,128]{2,1,0:T(1,128)S(1)}, f32[10,1,128]{2,1,0:T(1,128)S(1)}, u32[]{:S(2)}, u32[]{:S(2)}) collective-permute-start(f32[10,1,128]{2,1,0:T(1,128)S(1)} %get-tuple-element.60), channel_id=1, source_target_pairs={{0,8},{8,16},{16,24},{24,32},{32,40},{40,48},{48,56},{1,9},{9,17},... | collective-permute-start | bytes 15368 | tf_op jit(solution)/shard_map/ppermute | solution.py:21
  84.7 9.1 %collective-permute-start.11 = (f32[10,18,1]{2,1,0:T(8,128)S(1)}, f32[10,18,1]{2,1,0:T(8,128)S(1)}, u32[]{:S(2)}, u32[]{:S(2)}) collective-permute-start(f32[10,18,1]{2,1,0:T(8,128)S(1)} %get-tuple-element.47), channel_id=1, source_target_pairs={{1,0},{2,1},{3,2},{4,3},{5,4},{6,5},{7,6},{9,8},{10,9},{11,10},{12... | collective-permute-start | bytes 2168 | tf_op jit(solution)/shard_map/ppermute | solution.py:22
  86.0 7.8 collective-permute-start.10
  102.1 9.0 %collective-permute-start.13 = (f32[1,8,64]{2,1,0:T(8,128)S(1)}, f32[1,8,64]{2,1,0:T(8,128)S(1)}, u32[]{:S(2)}, u32[]{:S(2)}) collective-permute-start(f32[1,8,64]{2,1,0:T(8,128)S(1)} %get-tuple-element.120), channel_id=1, source_target_pairs={{64,0},{128,64},{192,128},{256,192},{320,256},{384,320},{448,384},... | collective-permute-start | bytes 6152 | tf_op jit(solution)/shard_map/ppermute | solution.py:22
  103.4 7.7 collective-permute-start.12
  156.9 7.8 collective-permute-start.27
  181.1 7.8 collective-permute-start.33
  205.1 7.8 collective-permute-start.39
  229.1 7.8 collective-permute-start.45
  253.3 7.8 collective-permute-start.51
  277.8 7.8 collective-permute-start.57
  302.5 7.8 collective-permute-start.62
  340.5 7.4 collective-permute-start.71
  341.8 7.7 collective-permute-start.70
  357.5 7.7 collective-permute-start.75
  366.1 7.4 collective-permute-start.77
  367.4 7.6 collective-permute-start.76
  571.5 8.1 collective-permute-start.99
  594.0 7.8 collective-permute-start.105
  616.8 7.8 collective-permute-start.111
  640.6 7.8 collective-permute-start.117
  664.9 7.8 collective-permute-start.123
  689.4 7.8 collective-permute-start.129
  714.0 7.8 collective-permute-start.134
  752.0 7.4 collective-permute-start.143
  753.3 7.8 collective-permute-start.142
  (114 other events, 994.5 us)
where the time goes:
time: 879 us; the launch traced here: 875 us
  starting transfers between devices  487 us (55%)
  blocking collectives  222 us (25%)
  waiting for transfers between devices  80.9 us (9%)
  local copies, waits for them, and re-layouts  53 us (6%)
  other arithmetic  25.4 us (3%)
    ppermute x72, starting transfers between devices, extended(): before = lax.ppermute(last, axis, up)  367 us
    ppermute x72, starting transfers between devices, extended(): after = lax.ppermute(first, axis, down)  120 us
    psum x1, blocking collectives, local(): projected = lax.psum(jnp.sum(right_side * first_pre), ('gx', 'gy', 'gz'))  111 us
    psum x1, blocking collectives, local(): lax.psum(jnp.sum(residual * next_pre), ('gx', 'gy', 'gz')) / projected  111 us
    ppermute x72, waiting for transfers between devices, extended(): before = lax.ppermute(last, axis, up)  46.3 us
    ppermute x72, waiting for transfers between devices, extended(): after = lax.ppermute(first, axis, down)  34.6 us
    another operation x6, local copies, waits for them, and re-layouts, blocked(): return values.reshape(size_x // 2, 2, size_y // 2, 2, size_z // 2, 2)  33.2 us
  transfers between devices with their start and end apart: 144, of which 72 were waited for; matrix products, arithmetic and copies ran while one was open for 4% of the time, Pallas kernels for 0%

commit v1 on v0

v1 whole, which is shorter than its diff:
```python
import functools

import jax
import jax.numpy as jnp
from jax import lax
from jax.experimental import pallas as pl
from jax.experimental.pallas import tpu as pltpu
from jax.sharding import PartitionSpec as P

F32 = jnp.float32
BF16 = jnp.bfloat16
ABSORB = 0.001
RELAX = 0.8
KEEP = 0.2
SWEEPS = 6
VMEM_LIMIT = 24 * 1024 * 1024


def one_hot(rows, cols, rule, weight=1.0):
    r = lax.broadcasted_iota(jnp.int32, (rows, cols), 0)
    c = lax.broadcasted_iota(jnp.int32, (rows, cols), 1)
    return jnp.where(rule(r, c), weight, 0.0).astype(BF16)


def spread(values, matrix):
    high = values.astype(BF16)
    low = (values - high.astype(F32)).astype(BF16)
    return jnp.dot(high, matrix, preferred_element_type=F32) + jnp.dot(
        low, matrix, preferred_element_type=F32
    )


def pick(matrix, values):
    high = values.astype(BF16)
    low = (values - high.astype(F32)).astype(BF16)
    return jnp.dot(matrix, high, preferred_element_type=F32) + jnp.dot(
        matrix, low, preferred_element_type=F32
    )


def turn(values, shift, axis):
    return pltpu.roll(values, shift % values.shape[axis], axis)


def iota(shape, dim):
    return lax.broadcasted_iota(jnp.int32, shape, dim)


def plane_terms(v, f1, f2):
    return turn(v, 1, 0) * f1 + turn(v * f1, -1, 0) + turn(v, 1, 1) * f2 + turn(v * f2, -1, 1)


def neighbours(v_ref, f0_ref, f1_ref, f2_ref, p):
    return (
        f0_ref[p] * v_ref[p - 1]
        + f0_ref[p + 1] * v_ref[p + 1]
        + plane_terms(v_ref[p], f1_ref[p], f2_ref[p])
    )


def neighbours_3d(v, f0, f1, f2):
    zero = jnp.zeros_like(v[:1])
    up = f0 * v
    return (
        f0 * jnp.concatenate([zero, v[:-1]], 0)
        + jnp.concatenate([up[1:], zero], 0)
        + turn(v, 1, 1) * f1
        + turn(v * f1, -1, 1)
        + turn(v, 1, 2) * f2
        + turn(v * f2, -1, 2)
    )


def row_pairs(t_ref, values, both):
    out = []
    for half in range(2):
        t_ref[half] = values[:, 128 * half : 128 * half + 128]
        first = t_ref[half, pl.ds(0, 20, 2), :]
        out.append(first + t_ref[half, pl.ds(1, 20, 2), :] if both else first)
    return out


def put_rows(r_ref, q, halves):
    for half in range(2):
        r_ref[q, pl.ds(0, 20), pl.ds(128 * half, 128)] = halves[half]


def prepare_kernel(s_ref, fc_ref, solid_ref, out_ref):
    s = s_ref[...]
    high = s.astype(BF16)
    out_ref[:, 0] = high
    out_ref[:, 1] = (s - high.astype(F32)).astype(BF16)
    weight = 1.0 - 0.75 * solid_ref[...].astype(F32)
    for a in range(3):
        out_ref[:, 2 + a] = (fc_ref[a].astype(F32) * weight).astype(BF16)


def rim_kernel(own_ref, before_ref, after_ref, out_ref):
    lane = iota((16, 128), 1)

    def body(p, carry):
        rim = jnp.zeros((16, 128), F32)
        for f in range(5):
            out_ref[p, f] = own_ref[p, f]
            t = jnp.where(lane < 64, after_ref[p, f].astype(F32), before_ref[p, f].astype(F32))
            t = turn(t, 24 * f + 12, 1)
            rim = jnp.where((lane >= 24 * f) & (lane < 24 * f + 24), t, rim)
        out_ref[p, 5] = rim.astype(BF16)
        return carry

    lax.fori_loop(0, 8, body, 0)


def first_kernel(
    x_ref, ym_ref, yp_ref,
    s_ref, f0_ref, f1_ref, f2_ref, w_ref, d_ref,
    s1_ref, f10_ref, f11_ref, f12_ref, w1_ref, pay_ref,
    c0_ref, c1_ref, c2_ref, sm_ref, t_ref, r0_ref, r1_ref, r2_ref, rs_ref,
    l10_ref, l11_ref, l12_ref, sm1_ref, t1_ref, u_ref,
):
    at_x = lax.axis_index("gx") == 0
    at_y = lax.axis_index("gy") == 0
    at_z = lax.axis_index("gz") == 0
    lane = iota((40, 128), 1)
    side = (lane < 12) | (lane >= 116)

    def unpack(p, carry):
        tiles = []
        for f in range(6):
            column = jnp.concatenate(
                [ym_ref[p, f].astype(F32), x_ref[p, f].astype(F32), yp_ref[p, f].astype(F32)], 0
            )
            tiles.append(turn(column, -4, 0)[:40])
        rims = [
            jnp.where(side, turn(tiles[5], -(24 * f + 12), 1), 0.0) for f in range(5)
        ]
        s_ref[p, :, 0:128] = tiles[0] + tiles[1]
        s_ref[p, :, 128:256] = rims[0] + rims[1]
        for a, c_ref in enumerate((c0_ref, c1_ref, c2_ref)):
            c_ref[p, :, 0:128] = tiles[2 + a]
            c_ref[p, :, 128:256] = rims[2 + a]
        return carry

    lax.fori_loop(0, 32, unpack, 0)

    def faces(p, carry):
        before = jnp.maximum(p - 1, 0)
        f0_ref[p] = jnp.sqrt(c0_ref[p] * c0_ref[before])
        c1 = c1_ref[p]
        f1_ref[p] = jnp.sqrt(c1 * turn(c1, 1, 0))
        c2 = c2_ref[p]
        f2_ref[p] = jnp.sqrt(c2 * turn(c2, 1, 1))
        return carry

    lax.fori_loop(0, 32, faces, 0)
    f0_ref[32] = jnp.zeros((40, 256), F32)

    first_row = (iota((40, 256), 0) == 12) & at_y
    first_lane = (iota((40, 256), 1) == 0) & at_z
    for ref in (r0_ref, r1_ref, r2_ref, rs_ref):
        ref[...] = jnp.zeros_like(ref)

    def diagonals(q, carry):
        lows = []
        for i in range(2):
            p = 2 * q + i
            f0, f1, f2 = f0_ref[p], f1_ref[p], f2_ref[p]
            low0 = f0 + jnp.where((p == 12) & at_x, c0_ref[p], 0.0)
            low1 = f1 + jnp.where(first_row, c1_ref[p], 0.0)
            low2 = f2 + jnp.where(first_lane, c2_ref[p], 0.0)
            d = ABSORB + low0 + f0_ref[p + 1] + low1 + turn(f1, -1, 0) + low2 + turn(f2, -1, 1)
            w = RELAX / d
            d_ref[p] = d
            w_ref[p] = w
            sm_ref[p] = w * s_ref[p]
            lows.append((low0, low1, low2))
        put_rows(r0_ref, q, row_pairs(t_ref, lows[0][0], True))
        put_rows(r1_ref, q, row_pairs(t_ref, lows[0][1] + lows[1][1], False))
        put_rows(r2_ref, q, row_pairs(t_ref, lows[0][2] + lows[1][2], True))
        return carry

    lax.fori_loop(0, 16, diagonals, 0)

    def leftovers(q, carry):
        total = jnp.zeros((40, 256), F32)
        for i in range(2):
            p = 2 * q + i
            total += KEEP * s_ref[p] + neighbours(sm_ref, f0_ref, f1_ref, f2_ref, p)
        put_rows(rs_ref, q, row_pairs(t_ref, total, True))
        return carry

    lax.fori_loop(1, 15, leftovers, 0)

    pairs = one_hot(256, 128, lambda r, c: lax.shift_right_logical(r, 1) == c, 0.25)
    evens = one_hot(256, 128, lambda r, c: r == 2 * c, 0.25)
    l10_ref[pl.ds(0, 16)] = spread(r0_ref[...].reshape(384, 256), pairs).reshape(16, 24, 128)
    l11_ref[...] = spread(r1_ref[...].reshape(384, 256), pairs).reshape(16, 24, 128)
    l12_ref[...] = spread(r2_ref[...].reshape(384, 256), evens).reshape(16, 24, 128)
    s1_ref[...] = 2.0 * spread(rs_ref[...].reshape(384, 256), pairs).reshape(16, 24, 128)
    l10_ref[16] = jnp.zeros((24, 128), F32)

    first_row_1 = (iota((24, 128), 0) == 6) & at_y
    first_lane_1 = (iota((24, 128), 1) == 0) & at_z

    def faces_1(p, carry):
        f10_ref[p] = jnp.where((p == 6) & at_x, 0.0, l10_ref[p])
        f11_ref[p] = jnp.where(first_row_1, 0.0, l11_ref[p])
        f12_ref[p] = jnp.where(first_lane_1, 0.0, l12_ref[p])
        return carry

    lax.fori_loop(0, 16, faces_1, 0)
    f10_ref[16] = jnp.zeros((24, 128), F32)

    def diagonals_1(p, carry):
        d = (
            4.0 * ABSORB + l10_ref[p] + f10_ref[p + 1]
            + l11_ref[p] + turn(f11_ref[p], -1, 0)
            + l12_ref[p] + turn(f12_ref[p], -1, 1)
        )
        w = RELAX / d
        w1_ref[p] = w
        sm1_ref[p] = w * s1_ref[p]
        return carry

    lax.fori_loop(0, 16, diagonals_1, 0)

    def quad(values, both):
        t1_ref[...] = values
        first = t1_ref[pl.ds(6, 4, 2), :]
        return first + t1_ref[pl.ds(7, 4, 2), :] if both else first

    def leftover_1(p):
        return KEEP * s1_ref[p] + neighbours(sm1_ref, f10_ref, f11_ref, f12_ref, p)

    total = jnp.zeros((8, 128), F32)
    for f in range(4):
        for i in range(2):
            p = 6 + 2 * i
            if f == 0:
                part = quad(leftover_1(p) + leftover_1(p + 1), True)
            elif f == 1:
                part = quad(l10_ref[p], True)
            elif f == 2:
                part = quad(l11_ref[p] + l11_ref[p + 1], False)
            else:
                part = quad(l12_ref[p] + l12_ref[p + 1], True)
            u_ref[pl.ds(4 * i, 4), :] = part
        place = one_hot(
            128, 128,
            lambda r, c, f=f: (
                ((lax.shift_right_logical(r, 1) + 32 * f == c) if f < 3 else (r + 192 == 2 * c))
                & (r < 64)
            ),
            0.5 if f == 0 else 0.25,
        )
        total += spread(u_ref[...], place)
    pay_ref[...] = total


def solve_2(s2, level_2, level_3, t3_ref, e_ref):
    f0, f1, f2, w = level_2
    g0, g1, g2, w3 = level_3
    nx, ny, _ = s2.shape
    sm = w * s2
    left = KEEP * s2 + neighbours_3d(sm, f0, f1, f2)
    s3 = coarse_2(left.reshape(nx // 2, 2, ny, 128).sum(1), t3_ref, True, 0.5, False)
    e = w3 * s3
    for _ in range(SWEEPS - 1):
        e = KEEP * e + w3 * (s3 + neighbours_3d(e, g0, g1, g2))
    widen = one_hot(128, 128, lambda r, c: (r == lax.shift_right_logical(c, 1)) & (c < 64))
    wide = spread(e.reshape(nx * ny // 4, 128), widen).reshape(nx // 2, ny // 2, 128)
    for x in range(nx // 2):
        for i in range(2):
            e_ref[x, pl.ds(i, ny // 2, 2), :] = wide[x]
    e2 = e_ref[...]
    corrected = sm + jnp.concatenate([e2[:, None], e2[:, None]], 1).reshape(nx, ny, 128)
    return KEEP * corrected + w * (s2 + neighbours_3d(corrected, f0, f1, f2))


def coarse_2(values, t3_ref, both, weight, even):
    nx, ny, _ = values.shape
    t3_ref[...] = values
    first = t3_ref[:, pl.ds(0, ny // 2, 2), :]
    if both:
        first = first + t3_ref[:, pl.ds(1, ny // 2, 2), :]
    if even:
        rule = lambda r, c: (r == 2 * c) & (r < 64)
    else:
        rule = lambda r, c: (lax.shift_right_logical(r, 1) == c) & (r < 64)
    flat = spread(first.reshape(nx * ny // 2, 128), one_hot(128, 128, rule, weight))
    return flat.reshape(nx, ny // 2, 128)


def coefficients(low, mask_lane, absorb):
    shape = low[0].shape
    f0 = jnp.where(iota(shape, 0) == 0, 0.0, low[0])
    f1 = jnp.where(iota(shape, 1) == 0, 0.0, low[1])
    f2 = jnp.where((iota(shape, 2) == mask_lane) & (lax.axis_index("gz") == 0), 0.0, low[2])
    d = (
        absorb + low[0] + jnp.concatenate([f0[1:], jnp.zeros_like(f0[:1])], 0)
        + low[1] + turn(f1, -1, 1) + low[2] + turn(f2, -1, 2)
    )
    return f0, f1, f2, RELAX / d


def fetch_level_2(m2_ref, planes, pick_ref):
    gx, gy = lax.axis_index("gx"), lax.axis_index("gy")
    ny = m2_ref.shape[1]

    def source(c):
        return jnp.where(c < 96, 16, -48) + lax.shift_right_logical(c, 1)

    widen = one_hot(128, 128, lambda r, c: r == source(c))
    rows = one_hot(24, ny, lambda r, c: c == 4 * gy - 3 + lax.shift_right_logical(r, 1))
    for k in planes:
        pick_ref[k] = spread(pick(rows, m2_ref[2 * gx + k]), widen)


def widen_level_1(m1_ref, wide_ref, lo, hi):
    rows = 24 * (hi - lo)
    widen = one_hot(128, 256, lambda r, c: r == lax.shift_right_logical(c, 1))
    wide_ref[pl.ds(lo, hi - lo)] = spread(m1_ref[pl.ds(lo, hi - lo)].reshape(rows, 128), widen).reshape(
        hi - lo, 24, 256
    )


def double_rows(t_ref, wide_ref, q):
    for half in range(2):
        part = wide_ref[q, pl.ds(0, 20), pl.ds(128 * half, 128)]
        for i in range(2):
            t_ref[half, pl.ds(i, 20, 2), :] = part
    return jnp.concatenate([t_ref[0], t_ref[1]], 1)


def second_kernel(
    s_ref, f0_ref, f1_ref, f2_ref, w_ref, d_ref,
    s1_ref, f10_ref, f11_ref, f12_ref, w1_ref,
    own_ref, before_ref, after_ref,
    fp_out, im_out, im_ref, t1s_ref, f20_ref, f21_ref, f22_ref, w2_ref,
    f30_ref, f31_ref, f32_ref, w3_ref, pay_ref,
    v_ref, t3_ref, e_ref, m2_ref, pick_ref, corr1_ref, m1_ref, wide_ref, t_ref,
    corr_ref, fp_ref, sm_ref, rs_ref, sm1_ref, tq_ref,
):
    nx2, ny2 = f20_ref.shape[:2]
    lane8 = iota((8, 128), 1)
    row8 = iota((8, 128), 0)

    def assemble(x, carry):
        for pair in range(ny2 // 8):
            for f in range(4):
                tiles = []
                for j in range(2):
                    g = x * (ny2 // 4) + 2 * pair + j
                    t = jnp.where(
                        lane8 < 16,
                        turn(before_ref[g], -(32 * f + 16), 1),
                        jnp.where(
                            lane8 < 48,
                            turn(own_ref[g], 16 - 32 * f, 1),
                            turn(after_ref[g], 48 - 32 * f, 1),
                        ),
                    )
                    tiles.append(jnp.where(lane8 < 64, t, 0.0))
                rows = pl.ds(8 * pair, 8)
                v_ref[f, 2 * x, rows, :] = jnp.where(row8 < 4, tiles[0], turn(tiles[1], 4, 0))
                v_ref[f, 2 * x + 1, rows, :] = jnp.where(row8 < 4, turn(tiles[0], 4, 0), tiles[1])
        return carry

    lax.fori_loop(0, nx2 // 2, assemble, 0)

    s2 = v_ref[0]
    low = (v_ref[1], v_ref[2], v_ref[3])
    level_2 = coefficients(low, 16, 16.0 * ABSORB)
    f20_ref[...], f21_ref[...], f22_ref[...], w2_ref[...] = level_2
    halves = [t.reshape(nx2 // 2, 2, ny2, 128) for t in low]
    low_3 = (
        coarse_2(halves[0][:, 0], t3_ref, True, 0.25, False),
        coarse_2(halves[1].sum(1), t3_ref, False, 0.25, False),
        coarse_2(halves[2].sum(1), t3_ref, True, 0.25, True),
    )
    level_3 = coefficients(low_3, 8, 64.0 * ABSORB)
    f30_ref[...], f31_ref[...], f32_ref[...], w3_ref[...] = level_3
    m2_ref[...] = jnp.zeros_like(m2_ref)
    m2_ref[pl.ds(3, nx2)] = solve_2(s2, level_2, level_3, t3_ref, e_ref)
    fetch_level_2(m2_ref, range(8), pick_ref)

    def correct_1(p, carry):
        corr1_ref[p] = w1_ref[p] * s1_ref[p] + pick_ref[lax.shift_right_logical(p, 1)]
        return carry

    lax.fori_loop(0, 16, correct_1, 0)

    def relax_1(p, carry):
        m1_ref[p] = KEEP * corr1_ref[p] + w1_ref[p] * (
            s1_ref[p] + neighbours(corr1_ref, f10_ref, f11_ref, f12_ref, p)
        )
        return carry

    lax.fori_loop(2, 14, relax_1, 0)
    widen_level_1(m1_ref, wide_ref, 2, 14)

    def correct(q, carry):
        e = double_rows(t_ref, wide_ref, q)
        for i in range(2):
            p = 2 * q + i
            corr_ref[p] = w_ref[p] * s_ref[p] + e
        return carry

    lax.fori_loop(2, 14, correct, 0)

    def relax(p, carry):
        fp_ref[p] = KEEP * corr_ref[p] + w_ref[p] * (
            s_ref[p] + neighbours(corr_ref, f0_ref, f1_ref, f2_ref, p)
        )
        return carry

    lax.fori_loop(6, 26, relax, 0)

    def image(p, carry):
        im = d_ref[p] * fp_ref[p] - neighbours(fp_ref, f0_ref, f1_ref, f2_ref, p)
        im_ref[p] = im
        sm_ref[p] = w_ref[p] * im
        return carry

    lax.fori_loop(7, 25, image, 0)

    rs_ref[...] = jnp.zeros_like(rs_ref)
    inside = (iota((40, 128), 0) >= 12) & (iota((40, 128), 0) < 28)

    def leftovers(q, sums):
        total = jnp.zeros((40, 256), F32)
        for i in range(2):
            p = 2 * q + i
            left = KEEP * im_ref[p] + neighbours(sm_ref, f0_ref, f1_ref, f2_ref, p)
            total += left
            own = jnp.where(inside & (p >= 12) & (p < 20), 1.0, 0.0)
            fp, im = fp_ref[p, :, 0:128], im_ref[p, :, 0:128]
            sums = (
                sums[0] + own * s_ref[p, :, 0:128] * fp,
                sums[1] + own * fp * im,
                sums[2] + own * sm_ref[p, :, 0:128] * (im + left[:, 0:128]),
            )
        put_rows(rs_ref, q - 4, row_pairs(t_ref, total, True))
        return sums

    zero = jnp.zeros((40, 128), F32)
    sums = lax.fori_loop(4, 12, leftovers, (zero, zero, zero))

    for p in range(8):
        fp_out[p] = fp_ref[12 + p, pl.ds(12, 16), 0:128]
        im_out[p] = im_ref[12 + p, pl.ds(12, 16), 0:128]

    pairs = one_hot(256, 128, lambda r, c: lax.shift_right_logical(r, 1) == c, 0.5)
    t1s_ref[...] = jnp.zeros_like(t1s_ref)
    t1s_ref[pl.ds(4, 8)] = spread(rs_ref[...].reshape(192, 256), pairs).reshape(8, 24, 128)
    for p in range(5, 11):
        sm1_ref[p] = w1_ref[p] * t1s_ref[p]
    inside_1 = jnp.where(
        (iota((24, 128), 0) >= 6) & (iota((24, 128), 0) < 14) & (iota((24, 128), 1) < 64), 1.0, 0.0
    )
    second = jnp.zeros((24, 128), F32)
    pay = jnp.zeros((8, 128), F32)
    tq_ref[...] = jnp.zeros_like(tq_ref)
    for i in range(2):
        total = jnp.zeros((24, 128), F32)
        for j in range(2):
            p = 6 + 2 * i + j
            s1 = t1s_ref[p]
            left = KEEP * s1 + neighbours(sm1_ref, f10_ref, f11_ref, f12_ref, p)
            second += inside_1 * sm1_ref[p] * (s1 + left)
            total += left
        tq_ref[pl.ds(0, 24), :] = total
        tq_ref[pl.ds(24, 4), :] = tq_ref[pl.ds(6, 4, 2), :] + tq_ref[pl.ds(7, 4, 2), :]
        place = one_hot(
            128, 128,
            lambda r, c, i=i: (lax.shift_right_logical(r, 1) + 32 * i == c) & (r < 64), 0.5,
        )
        pay += spread(tq_ref[pl.ds(24, 8), :], place)
    scalars = (jnp.sum(sums[0]), jnp.sum(sums[1]), jnp.sum(sums[2]) + 2.0 * jnp.sum(second))
    for k, value in enumerate(scalars):
        pay = jnp.where((lane8 == 64 + k) & (row8 == 0), value, pay)
    pay_ref[...] = pay[:4]


def third_kernel(
    f0_ref, f1_ref, f2_ref, w_ref, f10_ref, f11_ref, f12_ref, w1_ref,
    im_ref, t1s_ref, f20_ref, f21_ref, f22_ref, w2_ref, f30_ref, f31_ref, f32_ref, w3_ref,
    own_ref, before_ref, after_ref,
    mi_out, scalar_out,
    v_ref, t3_ref, e_ref, m2_ref, pick_ref, corr1_ref, m1_ref, wide_ref, t_ref, corr_ref,
):
    nx2, ny2 = f20_ref.shape[:2]
    lane8 = iota((8, 128), 1)

    def assemble(x, acc):
        for pair in range(ny2 // 8):
            g = x * (ny2 // 8) + pair
            acc = acc + own_ref[g]
            for i in range(2):
                t = jnp.where(
                    lane8 < 16,
                    turn(before_ref[g], -(32 * i + 16), 1),
                    jnp.where(
                        lane8 < 48,
                        turn(own_ref[g], 16 - 32 * i, 1),
                        turn(after_ref[g], 48 - 32 * i, 1),
                    ),
                )
                v_ref[2 * x + i, pl.ds(8 * pair, 8), :] = jnp.where(lane8 < 64, t, 0.0)
        return acc

    acc = lax.fori_loop(0, nx2 // 2, assemble, jnp.zeros((8, 128), F32))
    s2 = v_ref[...]
    level_2 = (f20_ref[...], f21_ref[...], f22_ref[...], w2_ref[...])
    level_3 = (f30_ref[...], f31_ref[...], f32_ref[...], w3_ref[...])
    m2 = solve_2(s2, level_2, level_3, t3_ref, e_ref)
    lane3 = iota(s2.shape, 2)
    part = 4.0 * jnp.sum(jnp.where((lane3 >= 16) & (lane3 < 48), s2 * m2, 0.0))
    sums = jnp.sum(acc, axis=0, keepdims=True)
    scalar_out[...] = jnp.where(iota((1, 128), 1) == 67, part, sums)
    m2_ref[...] = jnp.zeros_like(m2_ref)
    m2_ref[pl.ds(3, nx2)] = m2
    fetch_level_2(m2_ref, range(2, 6), pick_ref)
    for p in range(4, 12):
        corr1_ref[p] = w1_ref[p] * t1s_ref[p] + pick_ref[p // 2]
    for p in range(5, 11):
        m1_ref[p] = KEEP * corr1_ref[p] + w1_ref[p] * (
            t1s_ref[p] + neighbours(corr1_ref, f10_ref, f11_ref, f12_ref, p)
        )
    widen_level_1(m1_ref, wide_ref, 5, 11)

    def correct(q, carry):
        e = double_rows(t_ref, wide_ref, q)
        for i in range(2):
            p = 2 * q + i
            corr_ref[p] = w_ref[p] * im_ref[p] + e
        return carry

    lax.fori_loop(5, 11, correct, 0)

    def relax(p, carry):
        corr_ref[p - 4] = KEEP * corr_ref[p] + w_ref[p] * (
            im_ref[p] + neighbours(corr_ref, f0_ref, f1_ref, f2_ref, p)
        )
        return carry

    for p in range(8):
        q = 12 + p
        mi = KEEP * corr_ref[q] + w_ref[q] * (
            im_ref[q] + neighbours(corr_ref, f0_ref, f1_ref, f2_ref, q)
        )
        corr_ref[p] = mi
        mi_out[p] = corr_ref[p, pl.ds(12, 16), 0:128]


def last_kernel(sums_ref, s_ref, fp_ref, im_ref, mi_ref, solution_ref, residual_ref, direction_ref):
    total = jnp.sum(sums_ref[...], axis=0)
    lane = iota((1, 128), 1)

    def value(lanes):
        keep = lane == lanes[0]
        for k in lanes[1:]:
            keep = keep | (lane == k)
        return jnp.sum(jnp.where(keep, total, 0.0), axis=1, keepdims=True)

    projected, curvature, product = value((64,)), value((65,)), value((66, 67))
    step = projected / curvature
    share = product / curvature
    for p in range(8):
        fp = fp_ref[p]
        solution_ref[p] = step * fp
        residual_ref[p] = s_ref[p] - step * im_ref[p]
        direction_ref[p] = step * (share * fp - mi_ref[p])


def call(kernel, inputs, outs, scratch=(), keep_in=(), keep_out=()):
    vmem = pl.BlockSpec(memory_space=pltpu.VMEM)
    inputs = [
        pltpu.with_memory_space_constraint(value, pltpu.VMEM) if i in keep_in else value
        for i, value in enumerate(inputs)
    ]
    shapes = [
        pltpu.VMEM(shape, dtype) if i in keep_out else jax.ShapeDtypeStruct(shape, dtype)
        for i, (shape, dtype) in enumerate(outs)
    ]
    return pl.pallas_call(
        kernel,
        out_shape=shapes,
        in_specs=[vmem] * len(inputs),
        out_specs=[vmem] * len(outs),
        scratch_shapes=[pltpu.VMEM(shape, F32) for shape in scratch],
        compiler_params=pltpu.CompilerParams(vmem_limit_bytes=VMEM_LIMIT),
    )(*inputs)


def shift_along(value, axis, by):
    size = lax.axis_size(axis)
    return lax.ppermute(value, axis, [(i, i + by) for i in range(size) if 0 <= i + by < size])


def gather_plane(value):
    peers = lax.axis_size(("gx", "gy"))
    copies = jnp.broadcast_to(value[None], (peers,) + value.shape)
    return lax.all_to_all(copies, ("gx", "gy"), 0, 0, tiled=True)


def local(right_side, face_coefficients, solid):
    nx2, ny2 = 2 * lax.axis_size("gx"), 4 * lax.axis_size("gy")
    (own,) = call(
        prepare_kernel, [right_side, face_coefficients, solid], [((8, 5, 16, 128), BF16)]
    )
    before, after = shift_along(own, "gz", 1), shift_along(own, "gz", -1)
    (own,) = call(rim_kernel, [own, before, after], [((8, 6, 16, 128), BF16)])
    block = jnp.concatenate(
        [
            shift_along(own[4:], "gx", 2),
            shift_along(own, "gx", 1),
            own,
            shift_along(own, "gx", -1),
            shift_along(own[:4], "gx", -2),
        ],
        axis=0,
    )
    before, after = shift_along(block, "gy", 1), shift_along(block, "gy", -1)

    fine, fine_up = (32, 40, 256), (33, 40, 256)
    mid, mid_up = (16, 24, 128), (17, 24, 128)
    rows = (16, 24, 256)
    *state, pay = call(
        first_kernel,
        [block, before, after],
        [(shape, F32) for shape in (fine, fine_up, fine, fine, fine, fine, mid, mid_up, mid, mid, mid, (8, 128))],
        [fine, fine, fine, fine, (2, 40, 128), rows, rows, rows, rows, mid_up, mid, mid, mid, (24, 128), (8, 128)],
        keep_out=range(11),
    )
    own = gather_plane(pay)
    before, after = shift_along(own, "gz", 1), shift_along(own, "gz", -1)
    level_2, level_3 = (nx2, ny2, 128), (nx2 // 2, ny2 // 2, 128)
    window = (nx2 + 6, ny2, 128)
    half = (nx2 // 2, ny2, 128)
    first_pre, image, *more, pay = call(
        second_kernel,
        [*state, own, before, after],
        [((8, 16, 128), F32)] * 2
        + [(shape, F32) for shape in (fine, mid, *[level_2] * 4, *[level_3] * 4, (4, 128))],
        [(4,) + level_2, half, half, window, (8, 24, 128), mid, mid, rows, (2, 40, 128),
         fine, fine, fine, (8, 24, 256), mid, (32, 128)],
        keep_in=range(11),
        keep_out=range(2, 12),
    )
    own = gather_plane(pay).reshape(nx2 * ny2 // 16, 8, 128)
    before, after = shift_along(own, "gz", 1), shift_along(own, "gz", -1)
    _, f0, f1, f2, w, _, _, f10, f11, f12, w1 = state
    mapped, sums = call(
        third_kernel,
        [f0, f1, f2, w, f10, f11, f12, w1, *more, own, before, after],
        [((8, 16, 128), F32), ((1, 128), F32)],
        [level_2, half, half, window, (8, 24, 128), mid, mid, rows, (2, 40, 128), fine],
        keep_in=range(18),
    )
    peers = lax.axis_size("gz")
    sums = lax.all_to_all(jnp.broadcast_to(sums[None], (peers, 1, 128)), "gz", 0, 0, tiled=True)
    return tuple(
        call(
            last_kernel,
            [sums, right_side, first_pre, image, mapped],
            [((8, 16, 128), F32)] * 3,
        )
    )


def solution(mesh):
    placed = P("gx", "gy", "gz")
    return jax.shard_map(
        local,
        mesh=mesh,
        in_specs=(placed, P(None, "gx", "gy", "gz"), placed),
        out_specs=(placed, placed, placed),
        check_vma=False,
    )
```

time: 879 us -> 155 us (0.18)
  starting transfers between devices: 487 us -> 38.9 us
  blocking collectives: 222 us -> 57.3 us
  waiting for transfers between devices: 80.9 us -> 27.4 us
  local copies, waits for them, and re-layouts: 53 us -> 2.76 us
  Pallas kernels: 0 us -> 26.8 us
  other arithmetic: 25.4 us -> 0 us
    ppermute x144 -> x12, starting transfers between devices: 487 us -> 38.9 us  [shift_along(): lax.ppermute(value, axis, [(i, i + by) for i in range(size) if 0 <= i + b...]
    psum x2 -> x0, blocking collectives: 222 us -> none  [the longest x1 111 us: local(): projected = lax.psum(jnp.sum(right_side * first_pre), ('gx', 'gy', 'gz'))]
    all_to_all x0 -> x3, blocking collectives: none -> 57.3 us  [the longest x2 37.3 us: gather_plane(): return lax.all_to_all(copies, ('gx', 'gy'), 0, 0, tiled=True)]
    ppermute x144 -> x12, waiting for transfers between devices: 80.9 us -> 27.4 us  [shift_along(): lax.ppermute(value, axis, [(i, i + by) for i in range(size) if 0 <= i + b...]
    another operation x6 -> x0, local copies, waits for them, and re-layouts: 33.2 us -> none  [blocked(): return values.reshape(size_x // 2, 2, size_y // 2, 2, size_z // 2, 2)]
    pallas_call x0 -> x6, Pallas kernels: none -> 26.8 us  [call(): pl.pallas_call(kernel, out_shape=shapes, in_specs=[vmem] * len(inputs), o...]
    reduce_sum x25 -> x0, other arithmetic: 19.6 us -> none  [the longest x8 5.7 us: restrict(): return 0.5 * jnp.sum(blocked(values), axis=(1, 3, 5))]
    reshape x12 -> x0, local copies, waits for them, and re-layouts: 13.1 us -> none  [the longest x4 12.1 us: blocked(): return values.reshape(size_x // 2, 2, size_y // 2, 2, size_z // 2, 2)]
  transfers between devices with their start and end apart: 144 -> 12, of which waited for: 72 -> 11; matrix products, arithmetic and copies ran while one was open for 4% -> 0% of each run, Pallas kernels for 0% -> 0%
where the time goes in v1:
time: 155 us; the launch traced here: 154 us
  blocking collectives  57.3 us (37%)
  starting transfers between devices  38.9 us (25%)
  waiting for transfers between devices  27.4 us (18%)
  Pallas kernels  26.8 us (17%)
  local copies, waits for them, and re-layouts  2.76 us (2%)
    ppermute x12, starting transfers between devices, shift_along(): lax.ppermute(value, axis, [(i, i + by) for i in range(size) if 0 <= i + b...  38.9 us
    all_to_all x2, blocking collectives, gather_plane(): return lax.all_to_all(copies, ('gx', 'gy'), 0, 0, tiled=True)  37.3 us
    ppermute x12, waiting for transfers between devices, shift_along(): lax.ppermute(value, axis, [(i, i + by) for i in range(size) if 0 <= i + b...  27.4 us
    pallas_call x6, Pallas kernels, call(): pl.pallas_call(kernel, out_shape=shapes, in_specs=[vmem] * len(inputs), o...  26.8 us
    all_to_all x1, blocking collectives, local(): lax.all_to_all(jnp.broadcast_to(sums[None], (peers, 1, 128)), 'gz', 0, 0,...  20.1 us
  transfers between devices with their start and end apart: 12, of which 11 were waited for; matrix products, arithmetic and copies ran while one was open for 0% of the time, Pallas kernels for 0%

profile of v1, /device:TPU:1, one launch (start us, length us, event | category | flops | bytes accessed | tf_op | source)
XLA Modules:
  0.0 154.0 jit_solution(12740256236094312124)
XLA Ops:
  0.6 0.8 copy-done
  1.5 0.9 copy-done.2
  2.4 0.8 copy-done.3
  3.2 1.3 collective-permute-start.1
  4.5 5.5 %collective-permute-start = (bf16[8,5,16,128]{3,2,1,0:T(8,128)(2,1)S(1)}, bf16[8,5,16,128]{3,2,1,0:T(8,128)(2,1)S(1)}, u32[]{:S(2)}, u32[]{:S(2)}) collective-permute-start(bf16[8,5,16,128]{3,2,1,0:T(8,128)(2,1)S(1)} %shard_map.58.own_ref), channel_id=1, source_target_pairs={{0,1},{1,2},{2,3},{3,4},{4,5},{5,6},{6,7},{8,9},{9,10},{10,11},{11... | collective-permute-start | bytes 491528 | tf_op jit(solution)/shard_map/ppermute | solution.py:598
  10.8 1.5 collective-permute-done.before_ref
  12.9 4.8 %collective-permute-start.2 = (bf16[4,6,16,128]{3,2,1,0:T(8,128)(2,1)S(1)}, bf16[4,6,16,128]{3,2,1,0:T(8,128)(2,1)S(1)}, u32[]{:S(2)}, u32[]{:S(2)}) collective-permute-start(bf16[4,6,16,128]{3,2,1,0:T(8,128)(2,1)S(1)} %get-tuple-element.58), channel_id=1, source_target_pairs={{0,128},{64,192},{128,256},{192,320},{256,384},{320,448},{1,129},{... | collective-permute-start | bytes 294920 | tf_op jit(solution)/shard_map/ppermute | solution.py:598
  17.7 3.2 %collective-permute-start.3 = (bf16[8,6,16,128]{3,2,1,0:T(8,128)(2,1)S(1)}, bf16[8,6,16,128]{3,2,1,0:T(8,128)(2,1)S(1)}, u32[]{:S(2)}, u32[]{:S(2)}) collective-permute-start(bf16[8,6,16,128]{3,2,1,0:T(8,128)(2,1)S(1)} %shard_map.59), channel_id=1, source_target_pairs={{0,64},{64,128},{128,192},{192,256},{256,320},{320,384},{384,448},... | collective-permute-start | bytes 589832 | tf_op jit(solution)/shard_map/ppermute | solution.py:598
  21.0 1.3 collective-permute-start.4
  22.3 1.3 collective-permute-start.5
  23.6 1.8 %collective-permute-done.3 = bf16[8,6,16,128]{3,2,1,0:T(8,128)(2,1)S(1)} collective-permute-done((bf16[8,6,16,128]{3,2,1,0:T(8,128)(2,1)S(1)}, bf16[8,6,16,128]{3,2,1,0:T(8,128)(2,1)S(1)}, u32[]{:S(2)}, u32[]{:S(2)}) %collective-permute-start.3) | collective-permute-done | bytes 196640 | tf_op jit(solution)/shard_map/ppermute | solution.py:598
  25.4 3.0 %collective-permute-done.4 = bf16[8,6,16,128]{3,2,1,0:T(8,128)(2,1)S(1)} collective-permute-done((bf16[8,6,16,128]{3,2,1,0:T(8,128)(2,1)S(1)}, bf16[8,6,16,128]{3,2,1,0:T(8,128)(2,1)S(1)}, u32[]{:S(2)}, u32[]{:S(2)}) %collective-permute-start.4) | collective-permute-done | bytes 196640 | tf_op jit(solution)/shard_map/ppermute | solution.py:598
  28.4 3.6 %collective-permute-done.5 = bf16[4,6,16,128]{3,2,1,0:T(8,128)(2,1)S(1)} collective-permute-done((bf16[4,6,16,128]{3,2,1,0:T(8,128)(2,1)S(1)}, bf16[4,6,16,128]{3,2,1,0:T(8,128)(2,1)S(1)}, u32[]{:S(2)}, u32[]{:S(2)}) %collective-permute-start.5) | collective-permute-done | bytes 98336 | tf_op jit(solution)/shard_map/ppermute | solution.py:598
  32.0 6.5 %collective-permute-start.7 = (bf16[32,6,16,128]{3,2,1,0:T(8,128)(2,1)S(1)}, bf16[32,6,16,128]{3,2,1,0:T(8,128)(2,1)S(1)}, u32[]{:S(2)}, u32[]{:S(2)}) collective-permute-start(bf16[32,6,16,128]{3,2,1,0:T(8,128)(2,1)S(1)} %constant_dynamic-update-slice_fusion.x_ref), channel_id=1, source_target_pairs={{8,0},{16,8},{24,16},{32,24},{40,32},{48,40},{56,48},{9,1},{17,9},... | collective-permute-start | bytes 2359304 | tf_op jit(solution)/shard_map/ppermute | solution.py:598
  38.5 3.0 %collective-permute-start.6 = (bf16[32,6,16,128]{3,2,1,0:T(8,128)(2,1)S(1)}, bf16[32,6,16,128]{3,2,1,0:T(8,128)(2,1)S(1)}, u32[]{:S(2)}, u32[]{:S(2)}) collective-permute-start(bf16[32,6,16,128]{3,2,1,0:T(8,128)(2,1)S(1)} %constant_dynamic-update-slice_fusion.x_ref), channel_id=1, source_target_pairs={{0,8},{8,16},{16,24},{24,32},{32,40},{40,48},{48,56},{1,9},{9,17},... | collective-permute-start | bytes 2359304 | tf_op jit(solution)/shard_map/ppermute | solution.py:598
  41.6 7.7 %collective-permute-done.7.yp_ref = bf16[32,6,16,128]{3,2,1,0:T(8,128)(2,1)S(1)} collective-permute-done((bf16[32,6,16,128]{3,2,1,0:T(8,128)(2,1)S(1)}, bf16[32,6,16,128]{3,2,1,0:T(8,128)(2,1)S(1)}, u32[]{:S(2)}, u32[]{:S(2)}) %collective-permute-start.7) | collective-permute-done | bytes 786464 | tf_op jit(solution)/shard_map/ppermute | solution.py:598
  49.3 1.2 collective-permute-done.6.ym_ref
  50.5 11.8 %shard_map.60 = (f32[32,40,256]{2,1,0:T(8,128)S(1)}, f32[33,40,256]{2,1,0:T(8,128)S(1)}, f32[32,40,256]{2,1,0:T(8,128)S(1)}, f32[32,40,256]{2,1,0:T(8,128)S(1)},...) custom-call(bf16[32,6,16,128]{3,2,1,0:T(8,128)(2,1)S(1)} %constant_d, ...), custom_call_target="tpu_custom_call" | custom-call | tf_op jit(solution)/shard_map/pallas_call | solution.py:586
  62.3 21.1 %all_to_all.15.own_ref = f32[64,8,128]{2,1,0:T(8,128)S(1)} all-to-all(f32[64,8,128]{2,1,0:T(8,128)S(1)} %broadcast_in_dim.8), channel_id=1, replica_groups=mesh['gx'=8,'gy'=8,'gz'=8] {'gx','gy'}, dimensions={0} | all-to-all | bytes 524288 | tf_op jit(solution)/shard_map/all_to_all | solution.py:604
  83.4 1.3 collective-permute-start.9
  84.7 4.7 %collective-permute-start.8 = (f32[64,8,128]{2,1,0:T(8,128)S(1)}, f32[64,8,128]{2,1,0:T(8,128)S(1)}, u32[]{:S(2)}, u32[]{:S(2)}) collective-permute-start(f32[64,8,128]{2,1,0:T(8,128)S(1)} %all_to_all.15.own_ref), channel_id=1, source_target_pairs={{0,1},{1,2},{2,3},{3,4},{4,5},{5,6},{6,7},{8,9},{9,10},{10,11},{11... | collective-permute-start | bytes 786440 | tf_op jit(solution)/shard_map/ppermute | solution.py:598
  89.4 4.6 %collective-permute-done.9.after_ref = f32[64,8,128]{2,1,0:T(8,128)S(1)} collective-permute-done((f32[64,8,128]{2,1,0:T(8,128)S(1)}, f32[64,8,128]{2,1,0:T(8,128)S(1)}, u32[]{:S(2)}, u32[]{:S(2)}) %collective-permute-start.9) | collective-permute-done | bytes 262176 | tf_op jit(solution)/shard_map/ppermute | solution.py:598
  94.0 0.9 collective-permute-done.8.before_ref
  94.9 10.6 %shard_map.61 = (f32[8,16,128]{2,1,0:T(8,128)S(1)}, f32[8,16,128]{2,1,0:T(8,128)S(1)}, f32[32,40,256]{2,1,0:T(8,128)S(1)}, f32[16,24,128]{2,1,0:T(8,128)S(1)}, f...) custom-call(f32[32,40,256]{2,1,0:T(8,128)S(1)} %get-tuple-element.38, ...), custom_call_target="tpu_custom_call" | custom-call | tf_op jit(solution)/shard_map/pallas_call | solution.py:586
  105.5 16.2 %all_to_all.16 = f32[64,4,128]{2,1,0:T(4,128)S(1)} all-to-all(f32[64,4,128]{2,1,0:T(4,128)S(1)} %broadcast_in_dim.9), channel_id=1, replica_groups=mesh['gx'=8,'gy'=8,'gz'=8] {'gx','gy'}, dimensions={0} | all-to-all | bytes 262144 | tf_op jit(solution)/shard_map/all_to_all | solution.py:604
  121.6 1.3 collective-permute-start.11
  122.9 4.7 %collective-permute-start.10 = (f32[32,8,128]{2,1,0:T(8,128)S(1)}, f32[32,8,128]{2,1,0:T(8,128)S(1)}, u32[]{:S(2)}, u32[]{:S(2)}) collective-permute-start(f32[32,8,128]{2,1,0:T(8,128)S(1)} %bitcast.3), channel_id=1, source_target_pairs={{0,1},{1,2},{2,3},{3,4},{4,5},{5,6},{6,7},{8,9},{9,10},{10,11},{11... | collective-permute-start | bytes 393224 | tf_op jit(solution)/shard_map/ppermute | solution.py:598
  127.7 1.6 %collective-permute-done.11.after_ref = f32[32,8,128]{2,1,0:T(8,128)S(1)} collective-permute-done((f32[32,8,128]{2,1,0:T(8,128)S(1)}, f32[32,8,128]{2,1,0:T(8,128)S(1)}, u32[]{:S(2)}, u32[]{:S(2)}) %collective-permute-start.11) | collective-permute-done | bytes 131104 | tf_op jit(solution)/shard_map/ppermute | solution.py:598
  129.3 0.9 collective-permute-done.10.before_ref
  130.1 3.0 %shard_map.62 = (f32[8,16,128]{2,1,0:T(8,128)S(1)}, f32[1,128]{1,0:T(1,128)S(1)}) custom-call(f32[33,40,256]{2,1,0:T(8,128)S(1)} %get-tuple-element.30.f0_ref, f32[32,40,256]{2,1,0:T(8,128)S(1)} %get-tuple-element.31.f1_ref, f32[32,40,256]{2,1,0:T(8,128)S(1)} %get-tuple-element.32.f2_ref, f32[32,40,256]{2,1,0:T(8,128)S(1)} %get-tuple-element.33.w_ref, ...), custom_call_target="tpu_custom_call" | custom-call | tf_op jit(solution)/shard_map/pallas_call | solution.py:586
  133.1 20.1 %all_to_all.17.sums_ref = f32[8,1,128]{2,1,0:T(1,128)S(1)} all-to-all(f32[8,1,128]{2,1,0:T(1,128)S(1)} %broadcast_in_dim.11), channel_id=1, replica_groups=mesh['gx'=8,'gy'=8,'gz'=8] {'gz'}, dimensions={0} | all-to-all | bytes 8192 | tf_op jit(solution)/shard_map/all_to_all | solution.py:662
  153.2 0.8 shard_map.63
  (18 shorter events, 1.6 us)
Async XLA Ops:
  0.6 0.8 copy-start
  1.5 0.9 copy-start.2
  2.4 0.8 copy-start.3
  3.2 7.5 %collective-permute-start.1 = (bf16[8,5,16,128]{3,2,1,0:T(8,128)(2,1)S(1)}, bf16[8,5,16,128]{3,2,1,0:T(8,128)(2,1)S(1)}, u32[]{:S(2)}, u32[]{:S(2)}) collective-permute-start(bf16[8,5,16,128]{3,2,1,0:T(8,128)(2,1)S(1)} %shard_map.58.own_ref), channel_id=1, source_target_pairs={{1,0},{2,1},{3,2},{4,3},{5,4},{6,5},{7,6},{9,8},{10,9},{11,10},{12... | collective-permute-start | bytes 491528 | tf_op jit(solution)/shard_map/ppermute | solution.py:598
  4.5 7.7 %collective-permute-start = (bf16[8,5,16,128]{3,2,1,0:T(8,128)(2,1)S(1)}, bf16[8,5,16,128]{3,2,1,0:T(8,128)(2,1)S(1)}, u32[]{:S(2)}, u32[]{:S(2)}) collective-permute-start(bf16[8,5,16,128]{3,2,1,0:T(8,128)(2,1)S(1)} %shard_map.58.own_ref), channel_id=1, source_target_pairs={{0,1},{1,2},{2,3},{3,4},{4,5},{5,6},{6,7},{8,9},{9,10},{10,11},{11... | collective-permute-start | bytes 491528 | tf_op jit(solution)/shard_map/ppermute | solution.py:598
  12.9 10.7 %collective-permute-start.2 = (bf16[4,6,16,128]{3,2,1,0:T(8,128)(2,1)S(1)}, bf16[4,6,16,128]{3,2,1,0:T(8,128)(2,1)S(1)}, u32[]{:S(2)}, u32[]{:S(2)}) collective-permute-start(bf16[4,6,16,128]{3,2,1,0:T(8,128)(2,1)S(1)} %get-tuple-element.58), channel_id=1, source_target_pairs={{0,128},{64,192},{128,256},{192,320},{256,384},{320,448},{1,129},{... | collective-permute-start | bytes 294920 | tf_op jit(solution)/shard_map/ppermute | solution.py:598
  17.7 7.6 %collective-permute-start.3 = (bf16[8,6,16,128]{3,2,1,0:T(8,128)(2,1)S(1)}, bf16[8,6,16,128]{3,2,1,0:T(8,128)(2,1)S(1)}, u32[]{:S(2)}, u32[]{:S(2)}) collective-permute-start(bf16[8,6,16,128]{3,2,1,0:T(8,128)(2,1)S(1)} %shard_map.59), channel_id=1, source_target_pairs={{0,64},{64,128},{128,192},{192,256},{256,320},{320,384},{384,448},... | collective-permute-start | bytes 589832 | tf_op jit(solution)/shard_map/ppermute | solution.py:598
  21.0 7.5 %collective-permute-start.4 = (bf16[8,6,16,128]{3,2,1,0:T(8,128)(2,1)S(1)}, bf16[8,6,16,128]{3,2,1,0:T(8,128)(2,1)S(1)}, u32[]{:S(2)}, u32[]{:S(2)}) collective-permute-start(bf16[8,6,16,128]{3,2,1,0:T(8,128)(2,1)S(1)} %shard_map.59), channel_id=1, source_target_pairs={{64,0},{128,64},{192,128},{256,192},{320,256},{384,320},{448,384},... | collective-permute-start | bytes 589832 | tf_op jit(solution)/shard_map/ppermute | solution.py:598
  22.3 9.8 %collective-permute-start.5 = (bf16[4,6,16,128]{3,2,1,0:T(8,128)(2,1)S(1)}, bf16[4,6,16,128]{3,2,1,0:T(8,128)(2,1)S(1)}, u32[]{:S(2)}, u32[]{:S(2)}) collective-permute-start(bf16[4,6,16,128]{3,2,1,0:T(8,128)(2,1)S(1)} %get-tuple-element.57), channel_id=1, source_target_pairs={{128,0},{192,64},{256,128},{320,192},{384,256},{448,320},{129,1},{... | collective-permute-start | bytes 294920 | tf_op jit(solution)/shard_map/ppermute | solution.py:598
  32.0 17.2 %collective-permute-start.7 = (bf16[32,6,16,128]{3,2,1,0:T(8,128)(2,1)S(1)}, bf16[32,6,16,128]{3,2,1,0:T(8,128)(2,1)S(1)}, u32[]{:S(2)}, u32[]{:S(2)}) collective-permute-start(bf16[32,6,16,128]{3,2,1,0:T(8,128)(2,1)S(1)} %constant_dynamic-update-slice_fusion.x_ref), channel_id=1, source_target_pairs={{8,0},{16,8},{24,16},{32,24},{40,32},{48,40},{56,48},{9,1},{17,9},... | collective-permute-start | bytes 2359304 | tf_op jit(solution)/shard_map/ppermute | solution.py:598
  38.5 11.9 %collective-permute-start.6 = (bf16[32,6,16,128]{3,2,1,0:T(8,128)(2,1)S(1)}, bf16[32,6,16,128]{3,2,1,0:T(8,128)(2,1)S(1)}, u32[]{:S(2)}, u32[]{:S(2)}) collective-permute-start(bf16[32,6,16,128]{3,2,1,0:T(8,128)(2,1)S(1)} %constant_dynamic-update-slice_fusion.x_ref), channel_id=1, source_target_pairs={{0,8},{8,16},{16,24},{24,32},{32,40},{40,48},{48,56},{1,9},{9,17},... | collective-permute-start | bytes 2359304 | tf_op jit(solution)/shard_map/ppermute | solution.py:598
  83.4 10.6 %collective-permute-start.9 = (f32[64,8,128]{2,1,0:T(8,128)S(1)}, f32[64,8,128]{2,1,0:T(8,128)S(1)}, u32[]{:S(2)}, u32[]{:S(2)}) collective-permute-start(f32[64,8,128]{2,1,0:T(8,128)S(1)} %all_to_all.15.own_ref), channel_id=1, source_target_pairs={{1,0},{2,1},{3,2},{4,3},{5,4},{6,5},{7,6},{9,8},{10,9},{11,10},{12... | collective-permute-start | bytes 786440 | tf_op jit(solution)/shard_map/ppermute | solution.py:598
  84.7 10.2 %collective-permute-start.8 = (f32[64,8,128]{2,1,0:T(8,128)S(1)}, f32[64,8,128]{2,1,0:T(8,128)S(1)}, u32[]{:S(2)}, u32[]{:S(2)}) collective-permute-start(f32[64,8,128]{2,1,0:T(8,128)S(1)} %all_to_all.15.own_ref), channel_id=1, source_target_pairs={{0,1},{1,2},{2,3},{3,4},{4,5},{5,6},{6,7},{8,9},{9,10},{10,11},{11... | collective-permute-start | bytes 786440 | tf_op jit(solution)/shard_map/ppermute | solution.py:598
  121.6 7.6 %collective-permute-start.11 = (f32[32,8,128]{2,1,0:T(8,128)S(1)}, f32[32,8,128]{2,1,0:T(8,128)S(1)}, u32[]{:S(2)}, u32[]{:S(2)}) collective-permute-start(f32[32,8,128]{2,1,0:T(8,128)S(1)} %bitcast.2), channel_id=1, source_target_pairs={{1,0},{2,1},{3,2},{4,3},{5,4},{6,5},{7,6},{9,8},{10,9},{11,10},{12... | collective-permute-start | bytes 393224 | tf_op jit(solution)/shard_map/ppermute | solution.py:598
  122.9 7.2 %collective-permute-start.10 = (f32[32,8,128]{2,1,0:T(8,128)S(1)}, f32[32,8,128]{2,1,0:T(8,128)S(1)}, u32[]{:S(2)}, u32[]{:S(2)}) collective-permute-start(f32[32,8,128]{2,1,0:T(8,128)S(1)} %bitcast.3), channel_id=1, source_target_pairs={{0,1},{1,2},{2,3},{3,4},{4,5},{5,6},{6,7},{8,9},{9,10},{10,11},{11... | collective-permute-start | bytes 393224 | tf_op jit(solution)/shard_map/ppermute | solution.py:598
  130.1 23.0 %copy-start.1 = (f32[8,16,128]{2,1,0:T(8,128)S(1)}, f32[8,16,128]{2,1,0:T(8,128)}, u32[]{:S(2)}) copy-start(f32[8,16,128]{2,1,0:T(8,128)} %s_ref.3) | copy-start | bytes 196612

commit v2 on v1

--- a/solution.py
+++ b/solution.py
@@ -36,6 +36,10 @@
     return jnp.dot(matrix, high, preferred_element_type=F32) + jnp.dot(
         matrix, low, preferred_element_type=F32
     )
+
+
+def root(values):
+    return values * lax.rsqrt(jnp.maximum(values, 1e-12))
 
 
 def turn(values, shift, axis):
@@ -85,7 +89,17 @@
         r_ref[q, pl.ds(0, 20), pl.ds(128 * half, 128)] = halves[half]
 
 
-def prepare_kernel(s_ref, fc_ref, solid_ref, out_ref):
+def prepare_kernel(s_hbm, fc_hbm, solid_hbm, out_ref, s_ref, fc_ref, solid_ref, sems):
+    copies = [
+        pltpu.make_async_copy(source, target, sems.at[i])
+        for i, (source, target) in enumerate(
+            ((s_hbm, s_ref), (fc_hbm, fc_ref), (solid_hbm, solid_ref))
+        )
+    ]
+    for copy in copies:
+        copy.start()
+    for copy in copies:
+        copy.wait()
     s = s_ref[...]
     high = s.astype(BF16)
     out_ref[:, 0] = high
@@ -114,7 +128,7 @@
 def first_kernel(
     x_ref, ym_ref, yp_ref,
     s_ref, f0_ref, f1_ref, f2_ref, w_ref, d_ref,
-    s1_ref, f10_ref, f11_ref, f12_ref, w1_ref, pay_ref,
+    s1_ref, f10_ref, f11_ref, f12_ref, w1_ref, up_ref, down_ref, pay_ref,
     c0_ref, c1_ref, c2_ref, sm_ref, t_ref, r0_ref, r1_ref, r2_ref, rs_ref,
     l10_ref, l11_ref, l12_ref, sm1_ref, t1_ref, u_ref,
 ):
@@ -141,19 +155,19 @@
             c_ref[p, :, 128:256] = rims[2 + a]
         return carry
 
-    lax.fori_loop(0, 32, unpack, 0)
+    lax.fori_loop(0, 24, unpack, 0)
 
     def faces(p, carry):
         before = jnp.maximum(p - 1, 0)
-        f0_ref[p] = jnp.sqrt(c0_ref[p] * c0_ref[before])
+        f0_ref[p] = root(c0_ref[p] * c0_ref[before])
         c1 = c1_ref[p]
-        f1_ref[p] = jnp.sqrt(c1 * turn(c1, 1, 0))
+        f1_ref[p] = root(c1 * turn(c1, 1, 0))
         c2 = c2_ref[p]
-        f2_ref[p] = jnp.sqrt(c2 * turn(c2, 1, 1))
-        return carry
-
-    lax.fori_loop(0, 32, faces, 0)
-    f0_ref[32] = jnp.zeros((40, 256), F32)
+        f2_ref[p] = root(c2 * turn(c2, 1, 1))
+        return carry
+
+    lax.fori_loop(0, 24, faces, 0)
+    f0_ref[24] = jnp.zeros((40, 256), F32)
 
     first_row = (iota((40, 256), 0) == 12) & at_y
     first_lane = (iota((40, 256), 1) == 0) & at_z
@@ -165,7 +179,7 @@
         for i in range(2):
             p = 2 * q + i
             f0, f1, f2 = f0_ref[p], f1_ref[p], f2_ref[p]
-            low0 = f0 + jnp.where((p == 12) & at_x, c0_ref[p], 0.0)
+            low0 = f0 + jnp.where((p == 8) & at_x, c0_ref[p], 0.0)
             low1 = f1 + jnp.where(first_row, c1_ref[p], 0.0)
             low2 = f2 + jnp.where(first_lane, c2_ref[p], 0.0)
             d = ABSORB + low0 + f0_ref[p + 1] + low1 + turn(f1, -1, 0) + low2 + turn(f2, -1, 1)
@@ -179,7 +193,7 @@
         put_rows(r2_ref, q, row_pairs(t_ref, lows[0][2] + lows[1][2], True))
         return carry
 
-    lax.fori_loop(0, 16, diagonals, 0)
+    lax.fori_loop(0, 12, diagonals, 0)
 
     def leftovers(q, carry):
         total = jnp.zeros((40, 256), F32)
@@ -189,15 +203,17 @@
         put_rows(rs_ref, q, row_pairs(t_ref, total, True))
         return carry
 
-    lax.fori_loop(1, 15, leftovers, 0)
+    lax.fori_loop(1, 11, leftovers, 0)
 
     pairs = one_hot(256, 128, lambda r, c: lax.shift_right_logical(r, 1) == c, 0.25)
     evens = one_hot(256, 128, lambda r, c: r == 2 * c, 0.25)
-    l10_ref[pl.ds(0, 16)] = spread(r0_ref[...].reshape(384, 256), pairs).reshape(16, 24, 128)
-    l11_ref[...] = spread(r1_ref[...].reshape(384, 256), pairs).reshape(16, 24, 128)
-    l12_ref[...] = spread(r2_ref[...].reshape(384, 256), evens).reshape(16, 24, 128)
-    s1_ref[...] = 2.0 * spread(rs_ref[...].reshape(384, 256), pairs).reshape(16, 24, 128)
-    l10_ref[16] = jnp.zeros((24, 128), F32)
+    for target, source, matrix in (
+        (l10_ref, r0_ref, pairs), (l11_ref, r1_ref, pairs), (l12_ref, r2_ref, evens), (s1_ref, rs_ref, pairs)
+    ):
+        target[pl.ds(0, 2)] = jnp.zeros((2, 24, 128), F32)
+        target[pl.ds(14, 2)] = jnp.zeros((2, 24, 128), F32)
+        value = spread(source[...].reshape(288, 256), matrix).reshape(12, 24, 128)
+        target[pl.ds(2, 12)] = 2.0 * value if target is s1_ref else value
 
     first_row_1 = (iota((24, 128), 0) == 6) & at_y
     first_lane_1 = (iota((24, 128), 1) == 0) & at_z
@@ -222,7 +238,10 @@
         sm1_ref[p] = w * s1_ref[p]
         return carry
 
-    lax.fori_loop(0, 16, diagonals_1, 0)
+    lax.fori_loop(2, 14, diagonals_1, 0)
+    for i, ref in enumerate((s1_ref, w1_ref, f10_ref)):
+        up_ref[pl.ds(2 * i, 2)] = ref[pl.ds(5, 2)]
+        down_ref[pl.ds(2 * i, 2)] = ref[pl.ds(9, 2)]
 
     def quad(values, both):
         t1_ref[...] = values
@@ -335,7 +354,7 @@
 def second_kernel(
     s_ref, f0_ref, f1_ref, f2_ref, w_ref, d_ref,
     s1_ref, f10_ref, f11_ref, f12_ref, w1_ref,
-    own_ref, before_ref, after_ref,
+    low_ref, high_ref, own_ref, before_ref, after_ref,
     fp_out, im_out, im_ref, t1s_ref, f20_ref, f21_ref, f22_ref, w2_ref,
     f30_ref, f31_ref, f32_ref, w3_ref, pay_ref,
     v_ref, t3_ref, e_ref, m2_ref, pick_ref, corr1_ref, m1_ref, wide_ref, t_ref,
@@ -388,7 +407,10 @@
         corr1_ref[p] = w1_ref[p] * s1_ref[p] + pick_ref[lax.shift_right_logical(p, 1)]
         return carry
 
-    lax.fori_loop(0, 16, correct_1, 0)
+    lax.fori_loop(3, 13, correct_1, 0)
+    for k in range(2):
+        corr1_ref[1 + k] = low_ref[2 + k] * low_ref[k] + pick_ref[(1 + k) // 2]
+        corr1_ref[13 + k] = high_ref[2 + k] * high_ref[k] + pick_ref[(13 + k) // 2]
 
     def relax_1(p, carry):
         m1_ref[p] = KEEP * corr1_ref[p] + w1_ref[p] * (
@@ -396,13 +418,21 @@
         )
         return carry
 
-    lax.fori_loop(2, 14, relax_1, 0)
+    lax.fori_loop(3, 13, relax_1, 0)
+    for p, source, w, face, next_face in (
+        (2, low_ref[1], low_ref[3], low_ref[5], f10_ref[3]),
+        (13, high_ref[0], high_ref[2], f10_ref[13], high_ref[5]),
+    ):
+        m1_ref[p] = KEEP * corr1_ref[p] + w * (
+            source + face * corr1_ref[p - 1] + next_face * corr1_ref[p + 1]
+            + plane_terms(corr1_ref[p], f11_ref[p], f12_ref[p])
+        )
     widen_level_1(m1_ref, wide_ref, 2, 14)
 
     def correct(q, carry):
         e = double_rows(t_ref, wide_ref, q)
         for i in range(2):
-            p = 2 * q + i
+            p = 2 * q + i - 4
             corr_ref[p] = w_ref[p] * s_ref[p] + e
         return carry
 
@@ -414,7 +444,7 @@
         )
         return carry
 
-    lax.fori_loop(6, 26, relax, 0)
+    lax.fori_loop(2, 22, relax, 0)
 
     def image(p, carry):
         im = d_ref[p] * fp_ref[p] - neighbours(fp_ref, f0_ref, f1_ref, f2_ref, p)
@@ -422,7 +452,7 @@
         sm_ref[p] = w_ref[p] * im
         return carry
 
-    lax.fori_loop(7, 25, image, 0)
+    lax.fori_loop(3, 21, image, 0)
 
     rs_ref[...] = jnp.zeros_like(rs_ref)
     inside = (iota((40, 128), 0) >= 12) & (iota((40, 128), 0) < 28)
@@ -430,10 +460,10 @@
     def leftovers(q, sums):
         total = jnp.zeros((40, 256), F32)
         for i in range(2):
-            p = 2 * q + i
+            p = 2 * q + i - 4
             left = KEEP * im_ref[p] + neighbours(sm_ref, f0_ref, f1_ref, f2_ref, p)
             total += left
-            own = jnp.where(inside & (p >= 12) & (p < 20), 1.0, 0.0)
+            own = jnp.where(inside & (p >= 8) & (p < 16), 1.0, 0.0)
             fp, im = fp_ref[p, :, 0:128], im_ref[p, :, 0:128]
             sums = (
                 sums[0] + own * s_ref[p, :, 0:128] * fp,
@@ -447,8 +477,8 @@
     sums = lax.fori_loop(4, 12, leftovers, (zero, zero, zero))
 
     for p in range(8):
-        fp_out[p] = fp_ref[12 + p, pl.ds(12, 16), 0:128]
-        im_out[p] = im_ref[12 + p, pl.ds(12, 16), 0:128]
+        fp_out[p] = fp_ref[8 + p, pl.ds(12, 16), 0:128]
+        im_out[p] = im_ref[8 + p, pl.ds(12, 16), 0:128]
 
     pairs = one_hot(256, 128, lambda r, c: lax.shift_right_logical(r, 1) == c, 0.5)
     t1s_ref[...] = jnp.zeros_like(t1s_ref)
@@ -532,25 +562,19 @@
     def correct(q, carry):
         e = double_rows(t_ref, wide_ref, q)
         for i in range(2):
-            p = 2 * q + i
+            p = 2 * q + i - 4
             corr_ref[p] = w_ref[p] * im_ref[p] + e
         return carry
 
     lax.fori_loop(5, 11, correct, 0)
 
-    def relax(p, carry):
-        corr_ref[p - 4] = KEEP * corr_ref[p] + w_ref[p] * (
-            im_ref[p] + neighbours(corr_ref, f0_ref, f1_ref, f2_ref, p)
-        )
-        return carry
-
     for p in range(8):
-        q = 12 + p
+        q = 8 + p
         mi = KEEP * corr_ref[q] + w_ref[q] * (
             im_ref[q] + neighbours(corr_ref, f0_ref, f1_ref, f2_ref, q)
         )
-        corr_ref[p] = mi
-        mi_out[p] = corr_ref[p, pl.ds(12, 16), 0:128]
+        t_ref[0] = mi[:, 0:128]
+        mi_out[p] = t_ref[0, pl.ds(12, 16), :]
 
 
 def last_kernel(sums_ref, s_ref, fp_ref, im_ref, mi_ref, solution_ref, residual_ref, direction_ref):
@@ -573,7 +597,7 @@
         direction_ref[p] = step * (share * fp - mi_ref[p])
 
 
-def call(kernel, inputs, outs, scratch=(), keep_in=(), keep_out=()):
+def call(kernel, inputs, outs, scratch=(), keep_in=(), keep_out=(), space=pltpu.VMEM):
     vmem = pl.BlockSpec(memory_space=pltpu.VMEM)
     inputs = [
         pltpu.with_memory_space_constraint(value, pltpu.VMEM) if i in keep_in else value
@@ -586,9 +610,9 @@
     return pl.pallas_call(
         kernel,
         out_shape=shapes,
-        in_specs=[vmem] * len(inputs),
+        in_specs=[pl.BlockSpec(memory_space=space)] * len(inputs),
         out_specs=[vmem] * len(outs),
-        scratch_shapes=[pltpu.VMEM(shape, F32) for shape in scratch],
+        scratch_shapes=[pltpu.VMEM(shape, F32) if isinstance(shape, tuple) else shape for shape in scratch],
         compiler_params=pltpu.CompilerParams(vmem_limit_bytes=VMEM_LIMIT),
     )(*inputs)
 
@@ -607,32 +631,33 @@
 def local(right_side, face_coefficients, solid):
     nx2, ny2 = 2 * lax.axis_size("gx"), 4 * lax.axis_size("gy")
     (own,) = call(
-        prepare_kernel, [right_side, face_coefficients, solid], [((8, 5, 16, 128), BF16)]
+        prepare_kernel,
+        [right_side, face_coefficients, solid],
+        [((8, 5, 16, 128), BF16)],
+        [
+            (8, 16, 128),
+            pltpu.VMEM((3, 8, 16, 128), BF16),
+            pltpu.VMEM((8, 16, 128), jnp.int32),
+            pltpu.SemaphoreType.DMA((3,)),
+        ],
+        space=pltpu.HBM,
     )
     before, after = shift_along(own, "gz", 1), shift_along(own, "gz", -1)
     (own,) = call(rim_kernel, [own, before, after], [((8, 6, 16, 128), BF16)])
-    block = jnp.concatenate(
-        [
-            shift_along(own[4:], "gx", 2),
-            shift_along(own, "gx", 1),
-            own,
-            shift_along(own, "gx", -1),
-            shift_along(own[:4], "gx", -2),
-        ],
-        axis=0,
-    )
+    block = jnp.concatenate([shift_along(own, "gx", 1), own, shift_along(own, "gx", -1)], axis=0)
     before, after = shift_along(block, "gy", 1), shift_along(block, "gy", -1)
 
-    fine, fine_up = (32, 40, 256), (33, 40, 256)
+    fine, fine_up = (24, 40, 256), (25, 40, 256)
     mid, mid_up = (16, 24, 128), (17, 24, 128)
-    rows = (16, 24, 256)
-    *state, pay = call(
+    rows, wide, edge = (12, 24, 256), (16, 24, 256), (6, 24, 128)
+    *state, up, down, pay = call(
         first_kernel,
         [block, before, after],
-        [(shape, F32) for shape in (fine, fine_up, fine, fine, fine, fine, mid, mid_up, mid, mid, mid, (8, 128))],
-        [fine, fine, fine, fine, (2, 40, 128), rows, rows, rows, rows, mid_up, mid, mid, mid, (24, 128), (8, 128)],
+        [(shape, F32) for shape in (fine, fine_up, fine, fine, fine, fine, mid, mid_up, mid, mid, mid, edge, edge, (8, 128))],
+        [fine, fine, fine, fine, (2, 40, 128), rows, rows, rows, rows, mid, mid, mid, mid, (24, 128), (8, 128)],
         keep_out=range(11),
     )
+    low, high = shift_along(up, "gx", 1), shift_along(down, "gx", -1)
     own = gather_plane(pay)
     before, after = shift_along(own, "gz", 1), shift_along(own, "gz", -1)
     level_2, level_3 = (nx2, ny2, 128), (nx2 // 2, ny2 // 2, 128)
@@ -640,10 +665,10 @@
     half = (nx2 // 2, ny2, 128)
     first_pre, image, *more, pay = call(
         second_kernel,
-        [*state, own, before, after],
+        [*state, low, high, own, before, after],
         [((8, 16, 128), F32)] * 2
         + [(shape, F32) for shape in (fine, mid, *[level_2] * 4, *[level_3] * 4, (4, 128))],
-        [(4,) + level_2, half, half, window, (8, 24, 128), mid, mid, rows, (2, 40, 128),
+        [(4,) + level_2, half, half, window, (8, 24, 128), mid, mid, wide, (2, 40, 128),
          fine, fine, fine, (8, 24, 256), mid, (32, 128)],
         keep_in=range(11),
         keep_out=range(2, 12),
@@ -655,7 +680,7 @@
         third_kernel,
         [f0, f1, f2, w, f10, f11, f12, w1, *more, own, before, after],
         [((8, 16, 128), F32), ((1, 128), F32)],
-        [level_2, half, half, window, (8, 24, 128), mid, mid, rows, (2, 40, 128), fine],
+        [level_2, half, half, window, (8, 24, 128), mid, mid, wide, (2, 40, 128), fine],
         keep_in=range(18),
     )
     peers = lax.axis_size("gz")

time: 155 us -> 147 us (0.948)
  waiting for transfers between devices: 27.4 us -> 17.9 us
  blocking collectives: 57.3 us -> 60.4 us
  Pallas kernels: 26.8 us -> 24.1 us
    ppermute x12, waiting for transfers between devices: 27.4 us -> 17.9 us  [shift_along(): lax.ppermute(value, axis, [(i, i + by) for i in range(size) if 0 <= i + b...]
    all_to_all x2, blocking collectives: 37.3 us -> 41.3 us  [gather_plane(): return lax.all_to_all(copies, ('gx', 'gy'), 0, 0, tiled=True)]
    pallas_call x6, Pallas kernels: 26.8 us -> 24.1 us  [call(): pl.pallas_call(kernel, out_shape=shapes, in_specs=[pl.BlockSpec(memory_sp...]
  transfers between devices with their start and end apart: 12 -> 12, of which waited for: 11 -> 10; matrix products, arithmetic and copies ran while one was open for 0% -> 0% of each run, Pallas kernels for 0% -> 0%
where the time goes in v2:
time: 147 us; the launch traced here: 145 us
  blocking collectives  60.4 us (41%)
  starting transfers between devices  39.4 us (27%)
  Pallas kernels  24.1 us (16%)
  waiting for transfers between devices  17.9 us (12%)
  local copies, waits for them, and re-layouts  2.62 us (2%)
    all_to_all x2, blocking collectives, gather_plane(): return lax.all_to_all(copies, ('gx', 'gy'), 0, 0, tiled=True)  41.3 us
    ppermute x12, starting transfers between devices, shift_along(): lax.ppermute(value, axis, [(i, i + by) for i in range(size) if 0 <= i + b...  39.4 us
    pallas_call x6, Pallas kernels, call(): pl.pallas_call(kernel, out_shape=shapes, in_specs=[pl.BlockSpec(memory_sp...  24.1 us
    all_to_all x1, blocking collectives, local(): lax.all_to_all(jnp.broadcast_to(sums[None], (peers, 1, 128)), 'gz', 0, 0,...  19.1 us
    ppermute x12, waiting for transfers between devices, shift_along(): lax.ppermute(value, axis, [(i, i + by) for i in range(size) if 0 <= i + b...  17.9 us
  transfers between devices with their start and end apart: 12, of which 10 were waited for; matrix products, arithmetic and copies ran while one was open for 0% of the time, Pallas kernels for 0%

profile of v2, /device:TPU:1, one launch (start us, length us, event | category | flops | bytes accessed | tf_op | source)
XLA Modules:
  0.0 145.3 jit_solution(14132848453767019396)
XLA Ops:
  0.6 0.8 copy-done
  1.5 0.9 copy-done.2
  2.4 0.8 copy-done.3
  3.5 1.3 collective-permute-start.1
  4.8 5.5 %collective-permute-start = (bf16[8,5,16,128]{3,2,1,0:T(8,128)(2,1)S(1)}, bf16[8,5,16,128]{3,2,1,0:T(8,128)(2,1)S(1)}, u32[]{:S(2)}, u32[]{:S(2)}) collective-permute-start(bf16[8,5,16,128]{3,2,1,0:T(8,128)(2,1)S(1)} %shard_map.58.own_ref), channel_id=1, source_target_pairs={{0,1},{1,2},{2,3},{3,4},{4,5},{5,6},{6,7},{8,9},{9,10},{10,11},{11... | collective-permute-start | bytes 491528 | tf_op jit(solution)/shard_map/ppermute | solution.py:622
  10.3 0.8 collective-permute-done.1.after_ref
  11.1 1.5 %collective-permute-done.before_ref = bf16[8,5,16,128]{3,2,1,0:T(8,128)(2,1)S(1)} collective-permute-done((bf16[8,5,16,128]{3,2,1,0:T(8,128)(2,1)S(1)}, bf16[8,5,16,128]{3,2,1,0:T(8,128)(2,1)S(1)}, u32[]{:S(2)}, u32[]{:S(2)}) %collective-permute-start) | collective-permute-done | bytes 163872 | tf_op jit(solution)/shard_map/ppermute | solution.py:622
  12.5 0.6 shard_map.59
  13.2 1.3 collective-permute-start.3
  14.5 4.4 %collective-permute-start.2 = (bf16[8,6,16,128]{3,2,1,0:T(8,128)(2,1)S(1)}, bf16[8,6,16,128]{3,2,1,0:T(8,128)(2,1)S(1)}, u32[]{:S(2)}, u32[]{:S(2)}) collective-permute-start(bf16[8,6,16,128]{3,2,1,0:T(8,128)(2,1)S(1)} %shard_map.59), channel_id=1, source_target_pairs={{0,64},{64,128},{128,192},{192,256},{256,320},{320,384},{384,448},... | collective-permute-start | bytes 589832 | tf_op jit(solution)/shard_map/ppermute | solution.py:622
  18.9 1.1 collective-permute-done.3
  20.0 1.5 %collective-permute-done.2 = bf16[8,6,16,128]{3,2,1,0:T(8,128)(2,1)S(1)} collective-permute-done((bf16[8,6,16,128]{3,2,1,0:T(8,128)(2,1)S(1)}, bf16[8,6,16,128]{3,2,1,0:T(8,128)(2,1)S(1)}, u32[]{:S(2)}, u32[]{:S(2)}) %collective-permute-start.2) | collective-permute-done | bytes 196640 | tf_op jit(solution)/shard_map/ppermute | solution.py:622
  21.6 9.1 %collective-permute-start.5 = (bf16[24,6,16,128]{3,2,1,0:T(8,128)(2,1)S(1)}, bf16[24,6,16,128]{3,2,1,0:T(8,128)(2,1)S(1)}, u32[]{:S(2)}, u32[]{:S(2)}) collective-permute-start(bf16[24,6,16,128]{3,2,1,0:T(8,128)(2,1)S(1)} %pad_maximum_fusion.x_ref), channel_id=1, source_target_pairs={{8,0},{16,8},{24,16},{32,24},{40,32},{48,40},{56,48},{9,1},{17,9},... | collective-permute-start | bytes 1769480 | tf_op jit(solution)/shard_map/ppermute | solution.py:622
  30.7 1.9 %collective-permute-start.4 = (bf16[24,6,16,128]{3,2,1,0:T(8,128)(2,1)S(1)}, bf16[24,6,16,128]{3,2,1,0:T(8,128)(2,1)S(1)}, u32[]{:S(2)}, u32[]{:S(2)}) collective-permute-start(bf16[24,6,16,128]{3,2,1,0:T(8,128)(2,1)S(1)} %pad_maximum_fusion.x_ref), channel_id=1, source_target_pairs={{0,8},{8,16},{16,24},{24,32},{32,40},{40,48},{48,56},{1,9},{9,17},... | collective-permute-start | bytes 1769480 | tf_op jit(solution)/shard_map/ppermute | solution.py:622
  32.7 2.3 %collective-permute-done.5.yp_ref = bf16[24,6,16,128]{3,2,1,0:T(8,128)(2,1)S(1)} collective-permute-done((bf16[24,6,16,128]{3,2,1,0:T(8,128)(2,1)S(1)}, bf16[24,6,16,128]{3,2,1,0:T(8,128)(2,1)S(1)}, u32[]{:S(2)}, u32[]{:S(2)}) %collective-permute-start.5) | collective-permute-done | bytes 589856 | tf_op jit(solution)/shard_map/ppermute | solution.py:622
  35.0 4.5 %collective-permute-done.4.ym_ref = bf16[24,6,16,128]{3,2,1,0:T(8,128)(2,1)S(1)} collective-permute-done((bf16[24,6,16,128]{3,2,1,0:T(8,128)(2,1)S(1)}, bf16[24,6,16,128]{3,2,1,0:T(8,128)(2,1)S(1)}, u32[]{:S(2)}, u32[]{:S(2)}) %collective-permute-start.4) | collective-permute-done | bytes 589856 | tf_op jit(solution)/shard_map/ppermute | solution.py:622
  39.5 8.9 %shard_map.60 = (f32[24,40,256]{2,1,0:T(8,128)S(1)}, f32[25,40,256]{2,1,0:T(8,128)S(1)}, f32[24,40,256]{2,1,0:T(8,128)S(1)}, f32[24,40,256]{2,1,0:T(8,128)S(1)},...) custom-call(bf16[24,6,16,128]{3,2,1,0:T(8,128)(2,1)S(1)} %pad_maximu, ...), custom_call_target="tpu_custom_call" | custom-call | tf_op jit(solution)/shard_map/pallas_call | solution.py:610
  48.4 23.3 %all_to_all.15.own_ref = f32[64,8,128]{2,1,0:T(8,128)S(1)} all-to-all(f32[64,8,128]{2,1,0:T(8,128)S(1)} %broadcast_in_dim.8), channel_id=1, replica_groups=mesh['gx'=8,'gy'=8,'gz'=8] {'gx','gy'}, dimensions={0} | all-to-all | bytes 524288 | tf_op jit(solution)/shard_map/all_to_all | solution.py:628
  71.7 1.3 collective-permute-start.9
  73.0 4.7 %collective-permute-start.8 = (f32[64,8,128]{2,1,0:T(8,128)S(1)}, f32[64,8,128]{2,1,0:T(8,128)S(1)}, u32[]{:S(2)}, u32[]{:S(2)}) collective-permute-start(f32[64,8,128]{2,1,0:T(8,128)S(1)} %all_to_all.15.own_ref), channel_id=1, source_target_pairs={{0,1},{1,2},{2,3},{3,4},{4,5},{5,6},{6,7},{8,9},{9,10},{10,11},{11... | collective-permute-start | bytes 786440 | tf_op jit(solution)/shard_map/ppermute | solution.py:622
  77.8 2.7 %collective-permute-start.6 = (f32[6,24,128]{2,1,0:T(8,128)S(1)}, f32[6,24,128]{2,1,0:T(8,128)S(1)}, u32[]{:S(2)}, u32[]{:S(2)}) collective-permute-start(f32[6,24,128]{2,1,0:T(8,128)S(1)} %get-tuple-element.43), channel_id=1, source_target_pairs={{0,64},{64,128},{128,192},{192,256},{256,320},{320,384},{384,448},... | collective-permute-start | bytes 221192 | tf_op jit(solution)/shard_map/ppermute | solution.py:622
  80.4 1.3 collective-permute-start.7
  81.8 3.7 %collective-permute-done.7.high_ref = f32[6,24,128]{2,1,0:T(8,128)S(1)} collective-permute-done((f32[6,24,128]{2,1,0:T(8,128)S(1)}, f32[6,24,128]{2,1,0:T(8,128)S(1)}, u32[]{:S(2)}, u32[]{:S(2)}) %collective-permute-start.7) | collective-permute-done | bytes 73760 | tf_op jit(solution)/shard_map/ppermute | solution.py:622
  85.5 10.5 %shard_map.61 = (f32[8,16,128]{2,1,0:T(8,128)S(1)}, f32[8,16,128]{2,1,0:T(8,128)S(1)}, f32[24,40,256]{2,1,0:T(8,128)S(1)}, f32[16,24,128]{2,1,0:T(8,128)S(1)}, f...) custom-call(f32[24,40,256]{2,1,0:T(8,128)S(1)} %get-tuple-element.40, ...), custom_call_target="tpu_custom_call" | custom-call | tf_op jit(solution)/shard_map/pallas_call | solution.py:610
  96.0 18.0 %all_to_all.16 = f32[64,4,128]{2,1,0:T(4,128)S(1)} all-to-all(f32[64,4,128]{2,1,0:T(4,128)S(1)} %broadcast_in_dim.9), channel_id=1, replica_groups=mesh['gx'=8,'gy'=8,'gz'=8] {'gx','gy'}, dimensions={0} | all-to-all | bytes 262144 | tf_op jit(solution)/shard_map/all_to_all | solution.py:628
  114.1 1.3 collective-permute-start.11
  115.4 4.6 %collective-permute-start.10 = (f32[32,8,128]{2,1,0:T(8,128)S(1)}, f32[32,8,128]{2,1,0:T(8,128)S(1)}, u32[]{:S(2)}, u32[]{:S(2)}) collective-permute-start(f32[32,8,128]{2,1,0:T(8,128)S(1)} %bitcast.3), channel_id=1, source_target_pairs={{0,1},{1,2},{2,3},{3,4},{4,5},{5,6},{6,7},{8,9},{9,10},{10,11},{11... | collective-permute-start | bytes 393224 | tf_op jit(solution)/shard_map/ppermute | solution.py:622
  120.0 1.6 %collective-permute-done.11.after_ref = f32[32,8,128]{2,1,0:T(8,128)S(1)} collective-permute-done((f32[32,8,128]{2,1,0:T(8,128)S(1)}, f32[32,8,128]{2,1,0:T(8,128)S(1)}, u32[]{:S(2)}, u32[]{:S(2)}) %collective-permute-start.11) | collective-permute-done | bytes 131104 | tf_op jit(solution)/shard_map/ppermute | solution.py:622
  121.6 0.9 collective-permute-done.10.before_ref
  122.5 3.0 %shard_map.62 = (f32[8,16,128]{2,1,0:T(8,128)S(1)}, f32[1,128]{1,0:T(1,128)S(1)}) custom-call(f32[25,40,256]{2,1,0:T(8,128)S(1)} %get-tuple-element.32.f0_ref, f32[24,40,256]{2,1,0:T(8,128)S(1)} %get-tuple-element.33.f1_ref, f32[24,40,256]{2,1,0:T(8,128)S(1)} %get-tuple-element.34.f2_ref, f32[24,40,256]{2,1,0:T(8,128)S(1)} %get-tuple-element.35.w_ref, ...), custom_call_target="tpu_custom_call" | custom-call | tf_op jit(solution)/shard_map/pallas_call | solution.py:610
  125.4 19.1 %all_to_all.17.sums_ref = f32[8,1,128]{2,1,0:T(1,128)S(1)} all-to-all(f32[8,1,128]{2,1,0:T(1,128)S(1)} %broadcast_in_dim.11), channel_id=1, replica_groups=mesh['gx'=8,'gy'=8,'gz'=8] {'gz'}, dimensions={0} | all-to-all | bytes 8192 | tf_op jit(solution)/shard_map/all_to_all | solution.py:687
  144.6 0.8 shard_map.63
  (13 shorter events, 0.5 us)
Async XLA Ops:
  0.6 0.8 copy-start
  1.5 0.9 copy-start.2
  2.4 0.8 copy-start.3
  3.5 7.5 %collective-permute-start.1 = (bf16[8,5,16,128]{3,2,1,0:T(8,128)(2,1)S(1)}, bf16[8,5,16,128]{3,2,1,0:T(8,128)(2,1)S(1)}, u32[]{:S(2)}, u32[]{:S(2)}) collective-permute-start(bf16[8,5,16,128]{3,2,1,0:T(8,128)(2,1)S(1)} %shard_map.58.own_ref), channel_id=1, source_target_pairs={{1,0},{2,1},{3,2},{4,3},{5,4},{6,5},{7,6},{9,8},{10,9},{11,10},{12... | collective-permute-start | bytes 491528 | tf_op jit(solution)/shard_map/ppermute | solution.py:622
  4.8 7.7 %collective-permute-start = (bf16[8,5,16,128]{3,2,1,0:T(8,128)(2,1)S(1)}, bf16[8,5,16,128]{3,2,1,0:T(8,128)(2,1)S(1)}, u32[]{:S(2)}, u32[]{:S(2)}) collective-permute-start(bf16[8,5,16,128]{3,2,1,0:T(8,128)(2,1)S(1)} %shard_map.58.own_ref), channel_id=1, source_target_pairs={{0,1},{1,2},{2,3},{3,4},{4,5},{5,6},{6,7},{8,9},{9,10},{10,11},{11... | collective-permute-start | bytes 491528 | tf_op jit(solution)/shard_map/ppermute | solution.py:622
  13.2 6.9 %collective-permute-start.3 = (bf16[8,6,16,128]{3,2,1,0:T(8,128)(2,1)S(1)}, bf16[8,6,16,128]{3,2,1,0:T(8,128)(2,1)S(1)}, u32[]{:S(2)}, u32[]{:S(2)}) collective-permute-start(bf16[8,6,16,128]{3,2,1,0:T(8,128)(2,1)S(1)} %shard_map.59), channel_id=1, source_target_pairs={{64,0},{128,64},{192,128},{256,192},{320,256},{384,320},{448,384},... | collective-permute-start | bytes 589832 | tf_op jit(solution)/shard_map/ppermute | solution.py:622
  14.5 7.0 %collective-permute-start.2 = (bf16[8,6,16,128]{3,2,1,0:T(8,128)(2,1)S(1)}, bf16[8,6,16,128]{3,2,1,0:T(8,128)(2,1)S(1)}, u32[]{:S(2)}, u32[]{:S(2)}) collective-permute-start(bf16[8,6,16,128]{3,2,1,0:T(8,128)(2,1)S(1)} %shard_map.59), channel_id=1, source_target_pairs={{0,64},{64,128},{128,192},{192,256},{256,320},{320,384},{384,448},... | collective-permute-start | bytes 589832 | tf_op jit(solution)/shard_map/ppermute | solution.py:622
  21.6 13.4 %collective-permute-start.5 = (bf16[24,6,16,128]{3,2,1,0:T(8,128)(2,1)S(1)}, bf16[24,6,16,128]{3,2,1,0:T(8,128)(2,1)S(1)}, u32[]{:S(2)}, u32[]{:S(2)}) collective-permute-start(bf16[24,6,16,128]{3,2,1,0:T(8,128)(2,1)S(1)} %pad_maximum_fusion.x_ref), channel_id=1, source_target_pairs={{8,0},{16,8},{24,16},{32,24},{40,32},{48,40},{56,48},{9,1},{17,9},... | collective-permute-start | bytes 1769480 | tf_op jit(solution)/shard_map/ppermute | solution.py:622
  30.7 8.7 %collective-permute-start.4 = (bf16[24,6,16,128]{3,2,1,0:T(8,128)(2,1)S(1)}, bf16[24,6,16,128]{3,2,1,0:T(8,128)(2,1)S(1)}, u32[]{:S(2)}, u32[]{:S(2)}) collective-permute-start(bf16[24,6,16,128]{3,2,1,0:T(8,128)(2,1)S(1)} %pad_maximum_fusion.x_ref), channel_id=1, source_target_pairs={{0,8},{8,16},{16,24},{24,32},{32,40},{40,48},{48,56},{1,9},{9,17},... | collective-permute-start | bytes 1769480 | tf_op jit(solution)/shard_map/ppermute | solution.py:622
  71.7 13.8 %collective-permute-start.9 = (f32[64,8,128]{2,1,0:T(8,128)S(1)}, f32[64,8,128]{2,1,0:T(8,128)S(1)}, u32[]{:S(2)}, u32[]{:S(2)}) collective-permute-start(f32[64,8,128]{2,1,0:T(8,128)S(1)} %all_to_all.15.own_ref), channel_id=1, source_target_pairs={{1,0},{2,1},{3,2},{4,3},{5,4},{6,5},{7,6},{9,8},{10,9},{11,10},{12... | collective-permute-start | bytes 786440 | tf_op jit(solution)/shard_map/ppermute | solution.py:622
  73.0 12.5 %collective-permute-start.8 = (f32[64,8,128]{2,1,0:T(8,128)S(1)}, f32[64,8,128]{2,1,0:T(8,128)S(1)}, u32[]{:S(2)}, u32[]{:S(2)}) collective-permute-start(f32[64,8,128]{2,1,0:T(8,128)S(1)} %all_to_all.15.own_ref), channel_id=1, source_target_pairs={{0,1},{1,2},{2,3},{3,4},{4,5},{5,6},{6,7},{8,9},{9,10},{10,11},{11... | collective-permute-start | bytes 786440 | tf_op jit(solution)/shard_map/ppermute | solution.py:622
  77.8 4.1 %collective-permute-start.6 = (f32[6,24,128]{2,1,0:T(8,128)S(1)}, f32[6,24,128]{2,1,0:T(8,128)S(1)}, u32[]{:S(2)}, u32[]{:S(2)}) collective-permute-start(f32[6,24,128]{2,1,0:T(8,128)S(1)} %get-tuple-element.43), channel_id=1, source_target_pairs={{0,64},{64,128},{128,192},{192,256},{256,320},{320,384},{384,448},... | collective-permute-start | bytes 221192 | tf_op jit(solution)/shard_map/ppermute | solution.py:622
  80.4 5.1 %collective-permute-start.7 = (f32[6,24,128]{2,1,0:T(8,128)S(1)}, f32[6,24,128]{2,1,0:T(8,128)S(1)}, u32[]{:S(2)}, u32[]{:S(2)}) collective-permute-start(f32[6,24,128]{2,1,0:T(8,128)S(1)} %get-tuple-element.44), channel_id=1, source_target_pairs={{64,0},{128,64},{192,128},{256,192},{320,256},{384,320},{448,384},... | collective-permute-start | bytes 221192 | tf_op jit(solution)/shard_map/ppermute | solution.py:622
  114.1 7.5 %collective-permute-start.11 = (f32[32,8,128]{2,1,0:T(8,128)S(1)}, f32[32,8,128]{2,1,0:T(8,128)S(1)}, u32[]{:S(2)}, u32[]{:S(2)}) collective-permute-start(f32[32,8,128]{2,1,0:T(8,128)S(1)} %bitcast.2), channel_id=1, source_target_pairs={{1,0},{2,1},{3,2},{4,3},{5,4},{6,5},{7,6},{9,8},{10,9},{11,10},{12... | collective-permute-start | bytes 393224 | tf_op jit(solution)/shard_map/ppermute | solution.py:622
  115.4 7.1 %collective-permute-start.10 = (f32[32,8,128]{2,1,0:T(8,128)S(1)}, f32[32,8,128]{2,1,0:T(8,128)S(1)}, u32[]{:S(2)}, u32[]{:S(2)}) collective-permute-start(f32[32,8,128]{2,1,0:T(8,128)S(1)} %bitcast.3), channel_id=1, source_target_pairs={{0,1},{1,2},{2,3},{3,4},{4,5},{5,6},{6,7},{8,9},{9,10},{10,11},{11... | collective-permute-start | bytes 393224 | tf_op jit(solution)/shard_map/ppermute | solution.py:622
  122.5 22.1 %copy-start.1 = (f32[8,16,128]{2,1,0:T(8,128)S(1)}, f32[8,16,128]{2,1,0:T(8,128)}, u32[]{:S(2)}) copy-start(f32[8,16,128]{2,1,0:T(8,128)} %s_ref.1) | copy-start | bytes 196612

commit v3 on v2

--- a/solution.py
+++ b/solution.py
@@ -89,7 +89,7 @@
         r_ref[q, pl.ds(0, 20), pl.ds(128 * half, 128)] = halves[half]
 
 
-def prepare_kernel(s_hbm, fc_hbm, solid_hbm, out_ref, s_ref, fc_ref, solid_ref, sems):
+def prepare_kernel(s_hbm, fc_hbm, solid_hbm, out_ref, ends_ref, s_ref, fc_ref, solid_ref, sems):
     copies = [
         pltpu.make_async_copy(source, target, sems.at[i])
         for i, (source, target) in enumerate(
@@ -107,22 +107,27 @@
     weight = 1.0 - 0.75 * solid_ref[...].astype(F32)
     for a in range(3):
         out_ref[:, 2 + a] = (fc_ref[a].astype(F32) * weight).astype(BF16)
+    lane = iota((16, 128), 1)
+
+    def body(p, carry):
+        ends = jnp.zeros((16, 128), F32)
+        for f in range(5):
+            t = turn(out_ref[p, f].astype(F32), 24 * f + 12, 1)
+            ends = jnp.where((lane >= 24 * f) & (lane < 24 * f + 24), t, ends)
+        ends_ref[p] = ends.astype(BF16)
+        return carry
+
+    lax.fori_loop(0, 8, body, 0, unroll=4)
 
 
 def rim_kernel(own_ref, before_ref, after_ref, out_ref):
-    lane = iota((16, 128), 1)
-
-    def body(p, carry):
-        rim = jnp.zeros((16, 128), F32)
-        for f in range(5):
-            out_ref[p, f] = own_ref[p, f]
-            t = jnp.where(lane < 64, after_ref[p, f].astype(F32), before_ref[p, f].astype(F32))
-            t = turn(t, 24 * f + 12, 1)
-            rim = jnp.where((lane >= 24 * f) & (lane < 24 * f + 24), t, rim)
-        out_ref[p, 5] = rim.astype(BF16)
-        return carry
-
-    lax.fori_loop(0, 8, body, 0)
+    lane = iota((8, 16, 128), 2)
+    last = jnp.zeros((8, 16, 128), jnp.bool_)
+    for f in range(5):
+        last = last | ((lane >= 24 * f) & (lane < 24 * f + 12))
+    out_ref[:, 0:5] = own_ref[...]
+    rim = jnp.where(last, before_ref[...].astype(F32), after_ref[...].astype(F32))
+    out_ref[:, 5] = rim.astype(BF16)
 
 
 def first_kernel(
@@ -155,7 +160,7 @@
             c_ref[p, :, 128:256] = rims[2 + a]
         return carry
 
-    lax.fori_loop(0, 24, unpack, 0)
+    lax.fori_loop(0, 24, unpack, 0, unroll=4)
 
     def faces(p, carry):
         before = jnp.maximum(p - 1, 0)
@@ -166,7 +171,7 @@
         f2_ref[p] = root(c2 * turn(c2, 1, 1))
         return carry
 
-    lax.fori_loop(0, 24, faces, 0)
+    lax.fori_loop(0, 24, faces, 0, unroll=4)
     f0_ref[24] = jnp.zeros((40, 256), F32)
 
     first_row = (iota((40, 256), 0) == 12) & at_y
@@ -193,7 +198,7 @@
         put_rows(r2_ref, q, row_pairs(t_ref, lows[0][2] + lows[1][2], True))
         return carry
 
-    lax.fori_loop(0, 12, diagonals, 0)
+    lax.fori_loop(0, 12, diagonals, 0, unroll=2)
 
     def leftovers(q, carry):
         total = jnp.zeros((40, 256), F32)
@@ -203,7 +208,7 @@
         put_rows(rs_ref, q, row_pairs(t_ref, total, True))
         return carry
 
-    lax.fori_loop(1, 11, leftovers, 0)
+    lax.fori_loop(1, 11, leftovers, 0, unroll=2)
 
     pairs = one_hot(256, 128, lambda r, c: lax.shift_right_logical(r, 1) == c, 0.25)
     evens = one_hot(256, 128, lambda r, c: r == 2 * c, 0.25)
@@ -224,7 +229,7 @@
         f12_ref[p] = jnp.where(first_lane_1, 0.0, l12_ref[p])
         return carry
 
-    lax.fori_loop(0, 16, faces_1, 0)
+    lax.fori_loop(0, 16, faces_1, 0, unroll=4)
     f10_ref[16] = jnp.zeros((24, 128), F32)
 
     def diagonals_1(p, carry):
@@ -238,7 +243,7 @@
         sm1_ref[p] = w * s1_ref[p]
         return carry
 
-    lax.fori_loop(2, 14, diagonals_1, 0)
+    lax.fori_loop(2, 14, diagonals_1, 0, unroll=4)
     for i, ref in enumerate((s1_ref, w1_ref, f10_ref)):
         up_ref[pl.ds(2 * i, 2)] = ref[pl.ds(5, 2)]
         down_ref[pl.ds(2 * i, 2)] = ref[pl.ds(9, 2)]
@@ -251,6 +256,9 @@
     def leftover_1(p):
         return KEEP * s1_ref[p] + neighbours(sm1_ref, f10_ref, f11_ref, f12_ref, p)
 
+    row8, lane8 = iota((8, 128), 0), iota((8, 128), 1)
+    narrow = one_hot(128, 128, lambda r, c: (lax.shift_right_logical(r, 1) == c) & (r < 64))
+    narrow_even = one_hot(128, 128, lambda r, c: (r == 2 * c) & (r < 64))
     total = jnp.zeros((8, 128), F32)
     for f in range(4):
         for i in range(2):
@@ -263,17 +271,22 @@
                 part = quad(l11_ref[p] + l11_ref[p + 1], False)
             else:
                 part = quad(l12_ref[p] + l12_ref[p + 1], True)
-            u_ref[pl.ds(4 * i, 4), :] = part
-        place = one_hot(
-            128, 128,
-            lambda r, c, f=f: (
-                ((lax.shift_right_logical(r, 1) + 32 * f == c) if f < 3 else (r + 192 == 2 * c))
-                & (r < 64)
-            ),
-            0.5 if f == 0 else 0.25,
-        )
-        total += spread(u_ref[...], place)
+            u_ref[f, pl.ds(4 * i, 4), :] = part * (0.5 if f == 0 else 0.25)
+        part = spread(u_ref[f], narrow_even if f == 3 else narrow)
+        for i in range(2):
+            for h in range(2):
+                to = 32 * f + 16 * i
+                moved = turn(turn(part, 4 * (h - i), 0), to - 16 * h, 1)
+                here = (lax.shift_right_logical(row8, 2) == h) & (lane8 >= to) & (lane8 < to + 16)
+                total = jnp.where(here, moved, total)
     pay_ref[...] = total
+
+
+def window(pieces, to, lane):
+    out = jnp.zeros(pieces[0].shape, F32)
+    for k, piece in enumerate(pieces):
+        out = jnp.where((lane >= 16 * k) & (lane < 16 * k + 16), turn(piece, 16 * k - to, 1), out)
+    return out
 
 
 def solve_2(s2, level_2, level_3, t3_ref, e_ref):
@@ -354,7 +367,7 @@
 def second_kernel(
     s_ref, f0_ref, f1_ref, f2_ref, w_ref, d_ref,
     s1_ref, f10_ref, f11_ref, f12_ref, w1_ref,
-    low_ref, high_ref, own_ref, before_ref, after_ref,
+    low_ref, high_ref, before_ref, own0_ref, own1_ref, after_ref,
     fp_out, im_out, im_ref, t1s_ref, f20_ref, f21_ref, f22_ref, w2_ref,
     f30_ref, f31_ref, f32_ref, w3_ref, pay_ref,
     v_ref, t3_ref, e_ref, m2_ref, pick_ref, corr1_ref, m1_ref, wide_ref, t_ref,
@@ -366,23 +379,11 @@
 
     def assemble(x, carry):
         for pair in range(ny2 // 8):
+            g = x * (ny2 // 8) + pair
+            pieces = [ref[g] for ref in (before_ref, own0_ref, own1_ref, after_ref)]
             for f in range(4):
-                tiles = []
-                for j in range(2):
-                    g = x * (ny2 // 4) + 2 * pair + j
-                    t = jnp.where(
-                        lane8 < 16,
-                        turn(before_ref[g], -(32 * f + 16), 1),
-                        jnp.where(
-                            lane8 < 48,
-                            turn(own_ref[g], 16 - 32 * f, 1),
-                            turn(after_ref[g], 48 - 32 * f, 1),
-                        ),
-                    )
-                    tiles.append(jnp.where(lane8 < 64, t, 0.0))
-                rows = pl.ds(8 * pair, 8)
-                v_ref[f, 2 * x, rows, :] = jnp.where(row8 < 4, tiles[0], turn(tiles[1], 4, 0))
-                v_ref[f, 2 * x + 1, rows, :] = jnp.where(row8 < 4, turn(tiles[0], 4, 0), tiles[1])
+                for i in range(2):
+                    v_ref[f, 2 * x + i, pl.ds(8 * pair, 8), :] = window(pieces, 32 * f + 16 * i, lane8)
         return carry
 
     lax.fori_loop(0, nx2 // 2, assemble, 0)
@@ -407,7 +408,7 @@
         corr1_ref[p] = w1_ref[p] * s1_ref[p] + pick_ref[lax.shift_right_logical(p, 1)]
         return carry
 
-    lax.fori_loop(3, 13, correct_1, 0)
+    lax.fori_loop(3, 13, correct_1, 0, unroll=5)
     for k in range(2):
         corr1_ref[1 + k] = low_ref[2 + k] * low_ref[k] + pick_ref[(1 + k) // 2]
         corr1_ref[13 + k] = high_ref[2 + k] * high_ref[k] + pick_ref[(13 + k) // 2]
@@ -418,7 +419,7 @@
         )
         return carry
 
-    lax.fori_loop(3, 13, relax_1, 0)
+    lax.fori_loop(3, 13, relax_1, 0, unroll=5)
     for p, source, w, face, next_face in (
         (2, low_ref[1], low_ref[3], low_ref[5], f10_ref[3]),
         (13, high_ref[0], high_ref[2], f10_ref[13], high_ref[5]),
@@ -436,7 +437,7 @@
             corr_ref[p] = w_ref[p] * s_ref[p] + e
         return carry
 
-    lax.fori_loop(2, 14, correct, 0)
+    lax.fori_loop(2, 14, correct, 0, unroll=2)
 
     def relax(p, carry):
         fp_ref[p] = KEEP * corr_ref[p] + w_ref[p] * (
@@ -444,7 +445,7 @@
         )
         return carry
 
-    lax.fori_loop(2, 22, relax, 0)
+    lax.fori_loop(2, 22, relax, 0, unroll=4)
 
     def image(p, carry):
         im = d_ref[p] * fp_ref[p] - neighbours(fp_ref, f0_ref, f1_ref, f2_ref, p)
@@ -452,7 +453,7 @@
         sm_ref[p] = w_ref[p] * im
         return carry
 
-    lax.fori_loop(3, 21, image, 0)
+    lax.fori_loop(3, 21, image, 0, unroll=3)
 
     rs_ref[...] = jnp.zeros_like(rs_ref)
     inside = (iota((40, 128), 0) >= 12) & (iota((40, 128), 0) < 28)
@@ -474,7 +475,7 @@
         return sums
 
     zero = jnp.zeros((40, 128), F32)
-    sums = lax.fori_loop(4, 12, leftovers, (zero, zero, zero))
+    sums = lax.fori_loop(4, 12, leftovers, (zero, zero, zero), unroll=2)
 
     for p in range(8):
         fp_out[p] = fp_ref[8 + p, pl.ds(12, 16), 0:128]
@@ -489,7 +490,7 @@
         (iota((24, 128), 0) >= 6) & (iota((24, 128), 0) < 14) & (iota((24, 128), 1) < 64), 1.0, 0.0
     )
     second = jnp.zeros((24, 128), F32)
-    pay = jnp.zeros((8, 128), F32)
+    halves = [jnp.zeros((8, 128), F32)] * 2
     tq_ref[...] = jnp.zeros_like(tq_ref)
     for i in range(2):
         total = jnp.zeros((24, 128), F32)
@@ -501,53 +502,50 @@
             total += left
         tq_ref[pl.ds(0, 24), :] = total
         tq_ref[pl.ds(24, 4), :] = tq_ref[pl.ds(6, 4, 2), :] + tq_ref[pl.ds(7, 4, 2), :]
-        place = one_hot(
-            128, 128,
-            lambda r, c, i=i: (lax.shift_right_logical(r, 1) + 32 * i == c) & (r < 64), 0.5,
-        )
-        pay += spread(tq_ref[pl.ds(24, 8), :], place)
+        for h in range(2):
+            place = one_hot(
+                128, 128,
+                lambda r, c, i=i, h=h: (lax.shift_right_logical(r, 1) - 16 * h == (c & 15))
+                & (r < 64) & ((lax.shift_right_logical(c, 4) & 1) == i), 0.5,
+            )
+            halves[h] += spread(tq_ref[pl.ds(24, 8), :], place)
     scalars = (jnp.sum(sums[0]), jnp.sum(sums[1]), jnp.sum(sums[2]) + 2.0 * jnp.sum(second))
+    mine = lax.shift_right_logical(lane8, 5) == row8
+    pay = jnp.zeros((8, 128), F32)
+    for h in range(2):
+        line = jnp.sum(jnp.where(mine, halves[h], 0.0), axis=0, keepdims=True)
+        pay = jnp.where(row8 == h, line, pay)
     for k, value in enumerate(scalars):
-        pay = jnp.where((lane8 == 64 + k) & (row8 == 0), value, pay)
+        pay = jnp.where((lane8 == k) & (row8 == 2), value, pay)
     pay_ref[...] = pay[:4]
 
 
 def third_kernel(
     f0_ref, f1_ref, f2_ref, w_ref, f10_ref, f11_ref, f12_ref, w1_ref,
     im_ref, t1s_ref, f20_ref, f21_ref, f22_ref, w2_ref, f30_ref, f31_ref, f32_ref, w3_ref,
-    own_ref, before_ref, after_ref,
+    before_ref, own0_ref, own1_ref, after_ref, parts_ref,
     mi_out, scalar_out,
     v_ref, t3_ref, e_ref, m2_ref, pick_ref, corr1_ref, m1_ref, wide_ref, t_ref, corr_ref,
 ):
     nx2, ny2 = f20_ref.shape[:2]
-    lane8 = iota((8, 128), 1)
-
-    def assemble(x, acc):
-        for pair in range(ny2 // 8):
-            g = x * (ny2 // 8) + pair
-            acc = acc + own_ref[g]
-            for i in range(2):
-                t = jnp.where(
-                    lane8 < 16,
-                    turn(before_ref[g], -(32 * i + 16), 1),
-                    jnp.where(
-                        lane8 < 48,
-                        turn(own_ref[g], 16 - 32 * i, 1),
-                        turn(after_ref[g], 48 - 32 * i, 1),
-                    ),
-                )
-                v_ref[2 * x + i, pl.ds(8 * pair, 8), :] = jnp.where(lane8 < 64, t, 0.0)
-        return acc
-
-    acc = lax.fori_loop(0, nx2 // 2, assemble, jnp.zeros((8, 128), F32))
+    lane = iota((ny2 // 4, 128), 1)
+
+    def assemble(x, carry):
+        pieces = [ref[x] for ref in (before_ref, own0_ref, own1_ref, after_ref)]
+        for i in range(2):
+            for j in range(4):
+                v_ref[2 * x + i, pl.ds(j, ny2 // 4, 4), :] = window(pieces, 32 * j + 16 * i, lane)
+        return carry
+
+    lax.fori_loop(0, nx2 // 2, assemble, 0, unroll=2)
     s2 = v_ref[...]
     level_2 = (f20_ref[...], f21_ref[...], f22_ref[...], w2_ref[...])
     level_3 = (f30_ref[...], f31_ref[...], f32_ref[...], w3_ref[...])
     m2 = solve_2(s2, level_2, level_3, t3_ref, e_ref)
     lane3 = iota(s2.shape, 2)
     part = 4.0 * jnp.sum(jnp.where((lane3 >= 16) & (lane3 < 48), s2 * m2, 0.0))
-    sums = jnp.sum(acc, axis=0, keepdims=True)
-    scalar_out[...] = jnp.where(iota((1, 128), 1) == 67, part, sums)
+    sums = jnp.sum(jnp.sum(parts_ref[...], axis=0), axis=0, keepdims=True)
+    scalar_out[...] = jnp.where(iota((1, 128), 1) == 3, part, sums)
     m2_ref[...] = jnp.zeros_like(m2_ref)
     m2_ref[pl.ds(3, nx2)] = m2
     fetch_level_2(m2_ref, range(2, 6), pick_ref)
@@ -566,7 +564,7 @@
             corr_ref[p] = w_ref[p] * im_ref[p] + e
         return carry
 
-    lax.fori_loop(5, 11, correct, 0)
+    lax.fori_loop(5, 11, correct, 0, unroll=2)
 
     for p in range(8):
         q = 8 + p
@@ -587,7 +585,7 @@
             keep = keep | (lane == k)
         return jnp.sum(jnp.where(keep, total, 0.0), axis=1, keepdims=True)
 
-    projected, curvature, product = value((64,)), value((65,)), value((66, 67))
+    projected, curvature, product = value((0,)), value((1,)), value((2, 3))
     step = projected / curvature
     share = product / curvature
     for p in range(8):
@@ -600,7 +598,7 @@
 def call(kernel, inputs, outs, scratch=(), keep_in=(), keep_out=(), space=pltpu.VMEM):
     vmem = pl.BlockSpec(memory_space=pltpu.VMEM)
     inputs = [
-        pltpu.with_memory_space_constraint(value, pltpu.VMEM) if i in keep_in else value
+        pltpu.with_memory_space_constraint(value, space) if i in keep_in else value
         for i, value in enumerate(inputs)
     ]
     shapes = [
@@ -624,25 +622,26 @@
 
 def gather_plane(value):
     peers = lax.axis_size(("gx", "gy"))
-    copies = jnp.broadcast_to(value[None], (peers,) + value.shape)
+    copies = jnp.broadcast_to(value.reshape(1, 1, -1), (peers, 1, value.size))
     return lax.all_to_all(copies, ("gx", "gy"), 0, 0, tiled=True)
 
 
 def local(right_side, face_coefficients, solid):
     nx2, ny2 = 2 * lax.axis_size("gx"), 4 * lax.axis_size("gy")
-    (own,) = call(
+    own, ends = call(
         prepare_kernel,
         [right_side, face_coefficients, solid],
-        [((8, 5, 16, 128), BF16)],
+        [((8, 5, 16, 128), BF16), ((8, 16, 128), BF16)],
         [
             (8, 16, 128),
             pltpu.VMEM((3, 8, 16, 128), BF16),
             pltpu.VMEM((8, 16, 128), jnp.int32),
             pltpu.SemaphoreType.DMA((3,)),
         ],
+        keep_in=range(3),
         space=pltpu.HBM,
     )
-    before, after = shift_along(own, "gz", 1), shift_along(own, "gz", -1)
+    before, after = shift_along(ends, "gz", 1), shift_along(ends, "gz", -1)
     (own,) = call(rim_kernel, [own, before, after], [((8, 6, 16, 128), BF16)])
     block = jnp.concatenate([shift_along(own, "gx", 1), own, shift_along(own, "gx", -1)], axis=0)
     before, after = shift_along(block, "gy", 1), shift_along(block, "gy", -1)
@@ -654,18 +653,20 @@
         first_kernel,
         [block, before, after],
         [(shape, F32) for shape in (fine, fine_up, fine, fine, fine, fine, mid, mid_up, mid, mid, mid, edge, edge, (8, 128))],
-        [fine, fine, fine, fine, (2, 40, 128), rows, rows, rows, rows, mid, mid, mid, mid, (24, 128), (8, 128)],
+        [fine, fine, fine, fine, (2, 40, 128), rows, rows, rows, rows, mid, mid, mid, mid, (24, 128), (4, 8, 128)],
         keep_out=range(11),
     )
     low, high = shift_along(up, "gx", 1), shift_along(down, "gx", -1)
     own = gather_plane(pay)
-    before, after = shift_along(own, "gz", 1), shift_along(own, "gz", -1)
+    pairs = (nx2 * ny2 // 16, 8, 128)
+    own0, own1 = own[..., :512].reshape(pairs), own[..., 512:].reshape(pairs)
+    before, after = shift_along(own1, "gz", 1), shift_along(own0, "gz", -1)
     level_2, level_3 = (nx2, ny2, 128), (nx2 // 2, ny2 // 2, 128)
     window = (nx2 + 6, ny2, 128)
     half = (nx2 // 2, ny2, 128)
     first_pre, image, *more, pay = call(
         second_kernel,
-        [*state, low, high, own, before, after],
+        [*state, low, high, before, own0, own1, after],
         [((8, 16, 128), F32)] * 2
         + [(shape, F32) for shape in (fine, mid, *[level_2] * 4, *[level_3] * 4, (4, 128))],
         [(4,) + level_2, half, half, window, (8, 24, 128), mid, mid, wide, (2, 40, 128),
@@ -673,12 +674,14 @@
         keep_in=range(11),
         keep_out=range(2, 12),
     )
-    own = gather_plane(pay).reshape(nx2 * ny2 // 16, 8, 128)
-    before, after = shift_along(own, "gz", 1), shift_along(own, "gz", -1)
+    own = gather_plane(pay)
+    plane = (nx2 // 2, ny2 // 4, 128)
+    own0, own1, parts = (own[..., 128 * k : 128 * k + 128].reshape(plane) for k in range(3))
+    before, after = shift_along(own1, "gz", 1), shift_along(own0, "gz", -1)
     _, f0, f1, f2, w, _, _, f10, f11, f12, w1 = state
     mapped, sums = call(
         third_kernel,
-        [f0, f1, f2, w, f10, f11, f12, w1, *more, own, before, after],
+        [f0, f1, f2, w, f10, f11, f12, w1, *more, before, own0, own1, after, parts],
         [((8, 16, 128), F32), ((1, 128), F32)],
         [level_2, half, half, window, (8, 24, 128), mid, mid, wide, (2, 40, 128), fine],
         keep_in=range(18),

time: 147 us -> 134 us (0.912)
  Pallas kernels: 24.1 us -> 17.3 us
  waiting for transfers between devices: 17.9 us -> 15.2 us
  local copies, waits for them, and re-layouts: 2.62 us -> 0.33 us
    pallas_call x6, Pallas kernels: 24.1 us -> 17.3 us  [call(): pl.pallas_call(kernel, out_shape=shapes, in_specs=[pl.BlockSpec(memory_sp...]
    ppermute x12, waiting for transfers between devices: 17.9 us -> 15.2 us  [shift_along(): lax.ppermute(value, axis, [(i, i + by) for i in range(size) if 0 <= i + b...]
    unnamed x8 -> x2, local copies, waits for them, and re-layouts: 2.57 us -> 0.01 us
  transfers between devices with their start and end apart: 12 -> 12, of which waited for: 10 -> 8; matrix products, arithmetic and copies ran while one was open for 0% -> 0% of each run, Pallas kernels for 0% -> 0%
where the time goes in v3:
time: 134 us; the launch traced here: 133 us
  blocking collectives  59.9 us (45%)
  starting transfers between devices  39.3 us (29%)
  Pallas kernels  17.3 us (13%)
  waiting for transfers between devices  15.2 us (11%)
    all_to_all x2, blocking collectives, gather_plane(): return lax.all_to_all(copies, ('gx', 'gy'), 0, 0, tiled=True)  40.7 us
    ppermute x12, starting transfers between devices, shift_along(): lax.ppermute(value, axis, [(i, i + by) for i in range(size) if 0 <= i + b...  39.3 us
    all_to_all x1, blocking collectives, local(): lax.all_to_all(jnp.broadcast_to(sums[None], (peers, 1, 128)), 'gz', 0, 0,...  19.2 us
    pallas_call x6, Pallas kernels, call(): pl.pallas_call(kernel, out_shape=shapes, in_specs=[pl.BlockSpec(memory_sp...  17.3 us
    ppermute x12, waiting for transfers between devices, shift_along(): lax.ppermute(value, axis, [(i, i + by) for i in range(size) if 0 <= i + b...  15.2 us
  transfers between devices with their start and end apart: 12, of which 8 were waited for; matrix products, arithmetic and copies ran while one was open for 0% of the time, Pallas kernels for 0%

profile of v3, /device:TPU:1, one launch (start us, length us, event | category | flops | bytes accessed | tf_op | source)
XLA Modules:
  0.0 133.0 jit_solution(14722011907488166254)
XLA Ops:
  0.6 1.2 shard_map.58
  1.8 1.3 collective-permute-start.1
  3.1 5.5 %collective-permute-start = (bf16[8,16,128]{2,1,0:T(8,128)(2,1)S(1)}, bf16[8,16,128]{2,1,0:T(8,128)(2,1)S(1)}, u32[]{:S(2)}, u32[]{:S(2)}) collective-permute-start(bf16[8,16,128]{2,1,0:T(8,128)(2,1)S(1)} %get-tuple-element.35), channel_id=1, source_target_pairs={{0,1},{1,2},{2,3},{3,4},{4,5},{5,6},{6,7},{8,9},{9,10},{10,11},{11... | collective-permute-start | bytes 98312 | tf_op jit(solution)/shard_map/ppermute | solution.py:620
  8.6 1.0 collective-permute-done.before_ref
  9.6 1.3 collective-permute-start.3
  10.9 4.0 %collective-permute-start.2 = (bf16[8,6,16,128]{3,2,1,0:T(8,128)(2,1)S(1)}, bf16[8,6,16,128]{3,2,1,0:T(8,128)(2,1)S(1)}, u32[]{:S(2)}, u32[]{:S(2)}) collective-permute-start(bf16[8,6,16,128]{3,2,1,0:T(8,128)(2,1)S(1)} %shard_map.59), channel_id=1, source_target_pairs={{0,64},{64,128},{128,192},{192,256},{256,320},{320,384},{384,448},... | collective-permute-start | bytes 589832 | tf_op jit(solution)/shard_map/ppermute | solution.py:620
  14.9 1.1 collective-permute-done.3
  16.0 1.5 %collective-permute-done.2 = bf16[8,6,16,128]{3,2,1,0:T(8,128)(2,1)S(1)} collective-permute-done((bf16[8,6,16,128]{3,2,1,0:T(8,128)(2,1)S(1)}, bf16[8,6,16,128]{3,2,1,0:T(8,128)(2,1)S(1)}, u32[]{:S(2)}, u32[]{:S(2)}) %collective-permute-start.2) | collective-permute-done | bytes 196640 | tf_op jit(solution)/shard_map/ppermute | solution.py:620
  17.5 0.1 pad_maximum_fusion.x_ref
  17.6 9.6 %collective-permute-start.5 = (bf16[24,6,16,128]{3,2,1,0:T(8,128)(2,1)S(1)}, bf16[24,6,16,128]{3,2,1,0:T(8,128)(2,1)S(1)}, u32[]{:S(2)}, u32[]{:S(2)}) collective-permute-start(bf16[24,6,16,128]{3,2,1,0:T(8,128)(2,1)S(1)} %pad_maximum_fusion.x_ref), channel_id=1, source_target_pairs={{8,0},{16,8},{24,16},{32,24},{40,32},{48,40},{56,48},{9,1},{17,9},... | collective-permute-start | bytes 1769480 | tf_op jit(solution)/shard_map/ppermute | solution.py:620
  27.2 1.9 %collective-permute-start.4 = (bf16[24,6,16,128]{3,2,1,0:T(8,128)(2,1)S(1)}, bf16[24,6,16,128]{3,2,1,0:T(8,128)(2,1)S(1)}, u32[]{:S(2)}, u32[]{:S(2)}) collective-permute-start(bf16[24,6,16,128]{3,2,1,0:T(8,128)(2,1)S(1)} %pad_maximum_fusion.x_ref), channel_id=1, source_target_pairs={{0,8},{8,16},{16,24},{24,32},{32,40},{40,48},{48,56},{1,9},{9,17},... | collective-permute-start | bytes 1769480 | tf_op jit(solution)/shard_map/ppermute | solution.py:620
  29.1 1.7 %collective-permute-done.5.yp_ref = bf16[24,6,16,128]{3,2,1,0:T(8,128)(2,1)S(1)} collective-permute-done((bf16[24,6,16,128]{3,2,1,0:T(8,128)(2,1)S(1)}, bf16[24,6,16,128]{3,2,1,0:T(8,128)(2,1)S(1)}, u32[]{:S(2)}, u32[]{:S(2)}) %collective-permute-start.5) | collective-permute-done | bytes 589856 | tf_op jit(solution)/shard_map/ppermute | solution.py:620
  30.8 5.1 %collective-permute-done.4.ym_ref = bf16[24,6,16,128]{3,2,1,0:T(8,128)(2,1)S(1)} collective-permute-done((bf16[24,6,16,128]{3,2,1,0:T(8,128)(2,1)S(1)}, bf16[24,6,16,128]{3,2,1,0:T(8,128)(2,1)S(1)}, u32[]{:S(2)}, u32[]{:S(2)}) %collective-permute-start.4) | collective-permute-done | bytes 589856 | tf_op jit(solution)/shard_map/ppermute | solution.py:620
  35.9 4.9 %shard_map.60 = (f32[24,40,256]{2,1,0:T(8,128)S(1)}, f32[25,40,256]{2,1,0:T(8,128)S(1)}, f32[24,40,256]{2,1,0:T(8,128)S(1)}, f32[24,40,256]{2,1,0:T(8,128)S(1)},...) custom-call(bf16[24,6,16,128]{3,2,1,0:T(8,128)(2,1)S(1)} %pad_maximu, ...), custom_call_target="tpu_custom_call" | custom-call | tf_op jit(solution)/shard_map/pallas_call | solution.py:608
  40.8 0.1 broadcast_in_dim.23
  40.9 22.7 %all_to_all.15 = f32[64,1,1024]{2,1,0:T(1,128)S(1)} all-to-all(f32[64,1,1024]{2,1,0:T(1,128)S(1)} %broadcast_in_dim.23), channel_id=1, replica_groups=mesh['gx'=8,'gy'=8,'gz'=8] {'gx','gy'}, dimensions={0} | all-to-all | bytes 524288 | tf_op jit(solution)/shard_map/all_to_all | solution.py:626
  63.6 4.0 %collective-permute-start.8 = (f32[32,8,128]{2,1,0:T(8,128)S(1)}, f32[32,8,128]{2,1,0:T(8,128)S(1)}, u32[]{:S(2)}, u32[]{:S(2)}) collective-permute-start(f32[32,8,128]{2,1,0:T(8,128)S(1)} %bitcast.10), channel_id=1, source_target_pairs={{0,1},{1,2},{2,3},{3,4},{4,5},{5,6},{6,7},{8,9},{9,10},{10,11},{11... | collective-permute-start | bytes 393224 | tf_op jit(solution)/shard_map/ppermute | solution.py:620
  67.7 1.3 collective-permute-start.9
  69.0 2.7 %collective-permute-start.6 = (f32[6,24,128]{2,1,0:T(8,128)S(1)}, f32[6,24,128]{2,1,0:T(8,128)S(1)}, u32[]{:S(2)}, u32[]{:S(2)}) collective-permute-start(f32[6,24,128]{2,1,0:T(8,128)S(1)} %get-tuple-element.47), channel_id=1, source_target_pairs={{0,64},{64,128},{128,192},{192,256},{256,320},{320,384},{384,448},... | collective-permute-start | bytes 221192 | tf_op jit(solution)/shard_map/ppermute | solution.py:620
  71.6 1.3 collective-permute-start.7
  72.9 0.1 collective-permute-done.6.low_ref
  73.0 3.7 %collective-permute-done.7.high_ref = f32[6,24,128]{2,1,0:T(8,128)S(1)} collective-permute-done((f32[6,24,128]{2,1,0:T(8,128)S(1)}, f32[6,24,128]{2,1,0:T(8,128)S(1)}, u32[]{:S(2)}, u32[]{:S(2)}) %collective-permute-start.7) | collective-permute-done | bytes 73760 | tf_op jit(solution)/shard_map/ppermute | solution.py:620
  76.7 7.8 %shard_map.61 = (f32[8,16,128]{2,1,0:T(8,128)S(1)}, f32[8,16,128]{2,1,0:T(8,128)S(1)}, f32[24,40,256]{2,1,0:T(8,128)S(1)}, f32[16,24,128]{2,1,0:T(8,128)S(1)}, f...) custom-call(f32[24,40,256]{2,1,0:T(8,128)S(1)} %get-tuple-element.44, ...), custom_call_target="tpu_custom_call" | custom-call | tf_op jit(solution)/shard_map/pallas_call | solution.py:608
  84.5 0.1 broadcast_in_dim.25
  84.6 18.0 %all_to_all.16 = f32[64,1,512]{2,1,0:T(1,128)S(1)} all-to-all(f32[64,1,512]{2,1,0:T(1,128)S(1)} %broadcast_in_dim.25), channel_id=1, replica_groups=mesh['gx'=8,'gy'=8,'gz'=8] {'gx','gy'}, dimensions={0} | all-to-all | bytes 262144 | tf_op jit(solution)/shard_map/all_to_all | solution.py:626
  102.6 0.1 fusion.1
  102.7 1.3 collective-permute-start.11
  104.0 5.3 %collective-permute-start.10 = (f32[8,8,128]{2,1,0:T(8,128)S(1)}, f32[8,8,128]{2,1,0:T(8,128)S(1)}, u32[]{:S(2)}, u32[]{:S(2)}) collective-permute-start(f32[8,8,128]{2,1,0:T(8,128)S(1)} %bitcast.15), channel_id=1, source_target_pairs={{0,1},{1,2},{2,3},{3,4},{4,5},{5,6},{6,7},{8,9},{9,10},{10,11},{11... | collective-permute-start | bytes 98312 | tf_op jit(solution)/shard_map/ppermute | solution.py:620
  109.3 1.0 collective-permute-done.10.before_ref
  110.3 2.7 %shard_map.62 = (f32[8,16,128]{2,1,0:T(8,128)S(1)}, f32[1,128]{1,0:T(1,128)S(1)}) custom-call(f32[25,40,256]{2,1,0:T(8,128)S(1)} %get-tuple-element.36.f0_ref, f32[24,40,256]{2,1,0:T(8,128)S(1)} %get-tuple-element.37.f1_ref, f32[24,40,256]{2,1,0:T(8,128)S(1)} %get-tuple-element.38.f2_ref, f32[24,40,256]{2,1,0:T(8,128)S(1)} %get-tuple-element.39.w_ref, ...), custom_call_target="tpu_custom_call" | custom-call | tf_op jit(solution)/shard_map/pallas_call | solution.py:608
  113.0 19.2 %all_to_all.17.sums_ref = f32[8,1,128]{2,1,0:T(1,128)S(1)} all-to-all(f32[8,1,128]{2,1,0:T(1,128)S(1)} %broadcast_in_dim.27), channel_id=1, replica_groups=mesh['gx'=8,'gy'=8,'gz'=8] {'gz'}, dimensions={0} | all-to-all | bytes 8192 | tf_op jit(solution)/shard_map/all_to_all | solution.py:690
  132.2 0.8 shard_map.63
  (9 shorter events, 0.1 us)
Async XLA Ops:
  1.8 6.8 %collective-permute-start.1 = (bf16[8,16,128]{2,1,0:T(8,128)(2,1)S(1)}, bf16[8,16,128]{2,1,0:T(8,128)(2,1)S(1)}, u32[]{:S(2)}, u32[]{:S(2)}) collective-permute-start(bf16[8,16,128]{2,1,0:T(8,128)(2,1)S(1)} %get-tuple-element.35), channel_id=1, source_target_pairs={{1,0},{2,1},{3,2},{4,3},{5,4},{6,5},{7,6},{9,8},{10,9},{11,10},{12... | collective-permute-start | bytes 98312 | tf_op jit(solution)/shard_map/ppermute | solution.py:620
  3.1 6.5 %collective-permute-start = (bf16[8,16,128]{2,1,0:T(8,128)(2,1)S(1)}, bf16[8,16,128]{2,1,0:T(8,128)(2,1)S(1)}, u32[]{:S(2)}, u32[]{:S(2)}) collective-permute-start(bf16[8,16,128]{2,1,0:T(8,128)(2,1)S(1)} %get-tuple-element.35), channel_id=1, source_target_pairs={{0,1},{1,2},{2,3},{3,4},{4,5},{5,6},{6,7},{8,9},{9,10},{10,11},{11... | collective-permute-start | bytes 98312 | tf_op jit(solution)/shard_map/ppermute | solution.py:620
  9.6 6.4 %collective-permute-start.3 = (bf16[8,6,16,128]{3,2,1,0:T(8,128)(2,1)S(1)}, bf16[8,6,16,128]{3,2,1,0:T(8,128)(2,1)S(1)}, u32[]{:S(2)}, u32[]{:S(2)}) collective-permute-start(bf16[8,6,16,128]{3,2,1,0:T(8,128)(2,1)S(1)} %shard_map.59), channel_id=1, source_target_pairs={{64,0},{128,64},{192,128},{256,192},{320,256},{384,320},{448,384},... | collective-permute-start | bytes 589832 | tf_op jit(solution)/shard_map/ppermute | solution.py:620
  10.9 6.6 %collective-permute-start.2 = (bf16[8,6,16,128]{3,2,1,0:T(8,128)(2,1)S(1)}, bf16[8,6,16,128]{3,2,1,0:T(8,128)(2,1)S(1)}, u32[]{:S(2)}, u32[]{:S(2)}) collective-permute-start(bf16[8,6,16,128]{3,2,1,0:T(8,128)(2,1)S(1)} %shard_map.59), channel_id=1, source_target_pairs={{0,64},{64,128},{128,192},{192,256},{256,320},{320,384},{384,448},... | collective-permute-start | bytes 589832 | tf_op jit(solution)/shard_map/ppermute | solution.py:620
  17.6 13.2 %collective-permute-start.5 = (bf16[24,6,16,128]{3,2,1,0:T(8,128)(2,1)S(1)}, bf16[24,6,16,128]{3,2,1,0:T(8,128)(2,1)S(1)}, u32[]{:S(2)}, u32[]{:S(2)}) collective-permute-start(bf16[24,6,16,128]{3,2,1,0:T(8,128)(2,1)S(1)} %pad_maximum_fusion.x_ref), channel_id=1, source_target_pairs={{8,0},{16,8},{24,16},{32,24},{40,32},{48,40},{56,48},{9,1},{17,9},... | collective-permute-start | bytes 1769480 | tf_op jit(solution)/shard_map/ppermute | solution.py:620
  27.2 8.7 %collective-permute-start.4 = (bf16[24,6,16,128]{3,2,1,0:T(8,128)(2,1)S(1)}, bf16[24,6,16,128]{3,2,1,0:T(8,128)(2,1)S(1)}, u32[]{:S(2)}, u32[]{:S(2)}) collective-permute-start(bf16[24,6,16,128]{3,2,1,0:T(8,128)(2,1)S(1)} %pad_maximum_fusion.x_ref), channel_id=1, source_target_pairs={{0,8},{8,16},{16,24},{24,32},{32,40},{40,48},{48,56},{1,9},{9,17},... | collective-permute-start | bytes 1769480 | tf_op jit(solution)/shard_map/ppermute | solution.py:620
  63.6 13.1 %collective-permute-start.8 = (f32[32,8,128]{2,1,0:T(8,128)S(1)}, f32[32,8,128]{2,1,0:T(8,128)S(1)}, u32[]{:S(2)}, u32[]{:S(2)}) collective-permute-start(f32[32,8,128]{2,1,0:T(8,128)S(1)} %bitcast.10), channel_id=1, source_target_pairs={{0,1},{1,2},{2,3},{3,4},{4,5},{5,6},{6,7},{8,9},{9,10},{10,11},{11... | collective-permute-start | bytes 393224 | tf_op jit(solution)/shard_map/ppermute | solution.py:620
  67.7 9.1 %collective-permute-start.9 = (f32[32,8,128]{2,1,0:T(8,128)S(1)}, f32[32,8,128]{2,1,0:T(8,128)S(1)}, u32[]{:S(2)}, u32[]{:S(2)}) collective-permute-start(f32[32,8,128]{2,1,0:T(8,128)S(1)} %bitcast.8), channel_id=1, source_target_pairs={{1,0},{2,1},{3,2},{4,3},{5,4},{6,5},{7,6},{9,8},{10,9},{11,10},{12... | collective-permute-start | bytes 393224 | tf_op jit(solution)/shard_map/ppermute | solution.py:620
  69.0 4.1 %collective-permute-start.6 = (f32[6,24,128]{2,1,0:T(8,128)S(1)}, f32[6,24,128]{2,1,0:T(8,128)S(1)}, u32[]{:S(2)}, u32[]{:S(2)}) collective-permute-start(f32[6,24,128]{2,1,0:T(8,128)S(1)} %get-tuple-element.47), channel_id=1, source_target_pairs={{0,64},{64,128},{128,192},{192,256},{256,320},{320,384},{384,448},... | collective-permute-start | bytes 221192 | tf_op jit(solution)/shard_map/ppermute | solution.py:620
  71.6 5.1 %collective-permute-start.7 = (f32[6,24,128]{2,1,0:T(8,128)S(1)}, f32[6,24,128]{2,1,0:T(8,128)S(1)}, u32[]{:S(2)}, u32[]{:S(2)}) collective-permute-start(f32[6,24,128]{2,1,0:T(8,128)S(1)} %get-tuple-element.48), channel_id=1, source_target_pairs={{64,0},{128,64},{192,128},{256,192},{320,256},{384,320},{448,384},... | collective-permute-start | bytes 221192 | tf_op jit(solution)/shard_map/ppermute | solution.py:620
  102.7 6.6 %collective-permute-start.11 = (f32[8,8,128]{2,1,0:T(8,128)S(1)}, f32[8,8,128]{2,1,0:T(8,128)S(1)}, u32[]{:S(2)}, u32[]{:S(2)}) collective-permute-start(f32[8,8,128]{2,1,0:T(8,128)S(1)} %bitcast.13), channel_id=1, source_target_pairs={{1,0},{2,1},{3,2},{4,3},{5,4},{6,5},{7,6},{9,8},{10,9},{11,10},{12... | collective-permute-start | bytes 98312 | tf_op jit(solution)/shard_map/ppermute | solution.py:620
  104.0 6.3 %collective-permute-start.10 = (f32[8,8,128]{2,1,0:T(8,128)S(1)}, f32[8,8,128]{2,1,0:T(8,128)S(1)}, u32[]{:S(2)}, u32[]{:S(2)}) collective-permute-start(f32[8,8,128]{2,1,0:T(8,128)S(1)} %bitcast.15), channel_id=1, source_target_pairs={{0,1},{1,2},{2,3},{3,4},{4,5},{5,6},{6,7},{8,9},{9,10},{10,11},{11... | collective-permute-start | bytes 98312 | tf_op jit(solution)/shard_map/ppermute | solution.py:620
  110.3 21.9 %copy-start = (f32[8,16,128]{2,1,0:T(8,128)S(1)}, f32[8,16,128]{2,1,0:T(8,128)}, u32[]{:S(2)}) copy-start(f32[8,16,128]{2,1,0:T(8,128)} %s_ref.1) | copy-start | bytes 196612

commit v4 on v3

--- a/solution.py
+++ b/solution.py
@@ -77,16 +77,17 @@
 
 def row_pairs(t_ref, values, both):
     out = []
+    pairs = values.shape[0] // 2
     for half in range(2):
         t_ref[half] = values[:, 128 * half : 128 * half + 128]
-        first = t_ref[half, pl.ds(0, 20, 2), :]
-        out.append(first + t_ref[half, pl.ds(1, 20, 2), :] if both else first)
+        first = t_ref[half, pl.ds(0, pairs, 2), :]
+        out.append(first + t_ref[half, pl.ds(1, pairs, 2), :] if both else first)
     return out
 
 
 def put_rows(r_ref, q, halves):
     for half in range(2):
-        r_ref[q, pl.ds(0, 20), pl.ds(128 * half, 128)] = halves[half]
+        r_ref[q, pl.ds(0, halves[half].shape[0]), pl.ds(128 * half, 128)] = halves[half]
 
 
 def prepare_kernel(s_hbm, fc_hbm, solid_hbm, out_ref, ends_ref, s_ref, fc_ref, solid_ref, sems):
@@ -130,26 +131,32 @@
     out_ref[:, 5] = rim.astype(BF16)
 
 
-def first_kernel(
-    x_ref, ym_ref, yp_ref,
-    s_ref, f0_ref, f1_ref, f2_ref, w_ref, d_ref,
-    s1_ref, f10_ref, f11_ref, f12_ref, w1_ref, up_ref, down_ref, pay_ref,
-    c0_ref, c1_ref, c2_ref, sm_ref, t_ref, r0_ref, r1_ref, r2_ref, rs_ref,
-    l10_ref, l11_ref, l12_ref, sm1_ref, t1_ref, u_ref,
-):
+def fine_kernel(thin, x_ref, ym_ref, yp_ref, *refs):
+    if thin:
+        (up_ref, down_ref, pay_ref,
+         s_ref, f0_ref, f1_ref, f2_ref, s1_ref, f10_ref, f11_ref, f12_ref, w1_ref, *refs) = refs
+    else:
+        s_ref, f0_ref, f1_ref, f2_ref, w_ref, d_ref, s1_ref, f10_ref, f11_ref, f12_ref, w1_ref, *refs = refs
+    (c0_ref, c1_ref, c2_ref, sm_ref, t_ref, r0_ref, r1_ref, r2_ref, rs_ref,
+     l10_ref, l11_ref, l12_ref, *refs) = refs
+    planes = range(4, 20) if thin else range(24)
+    rows, rows_1 = s_ref.shape[1], s1_ref.shape[1]
+    own = 4 if thin else 12
+    shape, shape_1 = (rows, 256), (rows_1, 128)
     at_x = lax.axis_index("gx") == 0
     at_y = lax.axis_index("gy") == 0
     at_z = lax.axis_index("gz") == 0
-    lane = iota((40, 128), 1)
+    lane = iota((rows, 128), 1)
     side = (lane < 12) | (lane >= 116)
 
     def unpack(p, carry):
         tiles = []
         for f in range(6):
-            column = jnp.concatenate(
-                [ym_ref[p, f].astype(F32), x_ref[p, f].astype(F32), yp_ref[p, f].astype(F32)], 0
-            )
-            tiles.append(turn(column, -4, 0)[:40])
+            before, after = ym_ref[p, f].astype(F32), yp_ref[p, f].astype(F32)
+            if thin:
+                before, after = before[8:], after[:8]
+            column = jnp.concatenate([before, x_ref[p, f].astype(F32), after], 0)
+            tiles.append(turn(column, -4, 0)[:rows])
         rims = [
             jnp.where(side, turn(tiles[5], -(24 * f + 12), 1), 0.0) for f in range(5)
         ]
@@ -160,10 +167,10 @@
             c_ref[p, :, 128:256] = rims[2 + a]
         return carry
 
-    lax.fori_loop(0, 24, unpack, 0, unroll=4)
+    lax.fori_loop(planes.start, planes.stop, unpack, 0, unroll=4)
 
     def faces(p, carry):
-        before = jnp.maximum(p - 1, 0)
+        before = jnp.maximum(p - 1, planes.start)
         f0_ref[p] = root(c0_ref[p] * c0_ref[before])
         c1 = c1_ref[p]
         f1_ref[p] = root(c1 * turn(c1, 1, 0))
@@ -171,11 +178,11 @@
         f2_ref[p] = root(c2 * turn(c2, 1, 1))
         return carry
 
-    lax.fori_loop(0, 24, faces, 0, unroll=4)
-    f0_ref[24] = jnp.zeros((40, 256), F32)
-
-    first_row = (iota((40, 256), 0) == 12) & at_y
-    first_lane = (iota((40, 256), 1) == 0) & at_z
+    lax.fori_loop(planes.start, planes.stop, faces, 0, unroll=4)
+    f0_ref[planes.stop] = jnp.zeros(shape, F32)
+
+    first_row = (iota(shape, 0) == own) & at_y
+    first_lane = (iota(shape, 1) == 0) & at_z
     for ref in (r0_ref, r1_ref, r2_ref, rs_ref):
         ref[...] = jnp.zeros_like(ref)
 
@@ -189,8 +196,9 @@
             low2 = f2 + jnp.where(first_lane, c2_ref[p], 0.0)
             d = ABSORB + low0 + f0_ref[p + 1] + low1 + turn(f1, -1, 0) + low2 + turn(f2, -1, 1)
             w = RELAX / d
-            d_ref[p] = d
-            w_ref[p] = w
+            if not thin:
+                d_ref[p] = d
+                w_ref[p] = w
             sm_ref[p] = w * s_ref[p]
             lows.append((low0, low1, low2))
         put_rows(r0_ref, q, row_pairs(t_ref, lows[0][0], True))
@@ -198,30 +206,32 @@
         put_rows(r2_ref, q, row_pairs(t_ref, lows[0][2] + lows[1][2], True))
         return carry
 
-    lax.fori_loop(0, 12, diagonals, 0, unroll=2)
+    lax.fori_loop(planes.start // 2, planes.stop // 2, diagonals, 0, unroll=2)
 
     def leftovers(q, carry):
-        total = jnp.zeros((40, 256), F32)
+        total = jnp.zeros(shape, F32)
         for i in range(2):
             p = 2 * q + i
             total += KEEP * s_ref[p] + neighbours(sm_ref, f0_ref, f1_ref, f2_ref, p)
         put_rows(rs_ref, q, row_pairs(t_ref, total, True))
         return carry
 
-    lax.fori_loop(1, 11, leftovers, 0, unroll=2)
+    lax.fori_loop(planes.start // 2 + 1, planes.stop // 2 - 1, leftovers, 0, unroll=2)
 
     pairs = one_hot(256, 128, lambda r, c: lax.shift_right_logical(r, 1) == c, 0.25)
     evens = one_hot(256, 128, lambda r, c: r == 2 * c, 0.25)
+    first, count = planes.start // 2, len(planes) // 2
     for target, source, matrix in (
         (l10_ref, r0_ref, pairs), (l11_ref, r1_ref, pairs), (l12_ref, r2_ref, evens), (s1_ref, rs_ref, pairs)
     ):
-        target[pl.ds(0, 2)] = jnp.zeros((2, 24, 128), F32)
-        target[pl.ds(14, 2)] = jnp.zeros((2, 24, 128), F32)
-        value = spread(source[...].reshape(288, 256), matrix).reshape(12, 24, 128)
-        target[pl.ds(2, 12)] = 2.0 * value if target is s1_ref else value
-
-    first_row_1 = (iota((24, 128), 0) == 6) & at_y
-    first_lane_1 = (iota((24, 128), 1) == 0) & at_z
+        target[...] = jnp.zeros_like(target)
+        value = spread(source[pl.ds(first, count)].reshape(count * rows_1, 256), matrix)
+        value = value.reshape(count, rows_1, 128)
+        target[pl.ds(first + 2, count)] = 2.0 * value if target is s1_ref else value
+
+    first_row_1 = (iota(shape_1, 0) == own // 2) & at_y
+    first_lane_1 = (iota(shape_1, 1) == 0) & at_z
+    planes_1 = range(first + 2, first + 2 + count)
 
     def faces_1(p, carry):
         f10_ref[p] = jnp.where((p == 6) & at_x, 0.0, l10_ref[p])
@@ -229,8 +239,8 @@
         f12_ref[p] = jnp.where(first_lane_1, 0.0, l12_ref[p])
         return carry
 
-    lax.fori_loop(0, 16, faces_1, 0, unroll=4)
-    f10_ref[16] = jnp.zeros((24, 128), F32)
+    lax.fori_loop(planes_1.start, planes_1.stop, faces_1, 0, unroll=4)
+    f10_ref[planes_1.stop] = jnp.zeros(shape_1, F32)
 
     def diagonals_1(p, carry):
         d = (
@@ -238,20 +248,32 @@
             + l11_ref[p] + turn(f11_ref[p], -1, 0)
             + l12_ref[p] + turn(f12_ref[p], -1, 1)
         )
-        w = RELAX / d
-        w1_ref[p] = w
-        sm1_ref[p] = w * s1_ref[p]
-        return carry
-
-    lax.fori_loop(2, 14, diagonals_1, 0, unroll=4)
-    for i, ref in enumerate((s1_ref, w1_ref, f10_ref)):
-        up_ref[pl.ds(2 * i, 2)] = ref[pl.ds(5, 2)]
-        down_ref[pl.ds(2 * i, 2)] = ref[pl.ds(9, 2)]
+        w1_ref[p] = RELAX / d
+        return carry
+
+    lax.fori_loop(planes_1.start, planes_1.stop, diagonals_1, 0, unroll=4)
+    if thin:
+        pack_level_2(
+            up_ref, down_ref, pay_ref, s1_ref, f10_ref, f11_ref, f12_ref, w1_ref, l10_ref, l11_ref, l12_ref, *refs
+        )
+
+
+def pack_level_2(
+    up_ref, down_ref, pay_ref, s1_ref, f10_ref, f11_ref, f12_ref, w1_ref, l10_ref, l11_ref, l12_ref,
+    sm1_ref, t1_ref, u_ref,
+):
+    for target, start in ((up_ref, 5), (down_ref, 9)):
+        target[...] = jnp.zeros_like(target)
+        for i, ref in enumerate((s1_ref, w1_ref, f10_ref)):
+            for k in range(2):
+                target[2 * i + k, pl.ds(4, 12), :] = ref[start + k, pl.ds(0, 12), :]
+    for p in range(5, 11):
+        sm1_ref[p] = w1_ref[p] * s1_ref[p]
 
     def quad(values, both):
         t1_ref[...] = values
-        first = t1_ref[pl.ds(6, 4, 2), :]
-        return first + t1_ref[pl.ds(7, 4, 2), :] if both else first
+        first = t1_ref[pl.ds(2, 4, 2), :]
+        return first + t1_ref[pl.ds(3, 4, 2), :] if both else first
 
     def leftover_1(p):
         return KEEP * s1_ref[p] + neighbours(sm1_ref, f10_ref, f11_ref, f12_ref, p)
@@ -283,10 +305,12 @@
 
 
 def window(pieces, to, lane):
-    out = jnp.zeros(pieces[0].shape, F32)
-    for k, piece in enumerate(pieces):
-        out = jnp.where((lane >= 16 * k) & (lane < 16 * k + 16), turn(piece, 16 * k - to, 1), out)
-    return out
+    out = pieces[3]
+    for k in range(3):
+        start = (to + 16 * k) % 128
+        here = (lane >= start) & (lane < start + 16)
+        out = jnp.where(here, pieces[k], out)
+    return jnp.where(lane < 64, turn(out, -to, 1), 0.0)
 
 
 def solve_2(s2, level_2, level_3, t3_ref, e_ref):
@@ -380,13 +404,13 @@
     def assemble(x, carry):
         for pair in range(ny2 // 8):
             g = x * (ny2 // 8) + pair
-            pieces = [ref[g] for ref in (before_ref, own0_ref, own1_ref, after_ref)]
+            pieces = [turn(ref[g], 16 * k, 1) for k, ref in enumerate((before_ref, own0_ref, own1_ref, after_ref))]
             for f in range(4):
                 for i in range(2):
                     v_ref[f, 2 * x + i, pl.ds(8 * pair, 8), :] = window(pieces, 32 * f + 16 * i, lane8)
         return carry
 
-    lax.fori_loop(0, nx2 // 2, assemble, 0)
+    lax.fori_loop(0, nx2 // 2, assemble, 0, unroll=2)
 
     s2 = v_ref[0]
     low = (v_ref[1], v_ref[2], v_ref[3])
@@ -531,7 +555,7 @@
     lane = iota((ny2 // 4, 128), 1)
 
     def assemble(x, carry):
-        pieces = [ref[x] for ref in (before_ref, own0_ref, own1_ref, after_ref)]
+        pieces = [turn(ref[x], 16 * k, 1) for k, ref in enumerate((before_ref, own0_ref, own1_ref, after_ref))]
         for i in range(2):
             for j in range(4):
                 v_ref[2 * x + i, pl.ds(j, ny2 // 4, 4), :] = window(pieces, 32 * j + 16 * i, lane)
@@ -549,6 +573,7 @@
     m2_ref[...] = jnp.zeros_like(m2_ref)
     m2_ref[pl.ds(3, nx2)] = m2
     fetch_level_2(m2_ref, range(2, 6), pick_ref)
+
     for p in range(4, 12):
         corr1_ref[p] = w1_ref[p] * t1s_ref[p] + pick_ref[p // 2]
     for p in range(5, 11):
@@ -649,16 +674,28 @@
     fine, fine_up = (24, 40, 256), (25, 40, 256)
     mid, mid_up = (16, 24, 128), (17, 24, 128)
     rows, wide, edge = (12, 24, 256), (16, 24, 256), (6, 24, 128)
-    *state, up, down, pay = call(
-        first_kernel,
+    slim, slim_up, slim_mid, slim_mid_up, slim_rows = (
+        (20, 24, 256), (21, 24, 256), (16, 16, 128), (17, 16, 128), (12, 16, 256)
+    )
+    up, down, pay = call(
+        functools.partial(fine_kernel, True),
         [block, before, after],
-        [(shape, F32) for shape in (fine, fine_up, fine, fine, fine, fine, mid, mid_up, mid, mid, mid, edge, edge, (8, 128))],
-        [fine, fine, fine, fine, (2, 40, 128), rows, rows, rows, rows, mid, mid, mid, mid, (24, 128), (4, 8, 128)],
+        [(edge, F32), (edge, F32), ((8, 128), F32)],
+        [slim, slim_up, slim, slim, slim_mid, slim_mid_up, slim_mid, slim_mid, slim_mid,
+         slim, slim, slim, slim, (2, 24, 128), slim_rows, slim_rows, slim_rows, slim_rows,
+         slim_mid, slim_mid, slim_mid, slim_mid, (16, 128), (4, 8, 128)],
+    )
+    state = call(
+        functools.partial(fine_kernel, False),
+        [block, before, after],
+        [(shape, F32) for shape in (fine, fine_up, fine, fine, fine, fine, mid, mid_up, mid, mid, mid)],
+        [fine, fine, fine, fine, (2, 40, 128), rows, rows, rows, rows, mid, mid, mid],
         keep_out=range(11),
     )
     low, high = shift_along(up, "gx", 1), shift_along(down, "gx", -1)
     own = gather_plane(pay)
     pairs = (nx2 * ny2 // 16, 8, 128)
+    own, low, high = lax.optimization_barrier((own, low, high))
     own0, own1 = own[..., :512].reshape(pairs), own[..., 512:].reshape(pairs)
     before, after = shift_along(own1, "gz", 1), shift_along(own0, "gz", -1)
     level_2, level_3 = (nx2, ny2, 128), (nx2 // 2, ny2 // 2, 128)

time: 134 us -> 131 us (0.978)
  blocking collectives: 59.9 us -> 36.7 us
  starting transfers between devices: 39.3 us -> 50.2 us
  waiting for transfers between devices: 15.2 us -> 21.4 us
  Pallas kernels: 17.3 us -> 19 us
    all_to_all x2 -> x1, blocking collectives: 40.7 us -> 18.1 us  [gather_plane(): return lax.all_to_all(copies, ('gx', 'gy'), 0, 0, tiled=True)]
    all_to_all x0 -> x1, starting transfers between devices: none -> 9.7 us  [gather_plane(): return lax.all_to_all(copies, ('gx', 'gy'), 0, 0, tiled=True)]
    all_to_all x0 -> x1, waiting for transfers between devices: none -> 4.28 us  [gather_plane(): return lax.all_to_all(copies, ('gx', 'gy'), 0, 0, tiled=True)]
    ppermute x12, waiting for transfers between devices: 15.2 us -> 17.2 us  [shift_along(): lax.ppermute(value, axis, [(i, i + by) for i in range(size) if 0 <= i + b...]
    pallas_call x6 -> x7, Pallas kernels: 17.3 us -> 19 us  [call(): pl.pallas_call(kernel, out_shape=shapes, in_specs=[pl.BlockSpec(memory_sp...]
  transfers between devices with their start and end apart: 12 -> 13, of which waited for: 8 -> 10; matrix products, arithmetic and copies ran while one was open for 0% -> 0% of each run, Pallas kernels for 0% -> 4%
where the time goes in v4:
time: 131 us; the launch traced here: 129 us
  starting transfers between devices  50.2 us (38%)
  blocking collectives  36.7 us (28%)
  waiting for transfers between devices  21.4 us (16%)
  Pallas kernels  19 us (15%)
    ppermute x12, starting transfers between devices, shift_along(): lax.ppermute(value, axis, [(i, i + by) for i in range(size) if 0 <= i + b...  40.6 us
    pallas_call x7, Pallas kernels, call(): pl.pallas_call(kernel, out_shape=shapes, in_specs=[pl.BlockSpec(memory_sp...  19 us
    all_to_all x1, blocking collectives, local(): lax.all_to_all(jnp.broadcast_to(sums[None], (peers, 1, 128)), 'gz', 0, 0,...  18.6 us
    all_to_all x1, blocking collectives, gather_plane(): return lax.all_to_all(copies, ('gx', 'gy'), 0, 0, tiled=True)  18.1 us
    ppermute x12, waiting for transfers between devices, shift_along(): lax.ppermute(value, axis, [(i, i + by) for i in range(size) if 0 <= i + b...  17.2 us
    all_to_all x1, starting transfers between devices, gather_plane(): return lax.all_to_all(copies, ('gx', 'gy'), 0, 0, tiled=True)  9.7 us
    all_to_all x1, waiting for transfers between devices, gather_plane(): return lax.all_to_all(copies, ('gx', 'gy'), 0, 0, tiled=True)  4.28 us
  transfers between devices with their start and end apart: 13, of which 10 were waited for; matrix products, arithmetic and copies ran while one was open for 0% of the time, Pallas kernels for 4%

profile of v4, /device:TPU:1, one launch (start us, length us, event | category | flops | bytes accessed | tf_op | source)
XLA Modules:
  0.0 129.2 jit_solution(3954846634933978186)
XLA Ops:
  0.6 1.2 shard_map.58
  1.8 1.3 collective-permute-start.1
  3.1 5.5 %collective-permute-start = (bf16[8,16,128]{2,1,0:T(8,128)(2,1)S(1)}, bf16[8,16,128]{2,1,0:T(8,128)(2,1)S(1)}, u32[]{:S(2)}, u32[]{:S(2)}) collective-permute-start(bf16[8,16,128]{2,1,0:T(8,128)(2,1)S(1)} %get-tuple-element.38), channel_id=1, source_target_pairs={{0,1},{1,2},{2,3},{3,4},{4,5},{5,6},{6,7},{8,9},{9,10},{10,11},{11... | collective-permute-start | bytes 98312 | tf_op jit(solution)/shard_map/ppermute | solution.py:645
  8.6 1.0 collective-permute-done.before_ref
  9.6 1.3 collective-permute-start.3
  10.9 4.0 %collective-permute-start.2 = (bf16[8,6,16,128]{3,2,1,0:T(8,128)(2,1)S(1)}, bf16[8,6,16,128]{3,2,1,0:T(8,128)(2,1)S(1)}, u32[]{:S(2)}, u32[]{:S(2)}) collective-permute-start(bf16[8,6,16,128]{3,2,1,0:T(8,128)(2,1)S(1)} %shard_map.59), channel_id=1, source_target_pairs={{0,64},{64,128},{128,192},{192,256},{256,320},{320,384},{384,448},... | collective-permute-start | bytes 589832 | tf_op jit(solution)/shard_map/ppermute | solution.py:645
  14.9 1.1 collective-permute-done.3
  16.0 1.5 %collective-permute-done.2 = bf16[8,6,16,128]{3,2,1,0:T(8,128)(2,1)S(1)} collective-permute-done((bf16[8,6,16,128]{3,2,1,0:T(8,128)(2,1)S(1)}, bf16[8,6,16,128]{3,2,1,0:T(8,128)(2,1)S(1)}, u32[]{:S(2)}, u32[]{:S(2)}) %collective-permute-start.2) | collective-permute-done | bytes 196640 | tf_op jit(solution)/shard_map/ppermute | solution.py:645
  17.6 9.6 %collective-permute-start.5 = (bf16[24,6,16,128]{3,2,1,0:T(8,128)(2,1)S(1)}, bf16[24,6,16,128]{3,2,1,0:T(8,128)(2,1)S(1)}, u32[]{:S(2)}, u32[]{:S(2)}) collective-permute-start(bf16[24,6,16,128]{3,2,1,0:T(8,128)(2,1)S(1)} %pad_maximum_fusion.x_ref), channel_id=1, source_target_pairs={{8,0},{16,8},{24,16},{32,24},{40,32},{48,40},{56,48},{9,1},{17,9},... | collective-permute-start | bytes 1769480 | tf_op jit(solution)/shard_map/ppermute | solution.py:645
  27.2 1.9 %collective-permute-start.4 = (bf16[24,6,16,128]{3,2,1,0:T(8,128)(2,1)S(1)}, bf16[24,6,16,128]{3,2,1,0:T(8,128)(2,1)S(1)}, u32[]{:S(2)}, u32[]{:S(2)}) collective-permute-start(bf16[24,6,16,128]{3,2,1,0:T(8,128)(2,1)S(1)} %pad_maximum_fusion.x_ref), channel_id=1, source_target_pairs={{0,8},{8,16},{16,24},{24,32},{32,40},{40,48},{48,56},{1,9},{9,17},... | collective-permute-start | bytes 1769480 | tf_op jit(solution)/shard_map/ppermute | solution.py:645
  29.1 1.7 %collective-permute-done.5.yp_ref = bf16[24,6,16,128]{3,2,1,0:T(8,128)(2,1)S(1)} collective-permute-done((bf16[24,6,16,128]{3,2,1,0:T(8,128)(2,1)S(1)}, bf16[24,6,16,128]{3,2,1,0:T(8,128)(2,1)S(1)}, u32[]{:S(2)}, u32[]{:S(2)}) %collective-permute-start.5) | collective-permute-done | bytes 589856 | tf_op jit(solution)/shard_map/ppermute | solution.py:645
  30.8 5.1 %collective-permute-done.4.ym_ref = bf16[24,6,16,128]{3,2,1,0:T(8,128)(2,1)S(1)} collective-permute-done((bf16[24,6,16,128]{3,2,1,0:T(8,128)(2,1)S(1)}, bf16[24,6,16,128]{3,2,1,0:T(8,128)(2,1)S(1)}, u32[]{:S(2)}, u32[]{:S(2)}) %collective-permute-start.4) | collective-permute-done | bytes 589856 | tf_op jit(solution)/shard_map/ppermute | solution.py:645
  35.9 2.6 %shard_map.61 = (f32[6,24,128]{2,1,0:T(8,128)S(1)}, f32[6,24,128]{2,1,0:T(8,128)S(1)}, f32[8,128]{1,0:T(8,128)S(1)}) custom-call(bf16[24,6,16,128]{3,2,1,0:T(8,128)(2,1)S(1)} %pad_maximum_fusion.x_ref, bf16[24,6,16,128]{3,2,1,0:T(8,128)(2,1)S(1)} %collective-permute-done.4.ym_ref, bf16[24,6,16,128]{3,2,1,0:T(8,128)(2,1)S(1)} %collective-permute-done.5.yp_ref), custom_call_target="tpu_custom_call" | custom-call | tf_op jit(solution)/shard_map/pallas_call | solution.py:633
  38.5 0.8 broadcast_in_dim.23
  39.3 9.7 %all-to-all-start = ((f32[64,1,1024]{2,1,0:T(1,128)}), f32[64,1,1024]{2,1,0:T(1,128)S(1)}, u32[]{:S(2)}, u32[]{:S(2)}) async-start(f32[64,1,1024]{2,1,0:T(1,128)} %broadcast_in_dim.23), calls=%async_computation | async-start | bytes 524288 | tf_op jit(solution)/shard_map/all_to_all | solution.py:651
  49.0 3.3 %collective-permute-start.6 = (f32[6,24,128]{2,1,0:T(8,128)S(1)}, f32[6,24,128]{2,1,0:T(8,128)S(1)}, u32[]{:S(2)}, u32[]{:S(2)}) collective-permute-start(f32[6,24,128]{2,1,0:T(8,128)S(1)} %get-tuple-element.51), channel_id=1, source_target_pairs={{0,64},{64,128},{128,192},{192,256},{256,320},{320,384},{384,448},... | collective-permute-start | bytes 221192 | tf_op jit(solution)/shard_map/ppermute | solution.py:645
  52.3 1.3 collective-permute-start.7
  53.6 1.6 %collective-permute-done.6.low_ref = f32[6,24,128]{2,1,0:T(8,128)S(1)} collective-permute-done((f32[6,24,128]{2,1,0:T(8,128)S(1)}, f32[6,24,128]{2,1,0:T(8,128)S(1)}, u32[]{:S(2)}, u32[]{:S(2)}) %collective-permute-start.6) | collective-permute-done | bytes 73760 | tf_op jit(solution)/shard_map/ppermute | solution.py:645
  55.2 2.6 %collective-permute-done.7.high_ref = f32[6,24,128]{2,1,0:T(8,128)S(1)} collective-permute-done((f32[6,24,128]{2,1,0:T(8,128)S(1)}, f32[6,24,128]{2,1,0:T(8,128)S(1)}, u32[]{:S(2)}, u32[]{:S(2)}) %collective-permute-start.7) | collective-permute-done | bytes 73760 | tf_op jit(solution)/shard_map/ppermute | solution.py:645
  57.9 4.3 %all-to-all-done = f32[64,1,1024]{2,1,0:T(1,128)S(1)} async-done(((f32[64,1,1024]{2,1,0:T(1,128)}), f32[64,1,1024]{2,1,0:T(1,128)S(1)}, u32[]{:S(2)}, u32[]{:S(2)}) %all-to-all-start) | async-done | bytes 262176 | tf_op jit(solution)/shard_map/all_to_all | solution.py:651
  62.2 4.0 %collective-permute-start.8 = (f32[32,8,128]{2,1,0:T(8,128)S(1)}, f32[32,8,128]{2,1,0:T(8,128)S(1)}, u32[]{:S(2)}, u32[]{:S(2)}) collective-permute-start(f32[32,8,128]{2,1,0:T(8,128)S(1)} %bitcast.10), channel_id=1, source_target_pairs={{0,1},{1,2},{2,3},{3,4},{4,5},{5,6},{6,7},{8,9},{9,10},{10,11},{11... | collective-permute-start | bytes 393224 | tf_op jit(solution)/shard_map/ppermute | solution.py:645
  66.2 1.3 collective-permute-start.9
  67.5 4.6 %shard_map.60 = (f32[24,40,256]{2,1,0:T(8,128)S(1)}, f32[25,40,256]{2,1,0:T(8,128)S(1)}, f32[24,40,256]{2,1,0:T(8,128)S(1)}, f32[24,40,256]{2,1,0:T(8,128)S(1)},...) custom-call(bf16[24,6,16,128]{3,2,1,0:T(8,128)(2,1)S(1)} %pad_maximu, ...), custom_call_target="tpu_custom_call" | custom-call | tf_op jit(solution)/shard_map/pallas_call | solution.py:633
  72.1 1.5 %collective-permute-done.9.after_ref = f32[32,8,128]{2,1,0:T(8,128)S(1)} collective-permute-done((f32[32,8,128]{2,1,0:T(8,128)S(1)}, f32[32,8,128]{2,1,0:T(8,128)S(1)}, u32[]{:S(2)}, u32[]{:S(2)}) %collective-permute-start.9) | collective-permute-done | bytes 131104 | tf_op jit(solution)/shard_map/ppermute | solution.py:645
  73.6 7.1 %shard_map.62 = (f32[8,16,128]{2,1,0:T(8,128)S(1)}, f32[8,16,128]{2,1,0:T(8,128)S(1)}, f32[24,40,256]{2,1,0:T(8,128)S(1)}, f32[16,24,128]{2,1,0:T(8,128)S(1)}, f...) custom-call(f32[24,40,256]{2,1,0:T(8,128)S(1)} %get-tuple-element.47, ...), custom_call_target="tpu_custom_call" | custom-call | tf_op jit(solution)/shard_map/pallas_call | solution.py:633
  80.7 18.1 %all_to_all.15 = f32[64,1,512]{2,1,0:T(1,128)S(1)} all-to-all(f32[64,1,512]{2,1,0:T(1,128)S(1)} %broadcast_in_dim.25), channel_id=1, replica_groups=mesh['gx'=8,'gy'=8,'gz'=8] {'gx','gy'}, dimensions={0} | all-to-all | bytes 262144 | tf_op jit(solution)/shard_map/all_to_all | solution.py:651
  98.9 1.3 collective-permute-start.11
  100.2 5.8 %collective-permute-start.10 = (f32[8,8,128]{2,1,0:T(8,128)S(1)}, f32[8,8,128]{2,1,0:T(8,128)S(1)}, u32[]{:S(2)}, u32[]{:S(2)}) collective-permute-start(f32[8,8,128]{2,1,0:T(8,128)S(1)} %bitcast.15), channel_id=1, source_target_pairs={{0,1},{1,2},{2,3},{3,4},{4,5},{5,6},{6,7},{8,9},{9,10},{10,11},{11... | collective-permute-start | bytes 98312 | tf_op jit(solution)/shard_map/ppermute | solution.py:645
  106.1 1.0 collective-permute-done.10.before_ref
  107.1 2.8 %shard_map.63 = (f32[8,16,128]{2,1,0:T(8,128)S(1)}, f32[1,128]{1,0:T(1,128)S(1)}) custom-call(f32[25,40,256]{2,1,0:T(8,128)S(1)} %get-tuple-element.39.f0_ref, f32[24,40,256]{2,1,0:T(8,128)S(1)} %get-tuple-element.40.f1_ref, f32[24,40,256]{2,1,0:T(8,128)S(1)} %get-tuple-element.41.f2_ref, f32[24,40,256]{2,1,0:T(8,128)S(1)} %get-tuple-element.42.w_ref, ...), custom_call_target="tpu_custom_call" | custom-call | tf_op jit(solution)/shard_map/pallas_call | solution.py:633
  109.9 18.6 %all_to_all.16.sums_ref = f32[8,1,128]{2,1,0:T(1,128)S(1)} all-to-all(f32[8,1,128]{2,1,0:T(1,128)S(1)} %broadcast_in_dim.27), channel_id=1, replica_groups=mesh['gx'=8,'gy'=8,'gz'=8] {'gz'}, dimensions={0} | all-to-all | bytes 8192 | tf_op jit(solution)/shard_map/all_to_all | solution.py:727
  128.5 0.8 shard_map.64
  (11 shorter events, 0.3 us)
Async XLA Ops:
  1.8 6.8 %collective-permute-start.1 = (bf16[8,16,128]{2,1,0:T(8,128)(2,1)S(1)}, bf16[8,16,128]{2,1,0:T(8,128)(2,1)S(1)}, u32[]{:S(2)}, u32[]{:S(2)}) collective-permute-start(bf16[8,16,128]{2,1,0:T(8,128)(2,1)S(1)} %get-tuple-element.38), channel_id=1, source_target_pairs={{1,0},{2,1},{3,2},{4,3},{5,4},{6,5},{7,6},{9,8},{10,9},{11,10},{12... | collective-permute-start | bytes 98312 | tf_op jit(solution)/shard_map/ppermute | solution.py:645
  3.1 6.5 %collective-permute-start = (bf16[8,16,128]{2,1,0:T(8,128)(2,1)S(1)}, bf16[8,16,128]{2,1,0:T(8,128)(2,1)S(1)}, u32[]{:S(2)}, u32[]{:S(2)}) collective-permute-start(bf16[8,16,128]{2,1,0:T(8,128)(2,1)S(1)} %get-tuple-element.38), channel_id=1, source_target_pairs={{0,1},{1,2},{2,3},{3,4},{4,5},{5,6},{6,7},{8,9},{9,10},{10,11},{11... | collective-permute-start | bytes 98312 | tf_op jit(solution)/shard_map/ppermute | solution.py:645
  9.6 6.4 %collective-permute-start.3 = (bf16[8,6,16,128]{3,2,1,0:T(8,128)(2,1)S(1)}, bf16[8,6,16,128]{3,2,1,0:T(8,128)(2,1)S(1)}, u32[]{:S(2)}, u32[]{:S(2)}) collective-permute-start(bf16[8,6,16,128]{3,2,1,0:T(8,128)(2,1)S(1)} %shard_map.59), channel_id=1, source_target_pairs={{64,0},{128,64},{192,128},{256,192},{320,256},{384,320},{448,384},... | collective-permute-start | bytes 589832 | tf_op jit(solution)/shard_map/ppermute | solution.py:645
  10.9 6.6 %collective-permute-start.2 = (bf16[8,6,16,128]{3,2,1,0:T(8,128)(2,1)S(1)}, bf16[8,6,16,128]{3,2,1,0:T(8,128)(2,1)S(1)}, u32[]{:S(2)}, u32[]{:S(2)}) collective-permute-start(bf16[8,6,16,128]{3,2,1,0:T(8,128)(2,1)S(1)} %shard_map.59), channel_id=1, source_target_pairs={{0,64},{64,128},{128,192},{192,256},{256,320},{320,384},{384,448},... | collective-permute-start | bytes 589832 | tf_op jit(solution)/shard_map/ppermute | solution.py:645
  17.6 13.2 %collective-permute-start.5 = (bf16[24,6,16,128]{3,2,1,0:T(8,128)(2,1)S(1)}, bf16[24,6,16,128]{3,2,1,0:T(8,128)(2,1)S(1)}, u32[]{:S(2)}, u32[]{:S(2)}) collective-permute-start(bf16[24,6,16,128]{3,2,1,0:T(8,128)(2,1)S(1)} %pad_maximum_fusion.x_ref), channel_id=1, source_target_pairs={{8,0},{16,8},{24,16},{32,24},{40,32},{48,40},{56,48},{9,1},{17,9},... | collective-permute-start | bytes 1769480 | tf_op jit(solution)/shard_map/ppermute | solution.py:645
  27.2 8.7 %collective-permute-start.4 = (bf16[24,6,16,128]{3,2,1,0:T(8,128)(2,1)S(1)}, bf16[24,6,16,128]{3,2,1,0:T(8,128)(2,1)S(1)}, u32[]{:S(2)}, u32[]{:S(2)}) collective-permute-start(bf16[24,6,16,128]{3,2,1,0:T(8,128)(2,1)S(1)} %pad_maximum_fusion.x_ref), channel_id=1, source_target_pairs={{0,8},{8,16},{16,24},{24,32},{32,40},{40,48},{48,56},{1,9},{9,17},... | collective-permute-start | bytes 1769480 | tf_op jit(solution)/shard_map/ppermute | solution.py:645
  39.3 22.9 %all-to-all-start = ((f32[64,1,1024]{2,1,0:T(1,128)}), f32[64,1,1024]{2,1,0:T(1,128)S(1)}, u32[]{:S(2)}, u32[]{:S(2)}) async-start(f32[64,1,1024]{2,1,0:T(1,128)} %broadcast_in_dim.23), calls=%async_computation | async-start | bytes 524288 | tf_op jit(solution)/shard_map/all_to_all | solution.py:651
  49.0 6.2 %collective-permute-start.6 = (f32[6,24,128]{2,1,0:T(8,128)S(1)}, f32[6,24,128]{2,1,0:T(8,128)S(1)}, u32[]{:S(2)}, u32[]{:S(2)}) collective-permute-start(f32[6,24,128]{2,1,0:T(8,128)S(1)} %get-tuple-element.51), channel_id=1, source_target_pairs={{0,64},{64,128},{128,192},{192,256},{256,320},{320,384},{384,448},... | collective-permute-start | bytes 221192 | tf_op jit(solution)/shard_map/ppermute | solution.py:645
  52.3 5.6 %collective-permute-start.7 = (f32[6,24,128]{2,1,0:T(8,128)S(1)}, f32[6,24,128]{2,1,0:T(8,128)S(1)}, u32[]{:S(2)}, u32[]{:S(2)}) collective-permute-start(f32[6,24,128]{2,1,0:T(8,128)S(1)} %get-tuple-element.52), channel_id=1, source_target_pairs={{64,0},{128,64},{192,128},{256,192},{320,256},{384,320},{448,384},... | collective-permute-start | bytes 221192 | tf_op jit(solution)/shard_map/ppermute | solution.py:645
  62.2 9.9 %collective-permute-start.8 = (f32[32,8,128]{2,1,0:T(8,128)S(1)}, f32[32,8,128]{2,1,0:T(8,128)S(1)}, u32[]{:S(2)}, u32[]{:S(2)}) collective-permute-start(f32[32,8,128]{2,1,0:T(8,128)S(1)} %bitcast.10), channel_id=1, source_target_pairs={{0,1},{1,2},{2,3},{3,4},{4,5},{5,6},{6,7},{8,9},{9,10},{10,11},{11... | collective-permute-start | bytes 393224 | tf_op jit(solution)/shard_map/ppermute | solution.py:645
  66.2 7.4 %collective-permute-start.9 = (f32[32,8,128]{2,1,0:T(8,128)S(1)}, f32[32,8,128]{2,1,0:T(8,128)S(1)}, u32[]{:S(2)}, u32[]{:S(2)}) collective-permute-start(f32[32,8,128]{2,1,0:T(8,128)S(1)} %bitcast.8), channel_id=1, source_target_pairs={{1,0},{2,1},{3,2},{4,3},{5,4},{6,5},{7,6},{9,8},{10,9},{11,10},{12... | collective-permute-start | bytes 393224 | tf_op jit(solution)/shard_map/ppermute | solution.py:645
  98.9 7.1 %collective-permute-start.11 = (f32[8,8,128]{2,1,0:T(8,128)S(1)}, f32[8,8,128]{2,1,0:T(8,128)S(1)}, u32[]{:S(2)}, u32[]{:S(2)}) collective-permute-start(f32[8,8,128]{2,1,0:T(8,128)S(1)} %bitcast.13), channel_id=1, source_target_pairs={{1,0},{2,1},{3,2},{4,3},{5,4},{6,5},{7,6},{9,8},{10,9},{11,10},{12... | collective-permute-start | bytes 98312 | tf_op jit(solution)/shard_map/ppermute | solution.py:645
  100.2 6.9 %collective-permute-start.10 = (f32[8,8,128]{2,1,0:T(8,128)S(1)}, f32[8,8,128]{2,1,0:T(8,128)S(1)}, u32[]{:S(2)}, u32[]{:S(2)}) collective-permute-start(f32[8,8,128]{2,1,0:T(8,128)S(1)} %bitcast.15), channel_id=1, source_target_pairs={{0,1},{1,2},{2,3},{3,4},{4,5},{5,6},{6,7},{8,9},{9,10},{10,11},{11... | collective-permute-start | bytes 98312 | tf_op jit(solution)/shard_map/ppermute | solution.py:645
  107.1 21.4 %copy-start = (f32[8,16,128]{2,1,0:T(8,128)S(1)}, f32[8,16,128]{2,1,0:T(8,128)}, u32[]{:S(2)}) copy-start(f32[8,16,128]{2,1,0:T(8,128)} %s_ref.1) | copy-start | bytes 196612

commit v5 on v4

--- a/solution.py
+++ b/solution.py
@@ -129,6 +129,57 @@
     out_ref[:, 0:5] = own_ref[...]
     rim = jnp.where(last, before_ref[...].astype(F32), after_ref[...].astype(F32))
     out_ref[:, 5] = rim.astype(BF16)
+
+
+def edges_kernel(x_ref, up_ref, down_ref):
+    row = iota((8, 128), 0)
+    quarters = [(p, True) for p in range(5, 19)] + [(0, False), (23, False)]
+
+    def body(f, carry):
+        for t in range(11):
+            pair = [x_ref[1 + 2 * t + k, f].astype(F32) for k in range(2)]
+            up_ref[t, f] = jnp.concatenate([v[8:] for v in pair], 0).astype(BF16)
+            down_ref[t, f] = jnp.concatenate([v[:8] for v in pair], 0).astype(BF16)
+        for t in range(4):
+            ups, downs = [], []
+            for k in range(0, 4, 2):
+                pair = []
+                for p, inner in quarters[4 * t + k : 4 * t + k + 2]:
+                    v = x_ref[p, f].astype(F32)
+                    pair.append((v[:8], v[8:]) if inner else (v[8:], v[:8]))
+                ups.append(jnp.where(row < 4, turn(pair[0][0], 4, 0), pair[1][0]))
+                downs.append(jnp.where(row < 4, pair[0][1], turn(pair[1][1], 4, 0)))
+            up_ref[11 + t, f] = jnp.concatenate(ups, 0).astype(BF16)
+            down_ref[11 + t, f] = jnp.concatenate(downs, 0).astype(BF16)
+        return carry
+
+    lax.fori_loop(0, 6, body, 0)
+
+
+def edge_rows(ym_ref, yp_ref, p, f, thin):
+    row = iota((8, 128), 0)
+    zero = jnp.zeros((8, 128), F32)
+
+    def eight(ref, tile, k):
+        return ref[tile, f].astype(F32)[8 * k : 8 * k + 8]
+
+    def four(q, before):
+        v = eight(ym_ref if before else yp_ref, 11 + q // 4, q % 4 // 2)
+        moved = turn(v, 4, 0) if (q % 2 == 0) == before else v
+        return jnp.where((row >= 4) == before, moved, 0.0)
+
+    if p in (0, 23):
+        q = 14 if p == 0 else 15
+        near_before, near_after = four(q, True), four(q, False)
+    else:
+        near_before, near_after = (eight(ref, (p - 1) // 2, (p - 1) % 2) for ref in (ym_ref, yp_ref))
+    if thin:
+        return near_before, near_after
+    if 5 <= p <= 18:
+        far_before, far_after = four(p - 5, True), four(p - 5, False)
+    else:
+        far_before = far_after = zero
+    return jnp.concatenate([far_before, near_before], 0), jnp.concatenate([near_after, far_after], 0)
 
 
 def fine_kernel(thin, x_ref, ym_ref, yp_ref, *refs):
@@ -149,12 +200,10 @@
     lane = iota((rows, 128), 1)
     side = (lane < 12) | (lane >= 116)
 
-    def unpack(p, carry):
+    for p in planes:
         tiles = []
         for f in range(6):
-            before, after = ym_ref[p, f].astype(F32), yp_ref[p, f].astype(F32)
-            if thin:
-                before, after = before[8:], after[:8]
+            before, after = edge_rows(ym_ref, yp_ref, p, f, thin)
             column = jnp.concatenate([before, x_ref[p, f].astype(F32), after], 0)
             tiles.append(turn(column, -4, 0)[:rows])
         rims = [
@@ -165,9 +214,6 @@
         for a, c_ref in enumerate((c0_ref, c1_ref, c2_ref)):
             c_ref[p, :, 0:128] = tiles[2 + a]
             c_ref[p, :, 128:256] = rims[2 + a]
-        return carry
-
-    lax.fori_loop(planes.start, planes.stop, unpack, 0, unroll=4)
 
     def faces(p, carry):
         before = jnp.maximum(p - 1, planes.start)
@@ -301,7 +347,7 @@
                 moved = turn(turn(part, 4 * (h - i), 0), to - 16 * h, 1)
                 here = (lax.shift_right_logical(row8, 2) == h) & (lane8 >= to) & (lane8 < to + 16)
                 total = jnp.where(here, moved, total)
-    pay_ref[...] = total
+    pay_ref[...] = jnp.broadcast_to(total[None], pay_ref.shape)
 
 
 def window(pieces, to, lane):
@@ -541,7 +587,7 @@
         pay = jnp.where(row8 == h, line, pay)
     for k, value in enumerate(scalars):
         pay = jnp.where((lane8 == k) & (row8 == 2), value, pay)
-    pay_ref[...] = pay[:4]
+    pay_ref[...] = jnp.broadcast_to(pay[None, :4], pay_ref.shape)
 
 
 def third_kernel(
@@ -645,9 +691,8 @@
     return lax.ppermute(value, axis, [(i, i + by) for i in range(size) if 0 <= i + by < size])
 
 
-def gather_plane(value):
-    peers = lax.axis_size(("gx", "gy"))
-    copies = jnp.broadcast_to(value.reshape(1, 1, -1), (peers, 1, value.size))
+def gather_plane(copies):
+    copies = copies.reshape(copies.shape[0], 1, -1)
     return lax.all_to_all(copies, ("gx", "gy"), 0, 0, tiled=True)
 
 
@@ -669,7 +714,8 @@
     before, after = shift_along(ends, "gz", 1), shift_along(ends, "gz", -1)
     (own,) = call(rim_kernel, [own, before, after], [((8, 6, 16, 128), BF16)])
     block = jnp.concatenate([shift_along(own, "gx", 1), own, shift_along(own, "gx", -1)], axis=0)
-    before, after = shift_along(block, "gy", 1), shift_along(block, "gy", -1)
+    to_up, to_down = call(edges_kernel, [block], [((15, 6, 16, 128), BF16)] * 2)
+    before, after = shift_along(to_up, "gy", 1), shift_along(to_down, "gy", -1)
 
     fine, fine_up = (24, 40, 256), (25, 40, 256)
     mid, mid_up = (16, 24, 128), (17, 24, 128)
@@ -680,7 +726,7 @@
     up, down, pay = call(
         functools.partial(fine_kernel, True),
         [block, before, after],
-        [(edge, F32), (edge, F32), ((8, 128), F32)],
+        [(edge, F32), (edge, F32), ((lax.axis_size(("gx", "gy")), 8, 128), F32)],
         [slim, slim_up, slim, slim, slim_mid, slim_mid_up, slim_mid, slim_mid, slim_mid,
          slim, slim, slim, slim, (2, 24, 128), slim_rows, slim_rows, slim_rows, slim_rows,
          slim_mid, slim_mid, slim_mid, slim_mid, (16, 128), (4, 8, 128)],
@@ -705,7 +751,7 @@
         second_kernel,
         [*state, low, high, before, own0, own1, after],
         [((8, 16, 128), F32)] * 2
-        + [(shape, F32) for shape in (fine, mid, *[level_2] * 4, *[level_3] * 4, (4, 128))],
+        + [(shape, F32) for shape in (fine, mid, *[level_2] * 4, *[level_3] * 4, (nx2 * ny2 // 8, 4, 128))],
         [(4,) + level_2, half, half, window, (8, 24, 128), mid, mid, wide, (2, 40, 128),
          fine, fine, fine, (8, 24, 256), mid, (32, 128)],
         keep_in=range(11),

time: 131 us -> 129 us (0.985)
  waiting for transfers between devices: 21.4 us -> 18.6 us
  starting transfers between devices: 50.2 us -> 52 us
    ppermute x12, waiting for transfers between devices: 17.2 us -> 14.3 us  [shift_along(): lax.ppermute(value, axis, [(i, i + by) for i in range(size) if 0 <= i + b...]
    all_to_all x1, starting transfers between devices: 9.7 us -> 12 us  [gather_plane(): return lax.all_to_all(copies, ('gx', 'gy'), 0, 0, tiled=True)]
    pallas_call x7 -> x8, Pallas kernels: 19 us -> 19.5 us  [call(): pl.pallas_call(kernel, out_shape=shapes, in_specs=[pl.BlockSpec(memory_sp...]
  transfers between devices with their start and end apart: 13 -> 13, of which waited for: 10 -> 9; matrix products, arithmetic and copies ran while one was open for 0% -> 0% of each run, Pallas kernels for 4% -> 3%
where the time goes in v5:
time: 129 us; the launch traced here: 128 us
  starting transfers between devices  52 us (40%)
  blocking collectives  36.7 us (28%)
  Pallas kernels  19.5 us (15%)
  waiting for transfers between devices  18.6 us (14%)
    ppermute x12, starting transfers between devices, shift_along(): lax.ppermute(value, axis, [(i, i + by) for i in range(size) if 0 <= i + b...  40 us
    pallas_call x8, Pallas kernels, call(): pl.pallas_call(kernel, out_shape=shapes, in_specs=[pl.BlockSpec(memory_sp...  19.5 us
    all_to_all x1, blocking collectives, local(): lax.all_to_all(jnp.broadcast_to(sums[None], (peers, 1, 128)), 'gz', 0, 0,...  18.6 us
    all_to_all x1, blocking collectives, gather_plane(): return lax.all_to_all(copies, ('gx', 'gy'), 0, 0, tiled=True)  18.1 us
    ppermute x12, waiting for transfers between devices, shift_along(): lax.ppermute(value, axis, [(i, i + by) for i in range(size) if 0 <= i + b...  14.3 us
    all_to_all x1, starting transfers between devices, gather_plane(): return lax.all_to_all(copies, ('gx', 'gy'), 0, 0, tiled=True)  12 us
    all_to_all x1, waiting for transfers between devices, gather_plane(): return lax.all_to_all(copies, ('gx', 'gy'), 0, 0, tiled=True)  4.28 us
  transfers between devices with their start and end apart: 13, of which 9 were waited for; matrix products, arithmetic and copies ran while one was open for 0% of the time, Pallas kernels for 3%

profile of v5, /device:TPU:1, one launch (start us, length us, event | category | flops | bytes accessed | tf_op | source)
XLA Modules:
  0.0 127.8 jit_solution(973229462464443995)
XLA Ops:
  0.6 1.2 shard_map.58
  1.8 1.3 %collective-permute-start.1 = (bf16[8,16,128]{2,1,0:T(8,128)(2,1)S(1)}, bf16[8,16,128]{2,1,0:T(8,128)(2,1)S(1)}, u32[]{:S(2)}, u32[]{:S(2)}) collective-permute-start(bf16[8,16,128]{2,1,0:T(8,128)(2,1)S(1)} %get-tuple-element.40), channel_id=1, source_target_pairs={{1,0},{2,1},{3,2},{4,3},{5,4},{6,5},{7,6},{9,8},{10,9},{11,10},{12... | collective-permute-start | bytes 98312 | tf_op jit(solution)/shard_map/ppermute | solution.py:691
  3.1 5.5 %collective-permute-start = (bf16[8,16,128]{2,1,0:T(8,128)(2,1)S(1)}, bf16[8,16,128]{2,1,0:T(8,128)(2,1)S(1)}, u32[]{:S(2)}, u32[]{:S(2)}) collective-permute-start(bf16[8,16,128]{2,1,0:T(8,128)(2,1)S(1)} %get-tuple-element.40), channel_id=1, source_target_pairs={{0,1},{1,2},{2,3},{3,4},{4,5},{5,6},{6,7},{8,9},{9,10},{10,11},{11... | collective-permute-start | bytes 98312 | tf_op jit(solution)/shard_map/ppermute | solution.py:691
  8.6 1.0 collective-permute-done.before_ref
  9.6 1.3 %collective-permute-start.3 = (bf16[8,6,16,128]{3,2,1,0:T(8,128)(2,1)S(1)}, bf16[8,6,16,128]{3,2,1,0:T(8,128)(2,1)S(1)}, u32[]{:S(2)}, u32[]{:S(2)}) collective-permute-start(bf16[8,6,16,128]{3,2,1,0:T(8,128)(2,1)S(1)} %shard_map.59), channel_id=1, source_target_pairs={{64,0},{128,64},{192,128},{256,192},{320,256},{384,320},{448,384},... | collective-permute-start | bytes 589832 | tf_op jit(solution)/shard_map/ppermute | solution.py:691
  10.9 4.0 %collective-permute-start.2 = (bf16[8,6,16,128]{3,2,1,0:T(8,128)(2,1)S(1)}, bf16[8,6,16,128]{3,2,1,0:T(8,128)(2,1)S(1)}, u32[]{:S(2)}, u32[]{:S(2)}) collective-permute-start(bf16[8,6,16,128]{3,2,1,0:T(8,128)(2,1)S(1)} %shard_map.59), channel_id=1, source_target_pairs={{0,64},{64,128},{128,192},{192,256},{256,320},{320,384},{384,448},... | collective-permute-start | bytes 589832 | tf_op jit(solution)/shard_map/ppermute | solution.py:691
  14.9 1.1 collective-permute-done.3
  16.0 1.5 %collective-permute-done.2 = bf16[8,6,16,128]{3,2,1,0:T(8,128)(2,1)S(1)} collective-permute-done((bf16[8,6,16,128]{3,2,1,0:T(8,128)(2,1)S(1)}, bf16[8,6,16,128]{3,2,1,0:T(8,128)(2,1)S(1)}, u32[]{:S(2)}, u32[]{:S(2)}) %collective-permute-start.2) | collective-permute-done | bytes 196640 | tf_op jit(solution)/shard_map/ppermute | solution.py:691
  17.6 0.2 shard_map.60
  17.8 5.7 %collective-permute-start.4 = (bf16[15,6,16,128]{3,2,1,0:T(8,128)(2,1)S(1)}, bf16[15,6,16,128]{3,2,1,0:T(8,128)(2,1)S(1)}, u32[]{:S(2)}, u32[]{:S(2)}) collective-permute-start(bf16[15,6,16,128]{3,2,1,0:T(8,128)(2,1)S(1)} %get-tuple-element.41), channel_id=1, source_target_pairs={{0,8},{8,16},{16,24},{24,32},{32,40},{40,48},{48,56},{1,9},{9,17},... | collective-permute-start | bytes 1105928 | tf_op jit(solution)/shard_map/ppermute | solution.py:691
  23.4 5.2 %collective-permute-start.5 = (bf16[15,6,16,128]{3,2,1,0:T(8,128)(2,1)S(1)}, bf16[15,6,16,128]{3,2,1,0:T(8,128)(2,1)S(1)}, u32[]{:S(2)}, u32[]{:S(2)}) collective-permute-start(bf16[15,6,16,128]{3,2,1,0:T(8,128)(2,1)S(1)} %get-tuple-element.42), channel_id=1, source_target_pairs={{8,0},{16,8},{24,16},{32,24},{40,32},{48,40},{56,48},{9,1},{17,9},... | collective-permute-start | bytes 1105928 | tf_op jit(solution)/shard_map/ppermute | solution.py:691
  28.7 3.6 %collective-permute-done.5.yp_ref = bf16[15,6,16,128]{3,2,1,0:T(8,128)(2,1)S(1)} collective-permute-done((bf16[15,6,16,128]{3,2,1,0:T(8,128)(2,1)S(1)}, bf16[15,6,16,128]{3,2,1,0:T(8,128)(2,1)S(1)}, u32[]{:S(2)}, u32[]{:S(2)}) %collective-permute-start.5) | collective-permute-done | bytes 368672 | tf_op jit(solution)/shard_map/ppermute | solution.py:691
  32.3 3.1 %shard_map.62 = (f32[6,24,128]{2,1,0:T(8,128)S(1)}, f32[6,24,128]{2,1,0:T(8,128)S(1)}, f32[64,8,128]{2,1,0:T(8,128)}) custom-call(bf16[24,6,16,128]{3,2,1,0:T(8,128)(2,1)S(1)} %pad_maximum_fusion.x_ref, bf16[15,6,16,128]{3,2,1,0:T(8,128)(2,1)S(1)} %collective-permute-done.4.ym_ref, bf16[15,6,16,128]{3,2,1,0:T(8,128)(2,1)S(1)} %collective-permute-done.5.yp_ref), custom_call_target="tpu_custom_call" | custom-call | tf_op jit(solution)/shard_map/pallas_call | solution.py:679
  35.4 12.0 %all-to-all-start = ((f32[64,1,1024]{2,1,0:T(1,128)}), f32[64,1,1024]{2,1,0:T(1,128)S(1)}, u32[]{:S(2)}, u32[]{:S(2)}) async-start(f32[64,1,1024]{2,1,0:T(1,128)} %bitcast), calls=%async_computation | async-start | bytes 524288 | tf_op jit(solution)/shard_map/all_to_all | solution.py:696
  47.5 3.3 %collective-permute-start.6 = (f32[6,24,128]{2,1,0:T(8,128)S(1)}, f32[6,24,128]{2,1,0:T(8,128)S(1)}, u32[]{:S(2)}, u32[]{:S(2)}) collective-permute-start(f32[6,24,128]{2,1,0:T(8,128)S(1)} %get-tuple-element.55), channel_id=1, source_target_pairs={{0,64},{64,128},{128,192},{192,256},{256,320},{320,384},{384,448},... | collective-permute-start | bytes 221192 | tf_op jit(solution)/shard_map/ppermute | solution.py:691
  50.8 1.3 %collective-permute-start.7 = (f32[6,24,128]{2,1,0:T(8,128)S(1)}, f32[6,24,128]{2,1,0:T(8,128)S(1)}, u32[]{:S(2)}, u32[]{:S(2)}) collective-permute-start(f32[6,24,128]{2,1,0:T(8,128)S(1)} %get-tuple-element.56), channel_id=1, source_target_pairs={{64,0},{128,64},{192,128},{256,192},{320,256},{384,320},{448,384},... | collective-permute-start | bytes 221192 | tf_op jit(solution)/shard_map/ppermute | solution.py:691
  52.1 1.6 %collective-permute-done.6.low_ref = f32[6,24,128]{2,1,0:T(8,128)S(1)} collective-permute-done((f32[6,24,128]{2,1,0:T(8,128)S(1)}, f32[6,24,128]{2,1,0:T(8,128)S(1)}, u32[]{:S(2)}, u32[]{:S(2)}) %collective-permute-start.6) | collective-permute-done | bytes 73760 | tf_op jit(solution)/shard_map/ppermute | solution.py:691
  53.7 2.6 %collective-permute-done.7.high_ref = f32[6,24,128]{2,1,0:T(8,128)S(1)} collective-permute-done((f32[6,24,128]{2,1,0:T(8,128)S(1)}, f32[6,24,128]{2,1,0:T(8,128)S(1)}, u32[]{:S(2)}, u32[]{:S(2)}) %collective-permute-start.7) | collective-permute-done | bytes 73760 | tf_op jit(solution)/shard_map/ppermute | solution.py:691
  56.4 4.3 %all-to-all-done = f32[64,1,1024]{2,1,0:T(1,128)S(1)} async-done(((f32[64,1,1024]{2,1,0:T(1,128)}), f32[64,1,1024]{2,1,0:T(1,128)S(1)}, u32[]{:S(2)}, u32[]{:S(2)}) %all-to-all-start) | async-done | bytes 262176 | tf_op jit(solution)/shard_map/all_to_all | solution.py:696
  60.7 4.0 %collective-permute-start.8 = (f32[32,8,128]{2,1,0:T(8,128)S(1)}, f32[32,8,128]{2,1,0:T(8,128)S(1)}, u32[]{:S(2)}, u32[]{:S(2)}) collective-permute-start(f32[32,8,128]{2,1,0:T(8,128)S(1)} %bitcast.10), channel_id=1, source_target_pairs={{0,1},{1,2},{2,3},{3,4},{4,5},{5,6},{6,7},{8,9},{9,10},{10,11},{11... | collective-permute-start | bytes 393224 | tf_op jit(solution)/shard_map/ppermute | solution.py:691
  64.7 1.3 %collective-permute-start.9 = (f32[32,8,128]{2,1,0:T(8,128)S(1)}, f32[32,8,128]{2,1,0:T(8,128)S(1)}, u32[]{:S(2)}, u32[]{:S(2)}) collective-permute-start(f32[32,8,128]{2,1,0:T(8,128)S(1)} %bitcast.8), channel_id=1, source_target_pairs={{1,0},{2,1},{3,2},{4,3},{5,4},{6,5},{7,6},{9,8},{10,9},{11,10},{12... | collective-permute-start | bytes 393224 | tf_op jit(solution)/shard_map/ppermute | solution.py:691
  66.0 4.2 %shard_map.61 = (f32[24,40,256]{2,1,0:T(8,128)S(1)}, f32[25,40,256]{2,1,0:T(8,128)S(1)}, f32[24,40,256]{2,1,0:T(8,128)S(1)}, f32[24,40,256]{2,1,0:T(8,128)S(1)},...) custom-call(bf16[24,6,16,128]{3,2,1,0:T(8,128)(2,1)S(1)} %pad_maximu, ...), custom_call_target="tpu_custom_call" | custom-call | tf_op jit(solution)/shard_map/pallas_call | solution.py:679
  70.2 1.8 %collective-permute-done.9.after_ref = f32[32,8,128]{2,1,0:T(8,128)S(1)} collective-permute-done((f32[32,8,128]{2,1,0:T(8,128)S(1)}, f32[32,8,128]{2,1,0:T(8,128)S(1)}, u32[]{:S(2)}, u32[]{:S(2)}) %collective-permute-start.9) | collective-permute-done | bytes 131104 | tf_op jit(solution)/shard_map/ppermute | solution.py:691
  72.1 7.2 %shard_map.63 = (f32[8,16,128]{2,1,0:T(8,128)S(1)}, f32[8,16,128]{2,1,0:T(8,128)S(1)}, f32[24,40,256]{2,1,0:T(8,128)S(1)}, f32[16,24,128]{2,1,0:T(8,128)S(1)}, f...) custom-call(f32[24,40,256]{2,1,0:T(8,128)S(1)} %get-tuple-element.51, ...), custom_call_target="tpu_custom_call" | custom-call | tf_op jit(solution)/shard_map/pallas_call | solution.py:679
  79.3 18.1 %all_to_all.15 = f32[64,1,512]{2,1,0:T(1,128)S(1)} all-to-all(f32[64,1,512]{2,1,0:T(1,128)S(1)} %bitcast.17), channel_id=1, replica_groups=mesh['gx'=8,'gy'=8,'gz'=8] {'gx','gy'}, dimensions={0} | all-to-all | bytes 262144 | tf_op jit(solution)/shard_map/all_to_all | solution.py:696
  97.4 0.1 fusion.1
  97.5 1.3 %collective-permute-start.11 = (f32[8,8,128]{2,1,0:T(8,128)S(1)}, f32[8,8,128]{2,1,0:T(8,128)S(1)}, u32[]{:S(2)}, u32[]{:S(2)}) collective-permute-start(f32[8,8,128]{2,1,0:T(8,128)S(1)} %bitcast.13), channel_id=1, source_target_pairs={{1,0},{2,1},{3,2},{4,3},{5,4},{6,5},{7,6},{9,8},{10,9},{11,10},{12... | collective-permute-start | bytes 98312 | tf_op jit(solution)/shard_map/ppermute | solution.py:691
  98.8 5.8 %collective-permute-start.10 = (f32[8,8,128]{2,1,0:T(8,128)S(1)}, f32[8,8,128]{2,1,0:T(8,128)S(1)}, u32[]{:S(2)}, u32[]{:S(2)}) collective-permute-start(f32[8,8,128]{2,1,0:T(8,128)S(1)} %bitcast.15), channel_id=1, source_target_pairs={{0,1},{1,2},{2,3},{3,4},{4,5},{5,6},{6,7},{8,9},{9,10},{10,11},{11... | collective-permute-start | bytes 98312 | tf_op jit(solution)/shard_map/ppermute | solution.py:691
  104.6 1.0 collective-permute-done.10.before_ref
  105.6 2.8 %shard_map.64 = (f32[8,16,128]{2,1,0:T(8,128)S(1)}, f32[1,128]{1,0:T(1,128)S(1)}) custom-call(f32[25,40,256]{2,1,0:T(8,128)S(1)} %get-tuple-element.43.f0_ref, f32[24,40,256]{2,1,0:T(8,128)S(1)} %get-tuple-element.44.f1_ref, f32[24,40,256]{2,1,0:T(8,128)S(1)} %get-tuple-element.45.f2_ref, f32[24,40,256]{2,1,0:T(8,128)S(1)} %get-tuple-element.46.w_ref, ...), custom_call_target="tpu_custom_call" | custom-call | tf_op jit(solution)/shard_map/pallas_call | solution.py:679
  108.4 18.6 %all_to_all.16.sums_ref = f32[8,1,128]{2,1,0:T(1,128)S(1)} all-to-all(f32[8,1,128]{2,1,0:T(1,128)S(1)} %broadcast_in_dim.9), channel_id=1, replica_groups=mesh['gx'=8,'gy'=8,'gz'=8] {'gz'}, dimensions={0} | all-to-all | bytes 8192 | tf_op jit(solution)/shard_map/all_to_all | solution.py:773
  127.0 0.8 shard_map.65
  (10 shorter events, 0.2 us)
Async XLA Ops:
  1.8 6.8 %collective-permute-start.1 = (bf16[8,16,128]{2,1,0:T(8,128)(2,1)S(1)}, bf16[8,16,128]{2,1,0:T(8,128)(2,1)S(1)}, u32[]{:S(2)}, u32[]{:S(2)}) collective-permute-start(bf16[8,16,128]{2,1,0:T(8,128)(2,1)S(1)} %get-tuple-element.40), channel_id=1, source_target_pairs={{1,0},{2,1},{3,2},{4,3},{5,4},{6,5},{7,6},{9,8},{10,9},{11,10},{12... | collective-permute-start | bytes 98312 | tf_op jit(solution)/shard_map/ppermute | solution.py:691
  3.1 6.5 %collective-permute-start = (bf16[8,16,128]{2,1,0:T(8,128)(2,1)S(1)}, bf16[8,16,128]{2,1,0:T(8,128)(2,1)S(1)}, u32[]{:S(2)}, u32[]{:S(2)}) collective-permute-start(bf16[8,16,128]{2,1,0:T(8,128)(2,1)S(1)} %get-tuple-element.40), channel_id=1, source_target_pairs={{0,1},{1,2},{2,3},{3,4},{4,5},{5,6},{6,7},{8,9},{9,10},{10,11},{11... | collective-permute-start | bytes 98312 | tf_op jit(solution)/shard_map/ppermute | solution.py:691
  9.6 6.4 %collective-permute-start.3 = (bf16[8,6,16,128]{3,2,1,0:T(8,128)(2,1)S(1)}, bf16[8,6,16,128]{3,2,1,0:T(8,128)(2,1)S(1)}, u32[]{:S(2)}, u32[]{:S(2)}) collective-permute-start(bf16[8,6,16,128]{3,2,1,0:T(8,128)(2,1)S(1)} %shard_map.59), channel_id=1, source_target_pairs={{64,0},{128,64},{192,128},{256,192},{320,256},{384,320},{448,384},... | collective-permute-start | bytes 589832 | tf_op jit(solution)/shard_map/ppermute | solution.py:691
  10.9 6.6 %collective-permute-start.2 = (bf16[8,6,16,128]{3,2,1,0:T(8,128)(2,1)S(1)}, bf16[8,6,16,128]{3,2,1,0:T(8,128)(2,1)S(1)}, u32[]{:S(2)}, u32[]{:S(2)}) collective-permute-start(bf16[8,6,16,128]{3,2,1,0:T(8,128)(2,1)S(1)} %shard_map.59), channel_id=1, source_target_pairs={{0,64},{64,128},{128,192},{192,256},{256,320},{320,384},{384,448},... | collective-permute-start | bytes 589832 | tf_op jit(solution)/shard_map/ppermute | solution.py:691
  17.8 10.9 %collective-permute-start.4 = (bf16[15,6,16,128]{3,2,1,0:T(8,128)(2,1)S(1)}, bf16[15,6,16,128]{3,2,1,0:T(8,128)(2,1)S(1)}, u32[]{:S(2)}, u32[]{:S(2)}) collective-permute-start(bf16[15,6,16,128]{3,2,1,0:T(8,128)(2,1)S(1)} %get-tuple-element.41), channel_id=1, source_target_pairs={{0,8},{8,16},{16,24},{24,32},{32,40},{40,48},{48,56},{1,9},{9,17},... | collective-permute-start | bytes 1105928 | tf_op jit(solution)/shard_map/ppermute | solution.py:691
  23.4 8.8 %collective-permute-start.5 = (bf16[15,6,16,128]{3,2,1,0:T(8,128)(2,1)S(1)}, bf16[15,6,16,128]{3,2,1,0:T(8,128)(2,1)S(1)}, u32[]{:S(2)}, u32[]{:S(2)}) collective-permute-start(bf16[15,6,16,128]{3,2,1,0:T(8,128)(2,1)S(1)} %get-tuple-element.42), channel_id=1, source_target_pairs={{8,0},{16,8},{24,16},{32,24},{40,32},{48,40},{56,48},{9,1},{17,9},... | collective-permute-start | bytes 1105928 | tf_op jit(solution)/shard_map/ppermute | solution.py:691
  35.4 25.2 %all-to-all-start = ((f32[64,1,1024]{2,1,0:T(1,128)}), f32[64,1,1024]{2,1,0:T(1,128)S(1)}, u32[]{:S(2)}, u32[]{:S(2)}) async-start(f32[64,1,1024]{2,1,0:T(1,128)} %bitcast), calls=%async_computation | async-start | bytes 524288 | tf_op jit(solution)/shard_map/all_to_all | solution.py:696
  47.5 6.2 %collective-permute-start.6 = (f32[6,24,128]{2,1,0:T(8,128)S(1)}, f32[6,24,128]{2,1,0:T(8,128)S(1)}, u32[]{:S(2)}, u32[]{:S(2)}) collective-permute-start(f32[6,24,128]{2,1,0:T(8,128)S(1)} %get-tuple-element.55), channel_id=1, source_target_pairs={{0,64},{64,128},{128,192},{192,256},{256,320},{320,384},{384,448},... | collective-permute-start | bytes 221192 | tf_op jit(solution)/shard_map/ppermute | solution.py:691
  50.8 5.6 %collective-permute-start.7 = (f32[6,24,128]{2,1,0:T(8,128)S(1)}, f32[6,24,128]{2,1,0:T(8,128)S(1)}, u32[]{:S(2)}, u32[]{:S(2)}) collective-permute-start(f32[6,24,128]{2,1,0:T(8,128)S(1)} %get-tuple-element.56), channel_id=1, source_target_pairs={{64,0},{128,64},{192,128},{256,192},{320,256},{384,320},{448,384},... | collective-permute-start | bytes 221192 | tf_op jit(solution)/shard_map/ppermute | solution.py:691
  60.7 9.5 %collective-permute-start.8 = (f32[32,8,128]{2,1,0:T(8,128)S(1)}, f32[32,8,128]{2,1,0:T(8,128)S(1)}, u32[]{:S(2)}, u32[]{:S(2)}) collective-permute-start(f32[32,8,128]{2,1,0:T(8,128)S(1)} %bitcast.10), channel_id=1, source_target_pairs={{0,1},{1,2},{2,3},{3,4},{4,5},{5,6},{6,7},{8,9},{9,10},{10,11},{11... | collective-permute-start | bytes 393224 | tf_op jit(solution)/shard_map/ppermute | solution.py:691
  64.7 7.4 %collective-permute-start.9 = (f32[32,8,128]{2,1,0:T(8,128)S(1)}, f32[32,8,128]{2,1,0:T(8,128)S(1)}, u32[]{:S(2)}, u32[]{:S(2)}) collective-permute-start(f32[32,8,128]{2,1,0:T(8,128)S(1)} %bitcast.8), channel_id=1, source_target_pairs={{1,0},{2,1},{3,2},{4,3},{5,4},{6,5},{7,6},{9,8},{10,9},{11,10},{12... | collective-permute-start | bytes 393224 | tf_op jit(solution)/shard_map/ppermute | solution.py:691
  97.5 7.1 %collective-permute-start.11 = (f32[8,8,128]{2,1,0:T(8,128)S(1)}, f32[8,8,128]{2,1,0:T(8,128)S(1)}, u32[]{:S(2)}, u32[]{:S(2)}) collective-permute-start(f32[8,8,128]{2,1,0:T(8,128)S(1)} %bitcast.13), channel_id=1, source_target_pairs={{1,0},{2,1},{3,2},{4,3},{5,4},{6,5},{7,6},{9,8},{10,9},{11,10},{12... | collective-permute-start | bytes 98312 | tf_op jit(solution)/shard_map/ppermute | solution.py:691
  98.8 6.8 %collective-permute-start.10 = (f32[8,8,128]{2,1,0:T(8,128)S(1)}, f32[8,8,128]{2,1,0:T(8,128)S(1)}, u32[]{:S(2)}, u32[]{:S(2)}) collective-permute-start(f32[8,8,128]{2,1,0:T(8,128)S(1)} %bitcast.15), channel_id=1, source_target_pairs={{0,1},{1,2},{2,3},{3,4},{4,5},{5,6},{6,7},{8,9},{9,10},{10,11},{11... | collective-permute-start | bytes 98312 | tf_op jit(solution)/shard_map/ppermute | solution.py:691
  105.6 21.4 %copy-start = (f32[8,16,128]{2,1,0:T(8,128)S(1)}, f32[8,16,128]{2,1,0:T(8,128)}, u32[]{:S(2)}) copy-start(f32[8,16,128]{2,1,0:T(8,128)} %s_ref.1) | copy-start | bytes 196612

commit v6 on v5

--- a/solution.py
+++ b/solution.py
@@ -13,6 +13,7 @@
 RELAX = 0.8
 KEEP = 0.2
 SWEEPS = 6
+NEAR = pl.ds(8, 24)
 VMEM_LIMIT = 24 * 1024 * 1024
 
 
@@ -59,6 +60,18 @@
         f0_ref[p] * v_ref[p - 1]
         + f0_ref[p + 1] * v_ref[p + 1]
         + plane_terms(v_ref[p], f1_ref[p], f2_ref[p])
+    )
+
+
+def near_rows(v_ref, f0_ref, f1_ref, f2_ref, p):
+    v, f2 = v_ref[p, NEAR, :], f2_ref[p, NEAR, :]
+    return (
+        f0_ref[p, NEAR, :] * v_ref[p - 1, NEAR, :]
+        + f0_ref[p + 1, NEAR, :] * v_ref[p + 1, NEAR, :]
+        + f1_ref[p, NEAR, :] * v_ref[p, pl.ds(7, 24), :]
+        + f1_ref[p, pl.ds(9, 24), :] * v_ref[p, pl.ds(9, 24), :]
+        + turn(v, 1, 1) * f2
+        + turn(v * f2, -1, 1)
     )
 
 
@@ -79,15 +92,15 @@
     out = []
     pairs = values.shape[0] // 2
     for half in range(2):
-        t_ref[half] = values[:, 128 * half : 128 * half + 128]
+        t_ref[half, pl.ds(0, 2 * pairs), :] = values[:, 128 * half : 128 * half + 128]
         first = t_ref[half, pl.ds(0, pairs, 2), :]
         out.append(first + t_ref[half, pl.ds(1, pairs, 2), :] if both else first)
     return out
 
 
-def put_rows(r_ref, q, halves):
+def put_rows(r_ref, q, halves, start=0):
     for half in range(2):
-        r_ref[q, pl.ds(0, halves[half].shape[0]), pl.ds(128 * half, 128)] = halves[half]
+        r_ref[q, pl.ds(start, halves[half].shape[0]), pl.ds(128 * half, 128)] = halves[half]
 
 
 def prepare_kernel(s_hbm, fc_hbm, solid_hbm, out_ref, ends_ref, s_ref, fc_ref, solid_ref, sems):
@@ -224,7 +237,7 @@
         f2_ref[p] = root(c2 * turn(c2, 1, 1))
         return carry
 
-    lax.fori_loop(planes.start, planes.stop, faces, 0, unroll=4)
+    lax.fori_loop(planes.start, planes.stop, faces, 0, unroll=8)
     f0_ref[planes.stop] = jnp.zeros(shape, F32)
 
     first_row = (iota(shape, 0) == own) & at_y
@@ -262,7 +275,7 @@
         put_rows(rs_ref, q, row_pairs(t_ref, total, True))
         return carry
 
-    lax.fori_loop(planes.start // 2 + 1, planes.stop // 2 - 1, leftovers, 0, unroll=2)
+    lax.fori_loop(planes.start // 2 + 1, planes.stop // 2 - 1, leftovers, 0, unroll=3 if thin else 5)
 
     pairs = one_hot(256, 128, lambda r, c: lax.shift_right_logical(r, 1) == c, 0.25)
     evens = one_hot(256, 128, lambda r, c: r == 2 * c, 0.25)
@@ -285,7 +298,7 @@
         f12_ref[p] = jnp.where(first_lane_1, 0.0, l12_ref[p])
         return carry
 
-    lax.fori_loop(planes_1.start, planes_1.stop, faces_1, 0, unroll=4)
+    lax.fori_loop(planes_1.start, planes_1.stop, faces_1, 0, unroll=len(planes_1))
     f10_ref[planes_1.stop] = jnp.zeros(shape_1, F32)
 
     def diagonals_1(p, carry):
@@ -297,7 +310,7 @@
         w1_ref[p] = RELAX / d
         return carry
 
-    lax.fori_loop(planes_1.start, planes_1.stop, diagonals_1, 0, unroll=4)
+    lax.fori_loop(planes_1.start, planes_1.stop, diagonals_1, 0, unroll=len(planes_1))
     if thin:
         pack_level_2(
             up_ref, down_ref, pay_ref, s1_ref, f10_ref, f11_ref, f12_ref, w1_ref, l10_ref, l11_ref, l12_ref, *refs
@@ -414,8 +427,10 @@
 
     widen = one_hot(128, 128, lambda r, c: r == source(c))
     rows = one_hot(24, ny, lambda r, c: c == 4 * gy - 3 + lax.shift_right_logical(r, 1))
+    flat = m2_ref[pl.ds(2 * gx + planes.start, len(planes))].reshape(len(planes) * ny, 128)
+    wide = spread(flat, widen).reshape(len(planes), ny, 128)
     for k in planes:
-        pick_ref[k] = spread(pick(rows, m2_ref[2 * gx + k]), widen)
+        pick_ref[k] = pick(rows, wide[k - planes.start])
 
 
 def widen_level_1(m1_ref, wide_ref, lo, hi):
@@ -426,12 +441,12 @@
     )
 
 
-def double_rows(t_ref, wide_ref, q):
+def double_rows(t_ref, wide_ref, q, start=0, count=20):
     for half in range(2):
-        part = wide_ref[q, pl.ds(0, 20), pl.ds(128 * half, 128)]
-        for i in range(2):
-            t_ref[half, pl.ds(i, 20, 2), :] = part
-    return jnp.concatenate([t_ref[0], t_ref[1]], 1)
+        part = wide_ref[q, pl.ds(start, count), pl.ds(128 * half, 128)]
+        for i in range(2):
+            t_ref[half, pl.ds(i, count, 2), :] = part
+    return jnp.concatenate([t_ref[half, pl.ds(0, 2 * count), :] for half in range(2)], 1)
 
 
 def second_kernel(
@@ -456,7 +471,7 @@
                     v_ref[f, 2 * x + i, pl.ds(8 * pair, 8), :] = window(pieces, 32 * f + 16 * i, lane8)
         return carry
 
-    lax.fori_loop(0, nx2 // 2, assemble, 0, unroll=2)
+    lax.fori_loop(0, nx2 // 2, assemble, 0, unroll=4)
 
     s2 = v_ref[0]
     low = (v_ref[1], v_ref[2], v_ref[3])
@@ -478,7 +493,7 @@
         corr1_ref[p] = w1_ref[p] * s1_ref[p] + pick_ref[lax.shift_right_logical(p, 1)]
         return carry
 
-    lax.fori_loop(3, 13, correct_1, 0, unroll=5)
+    lax.fori_loop(3, 13, correct_1, 0, unroll=10)
     for k in range(2):
         corr1_ref[1 + k] = low_ref[2 + k] * low_ref[k] + pick_ref[(1 + k) // 2]
         corr1_ref[13 + k] = high_ref[2 + k] * high_ref[k] + pick_ref[(13 + k) // 2]
@@ -489,7 +504,7 @@
         )
         return carry
 
-    lax.fori_loop(3, 13, relax_1, 0, unroll=5)
+    lax.fori_loop(3, 13, relax_1, 0, unroll=10)
     for p, source, w, face, next_face in (
         (2, low_ref[1], low_ref[3], low_ref[5], f10_ref[3]),
         (13, high_ref[0], high_ref[2], f10_ref[13], high_ref[5]),
@@ -515,7 +530,15 @@
         )
         return carry
 
-    lax.fori_loop(2, 22, relax, 0, unroll=4)
+    def relax_near(p, carry):
+        fp_ref[p, NEAR, :] = KEEP * corr_ref[p, NEAR, :] + w_ref[p, NEAR, :] * (
+            s_ref[p, NEAR, :] + near_rows(corr_ref, f0_ref, f1_ref, f2_ref, p)
+        )
+        return carry
+
+    lax.fori_loop(2, 7, relax_near, 0, unroll=5)
+    lax.fori_loop(7, 17, relax, 0, unroll=10)
+    lax.fori_loop(17, 22, relax_near, 0, unroll=5)
 
     def image(p, carry):
         im = d_ref[p] * fp_ref[p] - neighbours(fp_ref, f0_ref, f1_ref, f2_ref, p)
@@ -523,29 +546,34 @@
         sm_ref[p] = w_ref[p] * im
         return carry
 
-    lax.fori_loop(3, 21, image, 0, unroll=3)
+    def image_near(p, carry):
+        im = d_ref[p, NEAR, :] * fp_ref[p, NEAR, :] - near_rows(fp_ref, f0_ref, f1_ref, f2_ref, p)
+        im_ref[p, NEAR, :] = im
+        sm_ref[p, NEAR, :] = w_ref[p, NEAR, :] * im
+        return carry
+
+    lax.fori_loop(3, 8, image_near, 0, unroll=5)
+    lax.fori_loop(8, 16, image, 0, unroll=8)
+    lax.fori_loop(16, 21, image_near, 0, unroll=5)
 
     rs_ref[...] = jnp.zeros_like(rs_ref)
-    inside = (iota((40, 128), 0) >= 12) & (iota((40, 128), 0) < 28)
+    inside = (iota((24, 128), 0) >= 4) & (iota((24, 128), 0) < 20)
 
     def leftovers(q, sums):
-        total = jnp.zeros((40, 256), F32)
+        total = jnp.zeros((24, 256), F32)
         for i in range(2):
             p = 2 * q + i - 4
-            left = KEEP * im_ref[p] + neighbours(sm_ref, f0_ref, f1_ref, f2_ref, p)
+            left = KEEP * im_ref[p, NEAR, :] + near_rows(sm_ref, f0_ref, f1_ref, f2_ref, p)
             total += left
-            own = jnp.where(inside & (p >= 8) & (p < 16), 1.0, 0.0)
-            fp, im = fp_ref[p, :, 0:128], im_ref[p, :, 0:128]
-            sums = (
-                sums[0] + own * s_ref[p, :, 0:128] * fp,
-                sums[1] + own * fp * im,
-                sums[2] + own * sm_ref[p, :, 0:128] * (im + left[:, 0:128]),
-            )
-        put_rows(rs_ref, q - 4, row_pairs(t_ref, total, True))
+            own = inside & (p >= 8) & (p < 16)
+            fp, im = fp_ref[p, NEAR, 0:128], im_ref[p, NEAR, 0:128]
+            terms = (s_ref[p, NEAR, 0:128] * fp, fp * im, sm_ref[p, NEAR, 0:128] * (im + left[:, 0:128]))
+            sums = tuple(old + jnp.where(own, new, 0.0) for old, new in zip(sums, terms))
+        put_rows(rs_ref, q - 4, row_pairs(t_ref, total, True), 4)
         return sums
 
-    zero = jnp.zeros((40, 128), F32)
-    sums = lax.fori_loop(4, 12, leftovers, (zero, zero, zero), unroll=2)
+    zero = jnp.zeros((24, 128), F32)
+    sums = lax.fori_loop(4, 12, leftovers, (zero, zero, zero), unroll=8)
 
     for p in range(8):
         fp_out[p] = fp_ref[8 + p, pl.ds(12, 16), 0:128]
@@ -556,9 +584,7 @@
     t1s_ref[pl.ds(4, 8)] = spread(rs_ref[...].reshape(192, 256), pairs).reshape(8, 24, 128)
     for p in range(5, 11):
         sm1_ref[p] = w1_ref[p] * t1s_ref[p]
-    inside_1 = jnp.where(
-        (iota((24, 128), 0) >= 6) & (iota((24, 128), 0) < 14) & (iota((24, 128), 1) < 64), 1.0, 0.0
-    )
+    inside_1 = (iota((24, 128), 0) >= 6) & (iota((24, 128), 0) < 14) & (iota((24, 128), 1) < 64)
     second = jnp.zeros((24, 128), F32)
     halves = [jnp.zeros((8, 128), F32)] * 2
     tq_ref[...] = jnp.zeros_like(tq_ref)
@@ -568,7 +594,7 @@
             p = 6 + 2 * i + j
             s1 = t1s_ref[p]
             left = KEEP * s1 + neighbours(sm1_ref, f10_ref, f11_ref, f12_ref, p)
-            second += inside_1 * sm1_ref[p] * (s1 + left)
+            second += jnp.where(inside_1, sm1_ref[p] * (s1 + left), 0.0)
             total += left
         tq_ref[pl.ds(0, 24), :] = total
         tq_ref[pl.ds(24, 4), :] = tq_ref[pl.ds(6, 4, 2), :] + tq_ref[pl.ds(7, 4, 2), :]
@@ -607,7 +633,7 @@
                 v_ref[2 * x + i, pl.ds(j, ny2 // 4, 4), :] = window(pieces, 32 * j + 16 * i, lane)
         return carry
 
-    lax.fori_loop(0, nx2 // 2, assemble, 0, unroll=2)
+    lax.fori_loop(0, nx2 // 2, assemble, 0, unroll=4)
     s2 = v_ref[...]
     level_2 = (f20_ref[...], f21_ref[...], f22_ref[...], w2_ref[...])
     level_3 = (f30_ref[...], f31_ref[...], f32_ref[...], w3_ref[...])
@@ -629,21 +655,20 @@
     widen_level_1(m1_ref, wide_ref, 5, 11)
 
     def correct(q, carry):
-        e = double_rows(t_ref, wide_ref, q)
+        e = double_rows(t_ref, wide_ref, q, 4, 12)
         for i in range(2):
             p = 2 * q + i - 4
-            corr_ref[p] = w_ref[p] * im_ref[p] + e
-        return carry
-
-    lax.fori_loop(5, 11, correct, 0, unroll=2)
+            corr_ref[p, NEAR, :] = w_ref[p, NEAR, :] * im_ref[p, NEAR, :] + e
+        return carry
+
+    lax.fori_loop(5, 11, correct, 0, unroll=6)
 
     for p in range(8):
         q = 8 + p
-        mi = KEEP * corr_ref[q] + w_ref[q] * (
-            im_ref[q] + neighbours(corr_ref, f0_ref, f1_ref, f2_ref, q)
-        )
-        t_ref[0] = mi[:, 0:128]
-        mi_out[p] = t_ref[0, pl.ds(12, 16), :]
+        mi = KEEP * corr_ref[q, NEAR, :] + w_ref[q, NEAR, :] * (
+            im_ref[q, NEAR, :] + near_rows(corr_ref, f0_ref, f1_ref, f2_ref, q)
+        )
+        mi_out[p] = mi[4:20, 0:128]
 
 
 def last_kernel(sums_ref, s_ref, fp_ref, im_ref, mi_ref, solution_ref, residual_ref, direction_ref):

time: 129 us -> 127 us (0.984)
  Pallas kernels: 19.5 us -> 16.2 us
    pallas_call x8, Pallas kernels: 19.5 us -> 16.2 us  [call(): pl.pallas_call(kernel, out_shape=shapes, in_specs=[pl.BlockSpec(memory_sp...]
where the time goes in v6:
time: 127 us; the launch traced here: 125 us
  starting transfers between devices  52 us (41%)
  blocking collectives  36.7 us (29%)
  waiting for transfers between devices  19.2 us (15%)
  Pallas kernels  16.2 us (13%)
    ppermute x12, starting transfers between devices, shift_along(): lax.ppermute(value, axis, [(i, i + by) for i in range(size) if 0 <= i + b...  39.9 us
    all_to_all x1, blocking collectives, local(): lax.all_to_all(jnp.broadcast_to(sums[None], (peers, 1, 128)), 'gz', 0, 0,...  18.6 us
    all_to_all x1, blocking collectives, gather_plane(): return lax.all_to_all(copies, ('gx', 'gy'), 0, 0, tiled=True)  18.1 us
    pallas_call x8, Pallas kernels, call(): pl.pallas_call(kernel, out_shape=shapes, in_specs=[pl.BlockSpec(memory_sp...  16.2 us
    ppermute x12, waiting for transfers between devices, shift_along(): lax.ppermute(value, axis, [(i, i + by) for i in range(size) if 0 <= i + b...  14.9 us
    all_to_all x1, starting transfers between devices, gather_plane(): return lax.all_to_all(copies, ('gx', 'gy'), 0, 0, tiled=True)  12.1 us
    all_to_all x1, waiting for transfers between devices, gather_plane(): return lax.all_to_all(copies, ('gx', 'gy'), 0, 0, tiled=True)  4.28 us
  transfers between devices with their start and end apart: 13, of which 9 were waited for; matrix products, arithmetic and copies ran while one was open for 0% of the time, Pallas kernels for 3%

profile of v6, /device:TPU:1, one launch (start us, length us, event | category | flops | bytes accessed | tf_op | source)
XLA Modules:
  0.0 125.1 jit_solution(8753947927674812029)
XLA Ops:
  0.6 1.2 shard_map.58
  1.8 1.3 %collective-permute-start.1 = (bf16[8,16,128]{2,1,0:T(8,128)(2,1)S(1)}, bf16[8,16,128]{2,1,0:T(8,128)(2,1)S(1)}, u32[]{:S(2)}, u32[]{:S(2)}) collective-permute-start(bf16[8,16,128]{2,1,0:T(8,128)(2,1)S(1)} %get-tuple-element.40), channel_id=1, source_target_pairs={{1,0},{2,1},{3,2},{4,3},{5,4},{6,5},{7,6},{9,8},{10,9},{11,10},{12... | collective-permute-start | bytes 98312 | tf_op jit(solution)/shard_map/ppermute | solution.py:716
  3.1 5.5 %collective-permute-start = (bf16[8,16,128]{2,1,0:T(8,128)(2,1)S(1)}, bf16[8,16,128]{2,1,0:T(8,128)(2,1)S(1)}, u32[]{:S(2)}, u32[]{:S(2)}) collective-permute-start(bf16[8,16,128]{2,1,0:T(8,128)(2,1)S(1)} %get-tuple-element.40), channel_id=1, source_target_pairs={{0,1},{1,2},{2,3},{3,4},{4,5},{5,6},{6,7},{8,9},{9,10},{10,11},{11... | collective-permute-start | bytes 98312 | tf_op jit(solution)/shard_map/ppermute | solution.py:716
  8.6 1.0 collective-permute-done.before_ref
  9.6 1.3 %collective-permute-start.3 = (bf16[8,6,16,128]{3,2,1,0:T(8,128)(2,1)S(1)}, bf16[8,6,16,128]{3,2,1,0:T(8,128)(2,1)S(1)}, u32[]{:S(2)}, u32[]{:S(2)}) collective-permute-start(bf16[8,6,16,128]{3,2,1,0:T(8,128)(2,1)S(1)} %shard_map.59), channel_id=1, source_target_pairs={{64,0},{128,64},{192,128},{256,192},{320,256},{384,320},{448,384},... | collective-permute-start | bytes 589832 | tf_op jit(solution)/shard_map/ppermute | solution.py:716
  10.9 4.0 %collective-permute-start.2 = (bf16[8,6,16,128]{3,2,1,0:T(8,128)(2,1)S(1)}, bf16[8,6,16,128]{3,2,1,0:T(8,128)(2,1)S(1)}, u32[]{:S(2)}, u32[]{:S(2)}) collective-permute-start(bf16[8,6,16,128]{3,2,1,0:T(8,128)(2,1)S(1)} %shard_map.59), channel_id=1, source_target_pairs={{0,64},{64,128},{128,192},{192,256},{256,320},{320,384},{384,448},... | collective-permute-start | bytes 589832 | tf_op jit(solution)/shard_map/ppermute | solution.py:716
  14.9 1.1 collective-permute-done.3
  16.0 1.5 %collective-permute-done.2 = bf16[8,6,16,128]{3,2,1,0:T(8,128)(2,1)S(1)} collective-permute-done((bf16[8,6,16,128]{3,2,1,0:T(8,128)(2,1)S(1)}, bf16[8,6,16,128]{3,2,1,0:T(8,128)(2,1)S(1)}, u32[]{:S(2)}, u32[]{:S(2)}) %collective-permute-start.2) | collective-permute-done | bytes 196640 | tf_op jit(solution)/shard_map/ppermute | solution.py:716
  17.6 0.2 shard_map.60
  17.8 5.7 %collective-permute-start.4 = (bf16[15,6,16,128]{3,2,1,0:T(8,128)(2,1)S(1)}, bf16[15,6,16,128]{3,2,1,0:T(8,128)(2,1)S(1)}, u32[]{:S(2)}, u32[]{:S(2)}) collective-permute-start(bf16[15,6,16,128]{3,2,1,0:T(8,128)(2,1)S(1)} %get-tuple-element.41), channel_id=1, source_target_pairs={{0,8},{8,16},{16,24},{24,32},{32,40},{40,48},{48,56},{1,9},{9,17},... | collective-permute-start | bytes 1105928 | tf_op jit(solution)/shard_map/ppermute | solution.py:716
  23.4 5.2 %collective-permute-start.5 = (bf16[15,6,16,128]{3,2,1,0:T(8,128)(2,1)S(1)}, bf16[15,6,16,128]{3,2,1,0:T(8,128)(2,1)S(1)}, u32[]{:S(2)}, u32[]{:S(2)}) collective-permute-start(bf16[15,6,16,128]{3,2,1,0:T(8,128)(2,1)S(1)} %get-tuple-element.42), channel_id=1, source_target_pairs={{8,0},{16,8},{24,16},{32,24},{40,32},{48,40},{56,48},{9,1},{17,9},... | collective-permute-start | bytes 1105928 | tf_op jit(solution)/shard_map/ppermute | solution.py:716
  28.7 3.6 %collective-permute-done.5.yp_ref = bf16[15,6,16,128]{3,2,1,0:T(8,128)(2,1)S(1)} collective-permute-done((bf16[15,6,16,128]{3,2,1,0:T(8,128)(2,1)S(1)}, bf16[15,6,16,128]{3,2,1,0:T(8,128)(2,1)S(1)}, u32[]{:S(2)}, u32[]{:S(2)}) %collective-permute-start.5) | collective-permute-done | bytes 368672 | tf_op jit(solution)/shard_map/ppermute | solution.py:716
  32.3 2.8 %shard_map.62 = (f32[6,24,128]{2,1,0:T(8,128)S(1)}, f32[6,24,128]{2,1,0:T(8,128)S(1)}, f32[64,8,128]{2,1,0:T(8,128)}) custom-call(bf16[24,6,16,128]{3,2,1,0:T(8,128)(2,1)S(1)} %pad_maximum_fusion.x_ref, bf16[15,6,16,128]{3,2,1,0:T(8,128)(2,1)S(1)} %collective-permute-done.4.ym_ref, bf16[15,6,16,128]{3,2,1,0:T(8,128)(2,1)S(1)} %collective-permute-done.5.yp_ref), custom_call_target="tpu_custom_call" | custom-call | tf_op jit(solution)/shard_map/pallas_call | solution.py:704
  35.0 12.1 %all-to-all-start = ((f32[64,1,1024]{2,1,0:T(1,128)}), f32[64,1,1024]{2,1,0:T(1,128)S(1)}, u32[]{:S(2)}, u32[]{:S(2)}) async-start(f32[64,1,1024]{2,1,0:T(1,128)} %bitcast), calls=%async_computation | async-start | bytes 524288 | tf_op jit(solution)/shard_map/all_to_all | solution.py:721
  47.1 3.3 %collective-permute-start.6 = (f32[6,24,128]{2,1,0:T(8,128)S(1)}, f32[6,24,128]{2,1,0:T(8,128)S(1)}, u32[]{:S(2)}, u32[]{:S(2)}) collective-permute-start(f32[6,24,128]{2,1,0:T(8,128)S(1)} %get-tuple-element.55), channel_id=1, source_target_pairs={{0,64},{64,128},{128,192},{192,256},{256,320},{320,384},{384,448},... | collective-permute-start | bytes 221192 | tf_op jit(solution)/shard_map/ppermute | solution.py:716
  50.4 1.3 %collective-permute-start.7 = (f32[6,24,128]{2,1,0:T(8,128)S(1)}, f32[6,24,128]{2,1,0:T(8,128)S(1)}, u32[]{:S(2)}, u32[]{:S(2)}) collective-permute-start(f32[6,24,128]{2,1,0:T(8,128)S(1)} %get-tuple-element.56), channel_id=1, source_target_pairs={{64,0},{128,64},{192,128},{256,192},{320,256},{384,320},{448,384},... | collective-permute-start | bytes 221192 | tf_op jit(solution)/shard_map/ppermute | solution.py:716
  51.7 1.6 %collective-permute-done.6.low_ref = f32[6,24,128]{2,1,0:T(8,128)S(1)} collective-permute-done((f32[6,24,128]{2,1,0:T(8,128)S(1)}, f32[6,24,128]{2,1,0:T(8,128)S(1)}, u32[]{:S(2)}, u32[]{:S(2)}) %collective-permute-start.6) | collective-permute-done | bytes 73760 | tf_op jit(solution)/shard_map/ppermute | solution.py:716
  53.3 2.6 %collective-permute-done.7.high_ref = f32[6,24,128]{2,1,0:T(8,128)S(1)} collective-permute-done((f32[6,24,128]{2,1,0:T(8,128)S(1)}, f32[6,24,128]{2,1,0:T(8,128)S(1)}, u32[]{:S(2)}, u32[]{:S(2)}) %collective-permute-start.7) | collective-permute-done | bytes 73760 | tf_op jit(solution)/shard_map/ppermute | solution.py:716
  56.0 4.3 %all-to-all-done = f32[64,1,1024]{2,1,0:T(1,128)S(1)} async-done(((f32[64,1,1024]{2,1,0:T(1,128)}), f32[64,1,1024]{2,1,0:T(1,128)S(1)}, u32[]{:S(2)}, u32[]{:S(2)}) %all-to-all-start) | async-done | bytes 262176 | tf_op jit(solution)/shard_map/all_to_all | solution.py:721
  60.3 4.0 %collective-permute-start.8 = (f32[32,8,128]{2,1,0:T(8,128)S(1)}, f32[32,8,128]{2,1,0:T(8,128)S(1)}, u32[]{:S(2)}, u32[]{:S(2)}) collective-permute-start(f32[32,8,128]{2,1,0:T(8,128)S(1)} %bitcast.10), channel_id=1, source_target_pairs={{0,1},{1,2},{2,3},{3,4},{4,5},{5,6},{6,7},{8,9},{9,10},{10,11},{11... | collective-permute-start | bytes 393224 | tf_op jit(solution)/shard_map/ppermute | solution.py:716
  64.3 1.3 %collective-permute-start.9 = (f32[32,8,128]{2,1,0:T(8,128)S(1)}, f32[32,8,128]{2,1,0:T(8,128)S(1)}, u32[]{:S(2)}, u32[]{:S(2)}) collective-permute-start(f32[32,8,128]{2,1,0:T(8,128)S(1)} %bitcast.8), channel_id=1, source_target_pairs={{1,0},{2,1},{3,2},{4,3},{5,4},{6,5},{7,6},{9,8},{10,9},{11,10},{12... | collective-permute-start | bytes 393224 | tf_op jit(solution)/shard_map/ppermute | solution.py:716
  65.6 3.6 %shard_map.61 = (f32[24,40,256]{2,1,0:T(8,128)S(1)}, f32[25,40,256]{2,1,0:T(8,128)S(1)}, f32[24,40,256]{2,1,0:T(8,128)S(1)}, f32[24,40,256]{2,1,0:T(8,128)S(1)},...) custom-call(bf16[24,6,16,128]{3,2,1,0:T(8,128)(2,1)S(1)} %pad_maximu, ...), custom_call_target="tpu_custom_call" | custom-call | tf_op jit(solution)/shard_map/pallas_call | solution.py:704
  69.2 2.4 %collective-permute-done.9.after_ref = f32[32,8,128]{2,1,0:T(8,128)S(1)} collective-permute-done((f32[32,8,128]{2,1,0:T(8,128)S(1)}, f32[32,8,128]{2,1,0:T(8,128)S(1)}, u32[]{:S(2)}, u32[]{:S(2)}) %collective-permute-start.9) | collective-permute-done | bytes 131104 | tf_op jit(solution)/shard_map/ppermute | solution.py:716
  71.7 5.4 %shard_map.63 = (f32[8,16,128]{2,1,0:T(8,128)S(1)}, f32[8,16,128]{2,1,0:T(8,128)S(1)}, f32[24,40,256]{2,1,0:T(8,128)S(1)}, f32[16,24,128]{2,1,0:T(8,128)S(1)}, f...) custom-call(f32[24,40,256]{2,1,0:T(8,128)S(1)} %get-tuple-element.51, ...), custom_call_target="tpu_custom_call" | custom-call | tf_op jit(solution)/shard_map/pallas_call | solution.py:704
  77.1 18.1 %all_to_all.15 = f32[64,1,512]{2,1,0:T(1,128)S(1)} all-to-all(f32[64,1,512]{2,1,0:T(1,128)S(1)} %bitcast.17), channel_id=1, replica_groups=mesh['gx'=8,'gy'=8,'gz'=8] {'gx','gy'}, dimensions={0} | all-to-all | bytes 262144 | tf_op jit(solution)/shard_map/all_to_all | solution.py:721
  95.2 0.1 fusion.1
  95.3 1.3 %collective-permute-start.11 = (f32[8,8,128]{2,1,0:T(8,128)S(1)}, f32[8,8,128]{2,1,0:T(8,128)S(1)}, u32[]{:S(2)}, u32[]{:S(2)}) collective-permute-start(f32[8,8,128]{2,1,0:T(8,128)S(1)} %bitcast.13), channel_id=1, source_target_pairs={{1,0},{2,1},{3,2},{4,3},{5,4},{6,5},{7,6},{9,8},{10,9},{11,10},{12... | collective-permute-start | bytes 98312 | tf_op jit(solution)/shard_map/ppermute | solution.py:716
  96.6 5.8 %collective-permute-start.10 = (f32[8,8,128]{2,1,0:T(8,128)S(1)}, f32[8,8,128]{2,1,0:T(8,128)S(1)}, u32[]{:S(2)}, u32[]{:S(2)}) collective-permute-start(f32[8,8,128]{2,1,0:T(8,128)S(1)} %bitcast.15), channel_id=1, source_target_pairs={{0,1},{1,2},{2,3},{3,4},{4,5},{5,6},{6,7},{8,9},{9,10},{10,11},{11... | collective-permute-start | bytes 98312 | tf_op jit(solution)/shard_map/ppermute | solution.py:716
  102.4 1.0 collective-permute-done.10.before_ref
  103.4 2.3 %shard_map.64 = (f32[8,16,128]{2,1,0:T(8,128)S(1)}, f32[1,128]{1,0:T(1,128)S(1)}) custom-call(f32[25,40,256]{2,1,0:T(8,128)S(1)} %get-tuple-element.43.f0_ref, f32[24,40,256]{2,1,0:T(8,128)S(1)} %get-tuple-element.44.f1_ref, f32[24,40,256]{2,1,0:T(8,128)S(1)} %get-tuple-element.45.f2_ref, f32[24,40,256]{2,1,0:T(8,128)S(1)} %get-tuple-element.46.w_ref, ...), custom_call_target="tpu_custom_call" | custom-call | tf_op jit(solution)/shard_map/pallas_call | solution.py:704
  105.7 18.6 %all_to_all.16.sums_ref = f32[8,1,128]{2,1,0:T(1,128)S(1)} all-to-all(f32[8,1,128]{2,1,0:T(1,128)S(1)} %broadcast_in_dim.9), channel_id=1, replica_groups=mesh['gx'=8,'gy'=8,'gz'=8] {'gz'}, dimensions={0} | all-to-all | bytes 8192 | tf_op jit(solution)/shard_map/all_to_all | solution.py:798
  124.3 0.8 shard_map.65
  (10 shorter events, 0.2 us)
Async XLA Ops:
  1.8 6.8 %collective-permute-start.1 = (bf16[8,16,128]{2,1,0:T(8,128)(2,1)S(1)}, bf16[8,16,128]{2,1,0:T(8,128)(2,1)S(1)}, u32[]{:S(2)}, u32[]{:S(2)}) collective-permute-start(bf16[8,16,128]{2,1,0:T(8,128)(2,1)S(1)} %get-tuple-element.40), channel_id=1, source_target_pairs={{1,0},{2,1},{3,2},{4,3},{5,4},{6,5},{7,6},{9,8},{10,9},{11,10},{12... | collective-permute-start | bytes 98312 | tf_op jit(solution)/shard_map/ppermute | solution.py:716
  3.1 6.5 %collective-permute-start = (bf16[8,16,128]{2,1,0:T(8,128)(2,1)S(1)}, bf16[8,16,128]{2,1,0:T(8,128)(2,1)S(1)}, u32[]{:S(2)}, u32[]{:S(2)}) collective-permute-start(bf16[8,16,128]{2,1,0:T(8,128)(2,1)S(1)} %get-tuple-element.40), channel_id=1, source_target_pairs={{0,1},{1,2},{2,3},{3,4},{4,5},{5,6},{6,7},{8,9},{9,10},{10,11},{11... | collective-permute-start | bytes 98312 | tf_op jit(solution)/shard_map/ppermute | solution.py:716
  9.6 6.4 %collective-permute-start.3 = (bf16[8,6,16,128]{3,2,1,0:T(8,128)(2,1)S(1)}, bf16[8,6,16,128]{3,2,1,0:T(8,128)(2,1)S(1)}, u32[]{:S(2)}, u32[]{:S(2)}) collective-permute-start(bf16[8,6,16,128]{3,2,1,0:T(8,128)(2,1)S(1)} %shard_map.59), channel_id=1, source_target_pairs={{64,0},{128,64},{192,128},{256,192},{320,256},{384,320},{448,384},... | collective-permute-start | bytes 589832 | tf_op jit(solution)/shard_map/ppermute | solution.py:716
  10.9 6.6 %collective-permute-start.2 = (bf16[8,6,16,128]{3,2,1,0:T(8,128)(2,1)S(1)}, bf16[8,6,16,128]{3,2,1,0:T(8,128)(2,1)S(1)}, u32[]{:S(2)}, u32[]{:S(2)}) collective-permute-start(bf16[8,6,16,128]{3,2,1,0:T(8,128)(2,1)S(1)} %shard_map.59), channel_id=1, source_target_pairs={{0,64},{64,128},{128,192},{192,256},{256,320},{320,384},{384,448},... | collective-permute-start | bytes 589832 | tf_op jit(solution)/shard_map/ppermute | solution.py:716
  17.8 10.9 %collective-permute-start.4 = (bf16[15,6,16,128]{3,2,1,0:T(8,128)(2,1)S(1)}, bf16[15,6,16,128]{3,2,1,0:T(8,128)(2,1)S(1)}, u32[]{:S(2)}, u32[]{:S(2)}) collective-permute-start(bf16[15,6,16,128]{3,2,1,0:T(8,128)(2,1)S(1)} %get-tuple-element.41), channel_id=1, source_target_pairs={{0,8},{8,16},{16,24},{24,32},{32,40},{40,48},{48,56},{1,9},{9,17},... | collective-permute-start | bytes 1105928 | tf_op jit(solution)/shard_map/ppermute | solution.py:716
  23.4 8.8 %collective-permute-start.5 = (bf16[15,6,16,128]{3,2,1,0:T(8,128)(2,1)S(1)}, bf16[15,6,16,128]{3,2,1,0:T(8,128)(2,1)S(1)}, u32[]{:S(2)}, u32[]{:S(2)}) collective-permute-start(bf16[15,6,16,128]{3,2,1,0:T(8,128)(2,1)S(1)} %get-tuple-element.42), channel_id=1, source_target_pairs={{8,0},{16,8},{24,16},{32,24},{40,32},{48,40},{56,48},{9,1},{17,9},... | collective-permute-start | bytes 1105928 | tf_op jit(solution)/shard_map/ppermute | solution.py:716
  35.0 25.2 %all-to-all-start = ((f32[64,1,1024]{2,1,0:T(1,128)}), f32[64,1,1024]{2,1,0:T(1,128)S(1)}, u32[]{:S(2)}, u32[]{:S(2)}) async-start(f32[64,1,1024]{2,1,0:T(1,128)} %bitcast), calls=%async_computation | async-start | bytes 524288 | tf_op jit(solution)/shard_map/all_to_all | solution.py:721
  47.1 6.2 %collective-permute-start.6 = (f32[6,24,128]{2,1,0:T(8,128)S(1)}, f32[6,24,128]{2,1,0:T(8,128)S(1)}, u32[]{:S(2)}, u32[]{:S(2)}) collective-permute-start(f32[6,24,128]{2,1,0:T(8,128)S(1)} %get-tuple-element.55), channel_id=1, source_target_pairs={{0,64},{64,128},{128,192},{192,256},{256,320},{320,384},{384,448},... | collective-permute-start | bytes 221192 | tf_op jit(solution)/shard_map/ppermute | solution.py:716
  50.4 5.6 %collective-permute-start.7 = (f32[6,24,128]{2,1,0:T(8,128)S(1)}, f32[6,24,128]{2,1,0:T(8,128)S(1)}, u32[]{:S(2)}, u32[]{:S(2)}) collective-permute-start(f32[6,24,128]{2,1,0:T(8,128)S(1)} %get-tuple-element.56), channel_id=1, source_target_pairs={{64,0},{128,64},{192,128},{256,192},{320,256},{384,320},{448,384},... | collective-permute-start | bytes 221192 | tf_op jit(solution)/shard_map/ppermute | solution.py:716
  60.3 8.9 %collective-permute-start.8 = (f32[32,8,128]{2,1,0:T(8,128)S(1)}, f32[32,8,128]{2,1,0:T(8,128)S(1)}, u32[]{:S(2)}, u32[]{:S(2)}) collective-permute-start(f32[32,8,128]{2,1,0:T(8,128)S(1)} %bitcast.10), channel_id=1, source_target_pairs={{0,1},{1,2},{2,3},{3,4},{4,5},{5,6},{6,7},{8,9},{9,10},{10,11},{11... | collective-permute-start | bytes 393224 | tf_op jit(solution)/shard_map/ppermute | solution.py:716
  64.3 7.4 %collective-permute-start.9 = (f32[32,8,128]{2,1,0:T(8,128)S(1)}, f32[32,8,128]{2,1,0:T(8,128)S(1)}, u32[]{:S(2)}, u32[]{:S(2)}) collective-permute-start(f32[32,8,128]{2,1,0:T(8,128)S(1)} %bitcast.8), channel_id=1, source_target_pairs={{1,0},{2,1},{3,2},{4,3},{5,4},{6,5},{7,6},{9,8},{10,9},{11,10},{12... | collective-permute-start | bytes 393224 | tf_op jit(solution)/shard_map/ppermute | solution.py:716
  95.3 7.2 %collective-permute-start.11 = (f32[8,8,128]{2,1,0:T(8,128)S(1)}, f32[8,8,128]{2,1,0:T(8,128)S(1)}, u32[]{:S(2)}, u32[]{:S(2)}) collective-permute-start(f32[8,8,128]{2,1,0:T(8,128)S(1)} %bitcast.13), channel_id=1, source_target_pairs={{1,0},{2,1},{3,2},{4,3},{5,4},{6,5},{7,6},{9,8},{10,9},{11,10},{12... | collective-permute-start | bytes 98312 | tf_op jit(solution)/shard_map/ppermute | solution.py:716
  96.6 6.9 %collective-permute-start.10 = (f32[8,8,128]{2,1,0:T(8,128)S(1)}, f32[8,8,128]{2,1,0:T(8,128)S(1)}, u32[]{:S(2)}, u32[]{:S(2)}) collective-permute-start(f32[8,8,128]{2,1,0:T(8,128)S(1)} %bitcast.15), channel_id=1, source_target_pairs={{0,1},{1,2},{2,3},{3,4},{4,5},{5,6},{6,7},{8,9},{9,10},{10,11},{11... | collective-permute-start | bytes 98312 | tf_op jit(solution)/shard_map/ppermute | solution.py:716
  103.4 20.9 %copy-start = (f32[8,16,128]{2,1,0:T(8,128)S(1)}, f32[8,16,128]{2,1,0:T(8,128)}, u32[]{:S(2)}) copy-start(f32[8,16,128]{2,1,0:T(8,128)} %s_ref.1) | copy-start | bytes 196612

commit v7 on v6

--- a/solution.py
+++ b/solution.py
@@ -166,7 +166,7 @@
             down_ref[11 + t, f] = jnp.concatenate(downs, 0).astype(BF16)
         return carry
 
-    lax.fori_loop(0, 6, body, 0)
+    lax.fori_loop(0, 6, body, 0, unroll=2)
 
 
 def edge_rows(ym_ref, yp_ref, p, f, thin):
@@ -237,7 +237,7 @@
         f2_ref[p] = root(c2 * turn(c2, 1, 1))
         return carry
 
-    lax.fori_loop(planes.start, planes.stop, faces, 0, unroll=8)
+    lax.fori_loop(planes.start, planes.stop, faces, 0, unroll=len(planes))
     f0_ref[planes.stop] = jnp.zeros(shape, F32)
 
     first_row = (iota(shape, 0) == own) & at_y
@@ -265,7 +265,7 @@
         put_rows(r2_ref, q, row_pairs(t_ref, lows[0][2] + lows[1][2], True))
         return carry
 
-    lax.fori_loop(planes.start // 2, planes.stop // 2, diagonals, 0, unroll=2)
+    lax.fori_loop(planes.start // 2, planes.stop // 2, diagonals, 0, unroll=len(planes) // 2)
 
     def leftovers(q, carry):
         total = jnp.zeros(shape, F32)
@@ -275,7 +275,7 @@
         put_rows(rs_ref, q, row_pairs(t_ref, total, True))
         return carry
 
-    lax.fori_loop(planes.start // 2 + 1, planes.stop // 2 - 1, leftovers, 0, unroll=3 if thin else 5)
+    lax.fori_loop(planes.start // 2 + 1, planes.stop // 2 - 1, leftovers, 0, unroll=len(planes) // 2 - 2)
 
     pairs = one_hot(256, 128, lambda r, c: lax.shift_right_logical(r, 1) == c, 0.25)
     evens = one_hot(256, 128, lambda r, c: r == 2 * c, 0.25)
@@ -471,7 +471,7 @@
                     v_ref[f, 2 * x + i, pl.ds(8 * pair, 8), :] = window(pieces, 32 * f + 16 * i, lane8)
         return carry
 
-    lax.fori_loop(0, nx2 // 2, assemble, 0, unroll=4)
+    lax.fori_loop(0, nx2 // 2, assemble, 0, unroll=8)
 
     s2 = v_ref[0]
     low = (v_ref[1], v_ref[2], v_ref[3])
@@ -522,7 +522,7 @@
             corr_ref[p] = w_ref[p] * s_ref[p] + e
         return carry
 
-    lax.fori_loop(2, 14, correct, 0, unroll=2)
+    lax.fori_loop(2, 14, correct, 0, unroll=12)
 
     def relax(p, carry):
         fp_ref[p] = KEEP * corr_ref[p] + w_ref[p] * (
@@ -633,7 +633,7 @@
                 v_ref[2 * x + i, pl.ds(j, ny2 // 4, 4), :] = window(pieces, 32 * j + 16 * i, lane)
         return carry
 
-    lax.fori_loop(0, nx2 // 2, assemble, 0, unroll=4)
+    lax.fori_loop(0, nx2 // 2, assemble, 0, unroll=8)
     s2 = v_ref[...]
     level_2 = (f20_ref[...], f21_ref[...], f22_ref[...], w2_ref[...])
     level_3 = (f30_ref[...], f31_ref[...], f32_ref[...], w3_ref[...])

time: 127 us -> 125 us (0.984)
  Pallas kernels: 16.2 us -> 14.4 us
    pallas_call x8, Pallas kernels: 16.2 us -> 14.4 us  [call(): pl.pallas_call(kernel, out_shape=shapes, in_specs=[pl.BlockSpec(memory_sp...]
where the time goes in v7:
time: 125 us; the launch traced here: 124 us
  starting transfers between devices  52 us (42%)
  blocking collectives  36.7 us (29%)
  waiting for transfers between devices  19.6 us (16%)
  Pallas kernels  14.4 us (12%)
    ppermute x12, starting transfers between devices, shift_along(): lax.ppermute(value, axis, [(i, i + by) for i in range(size) if 0 <= i + b...  40 us
    all_to_all x1, blocking collectives, local(): lax.all_to_all(jnp.broadcast_to(sums[None], (peers, 1, 128)), 'gz', 0, 0,...  18.6 us
    all_to_all x1, blocking collectives, gather_plane(): return lax.all_to_all(copies, ('gx', 'gy'), 0, 0, tiled=True)  18.1 us
    ppermute x12, waiting for transfers between devices, shift_along(): lax.ppermute(value, axis, [(i, i + by) for i in range(size) if 0 <= i + b...  15.3 us
    pallas_call x8, Pallas kernels, call(): pl.pallas_call(kernel, out_shape=shapes, in_specs=[pl.BlockSpec(memory_sp...  14.4 us
    all_to_all x1, starting transfers between devices, gather_plane(): return lax.all_to_all(copies, ('gx', 'gy'), 0, 0, tiled=True)  12.1 us
    all_to_all x1, waiting for transfers between devices, gather_plane(): return lax.all_to_all(copies, ('gx', 'gy'), 0, 0, tiled=True)  4.28 us
  transfers between devices with their start and end apart: 13, of which 9 were waited for; matrix products, arithmetic and copies ran while one was open for 0% of the time, Pallas kernels for 3%

profile of v7, /device:TPU:1, one launch (start us, length us, event | category | flops | bytes accessed | tf_op | source)
XLA Modules:
  0.0 123.7 jit_solution(1635577869117336826)
XLA Ops:
  0.6 1.2 shard_map.58
  1.8 1.3 %collective-permute-start.1 = (bf16[8,16,128]{2,1,0:T(8,128)(2,1)S(1)}, bf16[8,16,128]{2,1,0:T(8,128)(2,1)S(1)}, u32[]{:S(2)}, u32[]{:S(2)}) collective-permute-start(bf16[8,16,128]{2,1,0:T(8,128)(2,1)S(1)} %get-tuple-element.40), channel_id=1, source_target_pairs={{1,0},{2,1},{3,2},{4,3},{5,4},{6,5},{7,6},{9,8},{10,9},{11,10},{12... | collective-permute-start | bytes 98312 | tf_op jit(solution)/shard_map/ppermute | solution.py:716
  3.1 5.5 %collective-permute-start = (bf16[8,16,128]{2,1,0:T(8,128)(2,1)S(1)}, bf16[8,16,128]{2,1,0:T(8,128)(2,1)S(1)}, u32[]{:S(2)}, u32[]{:S(2)}) collective-permute-start(bf16[8,16,128]{2,1,0:T(8,128)(2,1)S(1)} %get-tuple-element.40), channel_id=1, source_target_pairs={{0,1},{1,2},{2,3},{3,4},{4,5},{5,6},{6,7},{8,9},{9,10},{10,11},{11... | collective-permute-start | bytes 98312 | tf_op jit(solution)/shard_map/ppermute | solution.py:716
  8.6 1.0 collective-permute-done.before_ref
  9.6 1.3 %collective-permute-start.3 = (bf16[8,6,16,128]{3,2,1,0:T(8,128)(2,1)S(1)}, bf16[8,6,16,128]{3,2,1,0:T(8,128)(2,1)S(1)}, u32[]{:S(2)}, u32[]{:S(2)}) collective-permute-start(bf16[8,6,16,128]{3,2,1,0:T(8,128)(2,1)S(1)} %shard_map.59), channel_id=1, source_target_pairs={{64,0},{128,64},{192,128},{256,192},{320,256},{384,320},{448,384},... | collective-permute-start | bytes 589832 | tf_op jit(solution)/shard_map/ppermute | solution.py:716
  10.9 4.0 %collective-permute-start.2 = (bf16[8,6,16,128]{3,2,1,0:T(8,128)(2,1)S(1)}, bf16[8,6,16,128]{3,2,1,0:T(8,128)(2,1)S(1)}, u32[]{:S(2)}, u32[]{:S(2)}) collective-permute-start(bf16[8,6,16,128]{3,2,1,0:T(8,128)(2,1)S(1)} %shard_map.59), channel_id=1, source_target_pairs={{0,64},{64,128},{128,192},{192,256},{256,320},{320,384},{384,448},... | collective-permute-start | bytes 589832 | tf_op jit(solution)/shard_map/ppermute | solution.py:716
  14.9 1.1 collective-permute-done.3
  16.0 1.5 %collective-permute-done.2 = bf16[8,6,16,128]{3,2,1,0:T(8,128)(2,1)S(1)} collective-permute-done((bf16[8,6,16,128]{3,2,1,0:T(8,128)(2,1)S(1)}, bf16[8,6,16,128]{3,2,1,0:T(8,128)(2,1)S(1)}, u32[]{:S(2)}, u32[]{:S(2)}) %collective-permute-start.2) | collective-permute-done | bytes 196640 | tf_op jit(solution)/shard_map/ppermute | solution.py:716
  17.6 0.1 shard_map.60
  17.7 5.7 %collective-permute-start.4 = (bf16[15,6,16,128]{3,2,1,0:T(8,128)(2,1)S(1)}, bf16[15,6,16,128]{3,2,1,0:T(8,128)(2,1)S(1)}, u32[]{:S(2)}, u32[]{:S(2)}) collective-permute-start(bf16[15,6,16,128]{3,2,1,0:T(8,128)(2,1)S(1)} %get-tuple-element.41), channel_id=1, source_target_pairs={{0,8},{8,16},{16,24},{24,32},{32,40},{40,48},{48,56},{1,9},{9,17},... | collective-permute-start | bytes 1105928 | tf_op jit(solution)/shard_map/ppermute | solution.py:716
  23.4 5.2 %collective-permute-start.5 = (bf16[15,6,16,128]{3,2,1,0:T(8,128)(2,1)S(1)}, bf16[15,6,16,128]{3,2,1,0:T(8,128)(2,1)S(1)}, u32[]{:S(2)}, u32[]{:S(2)}) collective-permute-start(bf16[15,6,16,128]{3,2,1,0:T(8,128)(2,1)S(1)} %get-tuple-element.42), channel_id=1, source_target_pairs={{8,0},{16,8},{24,16},{32,24},{40,32},{48,40},{56,48},{9,1},{17,9},... | collective-permute-start | bytes 1105928 | tf_op jit(solution)/shard_map/ppermute | solution.py:716
  28.6 3.6 %collective-permute-done.5.yp_ref = bf16[15,6,16,128]{3,2,1,0:T(8,128)(2,1)S(1)} collective-permute-done((bf16[15,6,16,128]{3,2,1,0:T(8,128)(2,1)S(1)}, bf16[15,6,16,128]{3,2,1,0:T(8,128)(2,1)S(1)}, u32[]{:S(2)}, u32[]{:S(2)}) %collective-permute-start.5) | collective-permute-done | bytes 368672 | tf_op jit(solution)/shard_map/ppermute | solution.py:716
  32.2 2.3 %shard_map.62 = (f32[6,24,128]{2,1,0:T(8,128)S(1)}, f32[6,24,128]{2,1,0:T(8,128)S(1)}, f32[64,8,128]{2,1,0:T(8,128)}) custom-call(bf16[24,6,16,128]{3,2,1,0:T(8,128)(2,1)S(1)} %pad_maximum_fusion.x_ref, bf16[15,6,16,128]{3,2,1,0:T(8,128)(2,1)S(1)} %collective-permute-done.4.ym_ref, bf16[15,6,16,128]{3,2,1,0:T(8,128)(2,1)S(1)} %collective-permute-done.5.yp_ref), custom_call_target="tpu_custom_call" | custom-call | tf_op jit(solution)/shard_map/pallas_call | solution.py:704
  34.5 12.1 %all-to-all-start = ((f32[64,1,1024]{2,1,0:T(1,128)}), f32[64,1,1024]{2,1,0:T(1,128)S(1)}, u32[]{:S(2)}, u32[]{:S(2)}) async-start(f32[64,1,1024]{2,1,0:T(1,128)} %bitcast), calls=%async_computation | async-start | bytes 524288 | tf_op jit(solution)/shard_map/all_to_all | solution.py:721
  46.6 3.3 %collective-permute-start.6 = (f32[6,24,128]{2,1,0:T(8,128)S(1)}, f32[6,24,128]{2,1,0:T(8,128)S(1)}, u32[]{:S(2)}, u32[]{:S(2)}) collective-permute-start(f32[6,24,128]{2,1,0:T(8,128)S(1)} %get-tuple-element.55), channel_id=1, source_target_pairs={{0,64},{64,128},{128,192},{192,256},{256,320},{320,384},{384,448},... | collective-permute-start | bytes 221192 | tf_op jit(solution)/shard_map/ppermute | solution.py:716
  49.9 1.3 %collective-permute-start.7 = (f32[6,24,128]{2,1,0:T(8,128)S(1)}, f32[6,24,128]{2,1,0:T(8,128)S(1)}, u32[]{:S(2)}, u32[]{:S(2)}) collective-permute-start(f32[6,24,128]{2,1,0:T(8,128)S(1)} %get-tuple-element.56), channel_id=1, source_target_pairs={{64,0},{128,64},{192,128},{256,192},{320,256},{384,320},{448,384},... | collective-permute-start | bytes 221192 | tf_op jit(solution)/shard_map/ppermute | solution.py:716
  51.2 1.6 %collective-permute-done.6.low_ref = f32[6,24,128]{2,1,0:T(8,128)S(1)} collective-permute-done((f32[6,24,128]{2,1,0:T(8,128)S(1)}, f32[6,24,128]{2,1,0:T(8,128)S(1)}, u32[]{:S(2)}, u32[]{:S(2)}) %collective-permute-start.6) | collective-permute-done | bytes 73760 | tf_op jit(solution)/shard_map/ppermute | solution.py:716
  52.8 2.6 %collective-permute-done.7.high_ref = f32[6,24,128]{2,1,0:T(8,128)S(1)} collective-permute-done((f32[6,24,128]{2,1,0:T(8,128)S(1)}, f32[6,24,128]{2,1,0:T(8,128)S(1)}, u32[]{:S(2)}, u32[]{:S(2)}) %collective-permute-start.7) | collective-permute-done | bytes 73760 | tf_op jit(solution)/shard_map/ppermute | solution.py:716
  55.5 4.3 %all-to-all-done = f32[64,1,1024]{2,1,0:T(1,128)S(1)} async-done(((f32[64,1,1024]{2,1,0:T(1,128)}), f32[64,1,1024]{2,1,0:T(1,128)S(1)}, u32[]{:S(2)}, u32[]{:S(2)}) %all-to-all-start) | async-done | bytes 262176 | tf_op jit(solution)/shard_map/all_to_all | solution.py:721
  59.8 4.0 %collective-permute-start.8 = (f32[32,8,128]{2,1,0:T(8,128)S(1)}, f32[32,8,128]{2,1,0:T(8,128)S(1)}, u32[]{:S(2)}, u32[]{:S(2)}) collective-permute-start(f32[32,8,128]{2,1,0:T(8,128)S(1)} %bitcast.10), channel_id=1, source_target_pairs={{0,1},{1,2},{2,3},{3,4},{4,5},{5,6},{6,7},{8,9},{9,10},{10,11},{11... | collective-permute-start | bytes 393224 | tf_op jit(solution)/shard_map/ppermute | solution.py:716
  63.8 1.3 %collective-permute-start.9 = (f32[32,8,128]{2,1,0:T(8,128)S(1)}, f32[32,8,128]{2,1,0:T(8,128)S(1)}, u32[]{:S(2)}, u32[]{:S(2)}) collective-permute-start(f32[32,8,128]{2,1,0:T(8,128)S(1)} %bitcast.8), channel_id=1, source_target_pairs={{1,0},{2,1},{3,2},{4,3},{5,4},{6,5},{7,6},{9,8},{10,9},{11,10},{12... | collective-permute-start | bytes 393224 | tf_op jit(solution)/shard_map/ppermute | solution.py:716
  65.1 3.2 %shard_map.61 = (f32[24,40,256]{2,1,0:T(8,128)S(1)}, f32[25,40,256]{2,1,0:T(8,128)S(1)}, f32[24,40,256]{2,1,0:T(8,128)S(1)}, f32[24,40,256]{2,1,0:T(8,128)S(1)},...) custom-call(bf16[24,6,16,128]{3,2,1,0:T(8,128)(2,1)S(1)} %pad_maximu, ...), custom_call_target="tpu_custom_call" | custom-call | tf_op jit(solution)/shard_map/pallas_call | solution.py:704
  68.3 2.9 %collective-permute-done.9.after_ref = f32[32,8,128]{2,1,0:T(8,128)S(1)} collective-permute-done((f32[32,8,128]{2,1,0:T(8,128)S(1)}, f32[32,8,128]{2,1,0:T(8,128)S(1)}, u32[]{:S(2)}, u32[]{:S(2)}) %collective-permute-start.9) | collective-permute-done | bytes 131104 | tf_op jit(solution)/shard_map/ppermute | solution.py:716
  71.2 4.7 %shard_map.63 = (f32[8,16,128]{2,1,0:T(8,128)S(1)}, f32[8,16,128]{2,1,0:T(8,128)S(1)}, f32[24,40,256]{2,1,0:T(8,128)S(1)}, f32[16,24,128]{2,1,0:T(8,128)S(1)}, f...) custom-call(f32[24,40,256]{2,1,0:T(8,128)S(1)} %get-tuple-element.51, ...), custom_call_target="tpu_custom_call" | custom-call | tf_op jit(solution)/shard_map/pallas_call | solution.py:704
  75.9 18.1 %all_to_all.15 = f32[64,1,512]{2,1,0:T(1,128)S(1)} all-to-all(f32[64,1,512]{2,1,0:T(1,128)S(1)} %bitcast.17), channel_id=1, replica_groups=mesh['gx'=8,'gy'=8,'gz'=8] {'gx','gy'}, dimensions={0} | all-to-all | bytes 262144 | tf_op jit(solution)/shard_map/all_to_all | solution.py:721
  94.0 0.1 fusion.1
  94.1 1.3 %collective-permute-start.11 = (f32[8,8,128]{2,1,0:T(8,128)S(1)}, f32[8,8,128]{2,1,0:T(8,128)S(1)}, u32[]{:S(2)}, u32[]{:S(2)}) collective-permute-start(f32[8,8,128]{2,1,0:T(8,128)S(1)} %bitcast.13), channel_id=1, source_target_pairs={{1,0},{2,1},{3,2},{4,3},{5,4},{6,5},{7,6},{9,8},{10,9},{11,10},{12... | collective-permute-start | bytes 98312 | tf_op jit(solution)/shard_map/ppermute | solution.py:716
  95.4 5.8 %collective-permute-start.10 = (f32[8,8,128]{2,1,0:T(8,128)S(1)}, f32[8,8,128]{2,1,0:T(8,128)S(1)}, u32[]{:S(2)}, u32[]{:S(2)}) collective-permute-start(f32[8,8,128]{2,1,0:T(8,128)S(1)} %bitcast.15), channel_id=1, source_target_pairs={{0,1},{1,2},{2,3},{3,4},{4,5},{5,6},{6,7},{8,9},{9,10},{10,11},{11... | collective-permute-start | bytes 98312 | tf_op jit(solution)/shard_map/ppermute | solution.py:716
  101.2 1.0 collective-permute-done.10.before_ref
  102.2 2.1 %shard_map.64 = (f32[8,16,128]{2,1,0:T(8,128)S(1)}, f32[1,128]{1,0:T(1,128)S(1)}) custom-call(f32[25,40,256]{2,1,0:T(8,128)S(1)} %get-tuple-element.43.f0_ref, f32[24,40,256]{2,1,0:T(8,128)S(1)} %get-tuple-element.44.f1_ref, f32[24,40,256]{2,1,0:T(8,128)S(1)} %get-tuple-element.45.f2_ref, f32[24,40,256]{2,1,0:T(8,128)S(1)} %get-tuple-element.46.w_ref, ...), custom_call_target="tpu_custom_call" | custom-call | tf_op jit(solution)/shard_map/pallas_call | solution.py:704
  104.3 18.6 %all_to_all.16.sums_ref = f32[8,1,128]{2,1,0:T(1,128)S(1)} all-to-all(f32[8,1,128]{2,1,0:T(1,128)S(1)} %broadcast_in_dim.9), channel_id=1, replica_groups=mesh['gx'=8,'gy'=8,'gz'=8] {'gz'}, dimensions={0} | all-to-all | bytes 8192 | tf_op jit(solution)/shard_map/all_to_all | solution.py:798
  122.9 0.8 shard_map.65
  (10 shorter events, 0.2 us)
Async XLA Ops:
  1.8 6.8 %collective-permute-start.1 = (bf16[8,16,128]{2,1,0:T(8,128)(2,1)S(1)}, bf16[8,16,128]{2,1,0:T(8,128)(2,1)S(1)}, u32[]{:S(2)}, u32[]{:S(2)}) collective-permute-start(bf16[8,16,128]{2,1,0:T(8,128)(2,1)S(1)} %get-tuple-element.40), channel_id=1, source_target_pairs={{1,0},{2,1},{3,2},{4,3},{5,4},{6,5},{7,6},{9,8},{10,9},{11,10},{12... | collective-permute-start | bytes 98312 | tf_op jit(solution)/shard_map/ppermute | solution.py:716
  3.1 6.5 %collective-permute-start = (bf16[8,16,128]{2,1,0:T(8,128)(2,1)S(1)}, bf16[8,16,128]{2,1,0:T(8,128)(2,1)S(1)}, u32[]{:S(2)}, u32[]{:S(2)}) collective-permute-start(bf16[8,16,128]{2,1,0:T(8,128)(2,1)S(1)} %get-tuple-element.40), channel_id=1, source_target_pairs={{0,1},{1,2},{2,3},{3,4},{4,5},{5,6},{6,7},{8,9},{9,10},{10,11},{11... | collective-permute-start | bytes 98312 | tf_op jit(solution)/shard_map/ppermute | solution.py:716
  9.6 6.4 %collective-permute-start.3 = (bf16[8,6,16,128]{3,2,1,0:T(8,128)(2,1)S(1)}, bf16[8,6,16,128]{3,2,1,0:T(8,128)(2,1)S(1)}, u32[]{:S(2)}, u32[]{:S(2)}) collective-permute-start(bf16[8,6,16,128]{3,2,1,0:T(8,128)(2,1)S(1)} %shard_map.59), channel_id=1, source_target_pairs={{64,0},{128,64},{192,128},{256,192},{320,256},{384,320},{448,384},... | collective-permute-start | bytes 589832 | tf_op jit(solution)/shard_map/ppermute | solution.py:716
  10.9 6.6 %collective-permute-start.2 = (bf16[8,6,16,128]{3,2,1,0:T(8,128)(2,1)S(1)}, bf16[8,6,16,128]{3,2,1,0:T(8,128)(2,1)S(1)}, u32[]{:S(2)}, u32[]{:S(2)}) collective-permute-start(bf16[8,6,16,128]{3,2,1,0:T(8,128)(2,1)S(1)} %shard_map.59), channel_id=1, source_target_pairs={{0,64},{64,128},{128,192},{192,256},{256,320},{320,384},{384,448},... | collective-permute-start | bytes 589832 | tf_op jit(solution)/shard_map/ppermute | solution.py:716
  17.7 10.9 %collective-permute-start.4 = (bf16[15,6,16,128]{3,2,1,0:T(8,128)(2,1)S(1)}, bf16[15,6,16,128]{3,2,1,0:T(8,128)(2,1)S(1)}, u32[]{:S(2)}, u32[]{:S(2)}) collective-permute-start(bf16[15,6,16,128]{3,2,1,0:T(8,128)(2,1)S(1)} %get-tuple-element.41), channel_id=1, source_target_pairs={{0,8},{8,16},{16,24},{24,32},{32,40},{40,48},{48,56},{1,9},{9,17},... | collective-permute-start | bytes 1105928 | tf_op jit(solution)/shard_map/ppermute | solution.py:716
  23.4 8.8 %collective-permute-start.5 = (bf16[15,6,16,128]{3,2,1,0:T(8,128)(2,1)S(1)}, bf16[15,6,16,128]{3,2,1,0:T(8,128)(2,1)S(1)}, u32[]{:S(2)}, u32[]{:S(2)}) collective-permute-start(bf16[15,6,16,128]{3,2,1,0:T(8,128)(2,1)S(1)} %get-tuple-element.42), channel_id=1, source_target_pairs={{8,0},{16,8},{24,16},{32,24},{40,32},{48,40},{56,48},{9,1},{17,9},... | collective-permute-start | bytes 1105928 | tf_op jit(solution)/shard_map/ppermute | solution.py:716
  34.5 25.2 %all-to-all-start = ((f32[64,1,1024]{2,1,0:T(1,128)}), f32[64,1,1024]{2,1,0:T(1,128)S(1)}, u32[]{:S(2)}, u32[]{:S(2)}) async-start(f32[64,1,1024]{2,1,0:T(1,128)} %bitcast), calls=%async_computation | async-start | bytes 524288 | tf_op jit(solution)/shard_map/all_to_all | solution.py:721
  46.6 6.2 %collective-permute-start.6 = (f32[6,24,128]{2,1,0:T(8,128)S(1)}, f32[6,24,128]{2,1,0:T(8,128)S(1)}, u32[]{:S(2)}, u32[]{:S(2)}) collective-permute-start(f32[6,24,128]{2,1,0:T(8,128)S(1)} %get-tuple-element.55), channel_id=1, source_target_pairs={{0,64},{64,128},{128,192},{192,256},{256,320},{320,384},{384,448},... | collective-permute-start | bytes 221192 | tf_op jit(solution)/shard_map/ppermute | solution.py:716
  49.9 5.6 %collective-permute-start.7 = (f32[6,24,128]{2,1,0:T(8,128)S(1)}, f32[6,24,128]{2,1,0:T(8,128)S(1)}, u32[]{:S(2)}, u32[]{:S(2)}) collective-permute-start(f32[6,24,128]{2,1,0:T(8,128)S(1)} %get-tuple-element.56), channel_id=1, source_target_pairs={{64,0},{128,64},{192,128},{256,192},{320,256},{384,320},{448,384},... | collective-permute-start | bytes 221192 | tf_op jit(solution)/shard_map/ppermute | solution.py:716
  59.8 8.5 %collective-permute-start.8 = (f32[32,8,128]{2,1,0:T(8,128)S(1)}, f32[32,8,128]{2,1,0:T(8,128)S(1)}, u32[]{:S(2)}, u32[]{:S(2)}) collective-permute-start(f32[32,8,128]{2,1,0:T(8,128)S(1)} %bitcast.10), channel_id=1, source_target_pairs={{0,1},{1,2},{2,3},{3,4},{4,5},{5,6},{6,7},{8,9},{9,10},{10,11},{11... | collective-permute-start | bytes 393224 | tf_op jit(solution)/shard_map/ppermute | solution.py:716
  63.8 7.4 %collective-permute-start.9 = (f32[32,8,128]{2,1,0:T(8,128)S(1)}, f32[32,8,128]{2,1,0:T(8,128)S(1)}, u32[]{:S(2)}, u32[]{:S(2)}) collective-permute-start(f32[32,8,128]{2,1,0:T(8,128)S(1)} %bitcast.8), channel_id=1, source_target_pairs={{1,0},{2,1},{3,2},{4,3},{5,4},{6,5},{7,6},{9,8},{10,9},{11,10},{12... | collective-permute-start | bytes 393224 | tf_op jit(solution)/shard_map/ppermute | solution.py:716
  94.1 7.1 %collective-permute-start.11 = (f32[8,8,128]{2,1,0:T(8,128)S(1)}, f32[8,8,128]{2,1,0:T(8,128)S(1)}, u32[]{:S(2)}, u32[]{:S(2)}) collective-permute-start(f32[8,8,128]{2,1,0:T(8,128)S(1)} %bitcast.13), channel_id=1, source_target_pairs={{1,0},{2,1},{3,2},{4,3},{5,4},{6,5},{7,6},{9,8},{10,9},{11,10},{12... | collective-permute-start | bytes 98312 | tf_op jit(solution)/shard_map/ppermute | solution.py:716
  95.4 6.8 %collective-permute-start.10 = (f32[8,8,128]{2,1,0:T(8,128)S(1)}, f32[8,8,128]{2,1,0:T(8,128)S(1)}, u32[]{:S(2)}, u32[]{:S(2)}) collective-permute-start(f32[8,8,128]{2,1,0:T(8,128)S(1)} %bitcast.15), channel_id=1, source_target_pairs={{0,1},{1,2},{2,3},{3,4},{4,5},{5,6},{6,7},{8,9},{9,10},{10,11},{11... | collective-permute-start | bytes 98312 | tf_op jit(solution)/shard_map/ppermute | solution.py:716
  102.2 20.7 %copy-start = (f32[8,16,128]{2,1,0:T(8,128)S(1)}, f32[8,16,128]{2,1,0:T(8,128)}, u32[]{:S(2)}) copy-start(f32[8,16,128]{2,1,0:T(8,128)} %s_ref.1) | copy-start | bytes 196612

commit v8 on v7

--- a/solution.py
+++ b/solution.py
@@ -195,7 +195,7 @@
     return jnp.concatenate([far_before, near_before], 0), jnp.concatenate([near_after, far_after], 0)
 
 
-def fine_kernel(thin, x_ref, ym_ref, yp_ref, *refs):
+def fine_kernel(thin, x_ref, yp_ref, ym_ref, *refs):
     if thin:
         (up_ref, down_ref, pay_ref,
          s_ref, f0_ref, f1_ref, f2_ref, s1_ref, f10_ref, f11_ref, f12_ref, w1_ref, *refs) = refs
@@ -750,7 +750,7 @@
     )
     up, down, pay = call(
         functools.partial(fine_kernel, True),
-        [block, before, after],
+        [block, after, before],
         [(edge, F32), (edge, F32), ((lax.axis_size(("gx", "gy")), 8, 128), F32)],
         [slim, slim_up, slim, slim, slim_mid, slim_mid_up, slim_mid, slim_mid, slim_mid,
          slim, slim, slim, slim, (2, 24, 128), slim_rows, slim_rows, slim_rows, slim_rows,
@@ -758,7 +758,7 @@
     )
     state = call(
         functools.partial(fine_kernel, False),
-        [block, before, after],
+        [block, after, before],
         [(shape, F32) for shape in (fine, fine_up, fine, fine, fine, fine, mid, mid_up, mid, mid, mid)],
         [fine, fine, fine, fine, (2, 40, 128), rows, rows, rows, rows, mid, mid, mid],
         keep_out=range(11),

time: 125 us -> 124 us (level)
  starting transfers between devices: 52 us -> 50.3 us
    all_to_all x1, starting transfers between devices: 12.1 us -> 9.7 us  [gather_plane(): return lax.all_to_all(copies, ('gx', 'gy'), 0, 0, tiled=True)]
where the time goes in v8:
time: 124 us; the launch traced here: 123 us
  starting transfers between devices  50.3 us (41%)
  blocking collectives  36.7 us (30%)
  waiting for transfers between devices  20.4 us (16%)
  Pallas kernels  14.4 us (12%)
    ppermute x12, starting transfers between devices, shift_along(): lax.ppermute(value, axis, [(i, i + by) for i in range(size) if 0 <= i + b...  40.6 us
    all_to_all x1, blocking collectives, local(): lax.all_to_all(jnp.broadcast_to(sums[None], (peers, 1, 128)), 'gz', 0, 0,...  18.6 us
    all_to_all x1, blocking collectives, gather_plane(): return lax.all_to_all(copies, ('gx', 'gy'), 0, 0, tiled=True)  18.1 us
    ppermute x12, waiting for transfers between devices, shift_along(): lax.ppermute(value, axis, [(i, i + by) for i in range(size) if 0 <= i + b...  16.2 us
    pallas_call x8, Pallas kernels, call(): pl.pallas_call(kernel, out_shape=shapes, in_specs=[pl.BlockSpec(memory_sp...  14.4 us
    all_to_all x1, starting transfers between devices, gather_plane(): return lax.all_to_all(copies, ('gx', 'gy'), 0, 0, tiled=True)  9.7 us
    all_to_all x1, waiting for transfers between devices, gather_plane(): return lax.all_to_all(copies, ('gx', 'gy'), 0, 0, tiled=True)  4.28 us
  transfers between devices with their start and end apart: 13, of which 9 were waited for; matrix products, arithmetic and copies ran while one was open for 0% of the time, Pallas kernels for 3%

profile of v8, /device:TPU:1, one launch (start us, length us, event | category | flops | bytes accessed | tf_op | source)
XLA Modules:
  0.0 122.8 jit_solution(15312609254936313854)
XLA Ops:
  0.6 1.2 shard_map.58
  1.8 1.3 %collective-permute-start.1 = (bf16[8,16,128]{2,1,0:T(8,128)(2,1)S(1)}, bf16[8,16,128]{2,1,0:T(8,128)(2,1)S(1)}, u32[]{:S(2)}, u32[]{:S(2)}) collective-permute-start(bf16[8,16,128]{2,1,0:T(8,128)(2,1)S(1)} %get-tuple-element.40), channel_id=1, source_target_pairs={{1,0},{2,1},{3,2},{4,3},{5,4},{6,5},{7,6},{9,8},{10,9},{11,10},{12... | collective-permute-start | bytes 98312 | tf_op jit(solution)/shard_map/ppermute | solution.py:716
  3.1 5.5 %collective-permute-start = (bf16[8,16,128]{2,1,0:T(8,128)(2,1)S(1)}, bf16[8,16,128]{2,1,0:T(8,128)(2,1)S(1)}, u32[]{:S(2)}, u32[]{:S(2)}) collective-permute-start(bf16[8,16,128]{2,1,0:T(8,128)(2,1)S(1)} %get-tuple-element.40), channel_id=1, source_target_pairs={{0,1},{1,2},{2,3},{3,4},{4,5},{5,6},{6,7},{8,9},{9,10},{10,11},{11... | collective-permute-start | bytes 98312 | tf_op jit(solution)/shard_map/ppermute | solution.py:716
  8.6 1.0 collective-permute-done.before_ref
  9.6 1.3 %collective-permute-start.3 = (bf16[8,6,16,128]{3,2,1,0:T(8,128)(2,1)S(1)}, bf16[8,6,16,128]{3,2,1,0:T(8,128)(2,1)S(1)}, u32[]{:S(2)}, u32[]{:S(2)}) collective-permute-start(bf16[8,6,16,128]{3,2,1,0:T(8,128)(2,1)S(1)} %shard_map.59), channel_id=1, source_target_pairs={{64,0},{128,64},{192,128},{256,192},{320,256},{384,320},{448,384},... | collective-permute-start | bytes 589832 | tf_op jit(solution)/shard_map/ppermute | solution.py:716
  10.9 4.0 %collective-permute-start.2 = (bf16[8,6,16,128]{3,2,1,0:T(8,128)(2,1)S(1)}, bf16[8,6,16,128]{3,2,1,0:T(8,128)(2,1)S(1)}, u32[]{:S(2)}, u32[]{:S(2)}) collective-permute-start(bf16[8,6,16,128]{3,2,1,0:T(8,128)(2,1)S(1)} %shard_map.59), channel_id=1, source_target_pairs={{0,64},{64,128},{128,192},{192,256},{256,320},{320,384},{384,448},... | collective-permute-start | bytes 589832 | tf_op jit(solution)/shard_map/ppermute | solution.py:716
  14.9 1.1 collective-permute-done.3
  16.0 1.5 %collective-permute-done.2 = bf16[8,6,16,128]{3,2,1,0:T(8,128)(2,1)S(1)} collective-permute-done((bf16[8,6,16,128]{3,2,1,0:T(8,128)(2,1)S(1)}, bf16[8,6,16,128]{3,2,1,0:T(8,128)(2,1)S(1)}, u32[]{:S(2)}, u32[]{:S(2)}) %collective-permute-start.2) | collective-permute-done | bytes 196640 | tf_op jit(solution)/shard_map/ppermute | solution.py:716
  17.6 0.1 shard_map.60
  17.7 9.6 %collective-permute-start.4 = (bf16[15,6,16,128]{3,2,1,0:T(8,128)(2,1)S(1)}, bf16[15,6,16,128]{3,2,1,0:T(8,128)(2,1)S(1)}, u32[]{:S(2)}, u32[]{:S(2)}) collective-permute-start(bf16[15,6,16,128]{3,2,1,0:T(8,128)(2,1)S(1)} %get-tuple-element.41), channel_id=1, source_target_pairs={{8,0},{16,8},{24,16},{32,24},{40,32},{48,40},{56,48},{9,1},{17,9},... | collective-permute-start | bytes 1105928 | tf_op jit(solution)/shard_map/ppermute | solution.py:716
  27.3 1.9 %collective-permute-start.5 = (bf16[15,6,16,128]{3,2,1,0:T(8,128)(2,1)S(1)}, bf16[15,6,16,128]{3,2,1,0:T(8,128)(2,1)S(1)}, u32[]{:S(2)}, u32[]{:S(2)}) collective-permute-start(bf16[15,6,16,128]{3,2,1,0:T(8,128)(2,1)S(1)} %get-tuple-element.42), channel_id=1, source_target_pairs={{0,8},{8,16},{16,24},{24,32},{32,40},{40,48},{48,56},{1,9},{9,17},... | collective-permute-start | bytes 1105928 | tf_op jit(solution)/shard_map/ppermute | solution.py:716
  29.3 4.4 %collective-permute-done.5.ym_ref = bf16[15,6,16,128]{3,2,1,0:T(8,128)(2,1)S(1)} collective-permute-done((bf16[15,6,16,128]{3,2,1,0:T(8,128)(2,1)S(1)}, bf16[15,6,16,128]{3,2,1,0:T(8,128)(2,1)S(1)}, u32[]{:S(2)}, u32[]{:S(2)}) %collective-permute-start.5) | collective-permute-done | bytes 368672 | tf_op jit(solution)/shard_map/ppermute | solution.py:716
  33.7 2.3 %shard_map.62 = (f32[6,24,128]{2,1,0:T(8,128)S(1)}, f32[6,24,128]{2,1,0:T(8,128)S(1)}, f32[64,8,128]{2,1,0:T(8,128)}) custom-call(bf16[24,6,16,128]{3,2,1,0:T(8,128)(2,1)S(1)} %pad_maximum_fusion.x_ref, bf16[15,6,16,128]{3,2,1,0:T(8,128)(2,1)S(1)} %collective-permute-done.4.yp_ref, bf16[15,6,16,128]{3,2,1,0:T(8,128)(2,1)S(1)} %collective-permute-done.5.ym_ref), custom_call_target="tpu_custom_call" | custom-call | tf_op jit(solution)/shard_map/pallas_call | solution.py:704
  36.0 9.7 %all-to-all-start = ((f32[64,1,1024]{2,1,0:T(1,128)}), f32[64,1,1024]{2,1,0:T(1,128)S(1)}, u32[]{:S(2)}, u32[]{:S(2)}) async-start(f32[64,1,1024]{2,1,0:T(1,128)} %bitcast), calls=%async_computation | async-start | bytes 524288 | tf_op jit(solution)/shard_map/all_to_all | solution.py:721
  45.7 3.3 %collective-permute-start.6 = (f32[6,24,128]{2,1,0:T(8,128)S(1)}, f32[6,24,128]{2,1,0:T(8,128)S(1)}, u32[]{:S(2)}, u32[]{:S(2)}) collective-permute-start(f32[6,24,128]{2,1,0:T(8,128)S(1)} %get-tuple-element.55), channel_id=1, source_target_pairs={{0,64},{64,128},{128,192},{192,256},{256,320},{320,384},{384,448},... | collective-permute-start | bytes 221192 | tf_op jit(solution)/shard_map/ppermute | solution.py:716
  49.0 1.3 %collective-permute-start.7 = (f32[6,24,128]{2,1,0:T(8,128)S(1)}, f32[6,24,128]{2,1,0:T(8,128)S(1)}, u32[]{:S(2)}, u32[]{:S(2)}) collective-permute-start(f32[6,24,128]{2,1,0:T(8,128)S(1)} %get-tuple-element.56), channel_id=1, source_target_pairs={{64,0},{128,64},{192,128},{256,192},{320,256},{384,320},{448,384},... | collective-permute-start | bytes 221192 | tf_op jit(solution)/shard_map/ppermute | solution.py:716
  50.3 1.6 %collective-permute-done.6.low_ref = f32[6,24,128]{2,1,0:T(8,128)S(1)} collective-permute-done((f32[6,24,128]{2,1,0:T(8,128)S(1)}, f32[6,24,128]{2,1,0:T(8,128)S(1)}, u32[]{:S(2)}, u32[]{:S(2)}) %collective-permute-start.6) | collective-permute-done | bytes 73760 | tf_op jit(solution)/shard_map/ppermute | solution.py:716
  51.9 2.6 %collective-permute-done.7.high_ref = f32[6,24,128]{2,1,0:T(8,128)S(1)} collective-permute-done((f32[6,24,128]{2,1,0:T(8,128)S(1)}, f32[6,24,128]{2,1,0:T(8,128)S(1)}, u32[]{:S(2)}, u32[]{:S(2)}) %collective-permute-start.7) | collective-permute-done | bytes 73760 | tf_op jit(solution)/shard_map/ppermute | solution.py:716
  54.5 4.3 %all-to-all-done = f32[64,1,1024]{2,1,0:T(1,128)S(1)} async-done(((f32[64,1,1024]{2,1,0:T(1,128)}), f32[64,1,1024]{2,1,0:T(1,128)S(1)}, u32[]{:S(2)}, u32[]{:S(2)}) %all-to-all-start) | async-done | bytes 262176 | tf_op jit(solution)/shard_map/all_to_all | solution.py:721
  58.9 4.0 %collective-permute-start.8 = (f32[32,8,128]{2,1,0:T(8,128)S(1)}, f32[32,8,128]{2,1,0:T(8,128)S(1)}, u32[]{:S(2)}, u32[]{:S(2)}) collective-permute-start(f32[32,8,128]{2,1,0:T(8,128)S(1)} %bitcast.10), channel_id=1, source_target_pairs={{0,1},{1,2},{2,3},{3,4},{4,5},{5,6},{6,7},{8,9},{9,10},{10,11},{11... | collective-permute-start | bytes 393224 | tf_op jit(solution)/shard_map/ppermute | solution.py:716
  62.9 1.3 %collective-permute-start.9 = (f32[32,8,128]{2,1,0:T(8,128)S(1)}, f32[32,8,128]{2,1,0:T(8,128)S(1)}, u32[]{:S(2)}, u32[]{:S(2)}) collective-permute-start(f32[32,8,128]{2,1,0:T(8,128)S(1)} %bitcast.8), channel_id=1, source_target_pairs={{1,0},{2,1},{3,2},{4,3},{5,4},{6,5},{7,6},{9,8},{10,9},{11,10},{12... | collective-permute-start | bytes 393224 | tf_op jit(solution)/shard_map/ppermute | solution.py:716
  64.2 3.2 %shard_map.61 = (f32[24,40,256]{2,1,0:T(8,128)S(1)}, f32[25,40,256]{2,1,0:T(8,128)S(1)}, f32[24,40,256]{2,1,0:T(8,128)S(1)}, f32[24,40,256]{2,1,0:T(8,128)S(1)},...) custom-call(bf16[24,6,16,128]{3,2,1,0:T(8,128)(2,1)S(1)} %pad_maximu, ...), custom_call_target="tpu_custom_call" | custom-call | tf_op jit(solution)/shard_map/pallas_call | solution.py:704
  67.4 2.9 %collective-permute-done.9.after_ref = f32[32,8,128]{2,1,0:T(8,128)S(1)} collective-permute-done((f32[32,8,128]{2,1,0:T(8,128)S(1)}, f32[32,8,128]{2,1,0:T(8,128)S(1)}, u32[]{:S(2)}, u32[]{:S(2)}) %collective-permute-start.9) | collective-permute-done | bytes 131104 | tf_op jit(solution)/shard_map/ppermute | solution.py:716
  70.3 4.7 %shard_map.63 = (f32[8,16,128]{2,1,0:T(8,128)S(1)}, f32[8,16,128]{2,1,0:T(8,128)S(1)}, f32[24,40,256]{2,1,0:T(8,128)S(1)}, f32[16,24,128]{2,1,0:T(8,128)S(1)}, f...) custom-call(f32[24,40,256]{2,1,0:T(8,128)S(1)} %get-tuple-element.51, ...), custom_call_target="tpu_custom_call" | custom-call | tf_op jit(solution)/shard_map/pallas_call | solution.py:704
  75.0 18.1 %all_to_all.15 = f32[64,1,512]{2,1,0:T(1,128)S(1)} all-to-all(f32[64,1,512]{2,1,0:T(1,128)S(1)} %bitcast.17), channel_id=1, replica_groups=mesh['gx'=8,'gy'=8,'gz'=8] {'gx','gy'}, dimensions={0} | all-to-all | bytes 262144 | tf_op jit(solution)/shard_map/all_to_all | solution.py:721
  93.1 0.1 fusion.1
  93.2 1.3 %collective-permute-start.11 = (f32[8,8,128]{2,1,0:T(8,128)S(1)}, f32[8,8,128]{2,1,0:T(8,128)S(1)}, u32[]{:S(2)}, u32[]{:S(2)}) collective-permute-start(f32[8,8,128]{2,1,0:T(8,128)S(1)} %bitcast.13), channel_id=1, source_target_pairs={{1,0},{2,1},{3,2},{4,3},{5,4},{6,5},{7,6},{9,8},{10,9},{11,10},{12... | collective-permute-start | bytes 98312 | tf_op jit(solution)/shard_map/ppermute | solution.py:716
  94.5 5.8 %collective-permute-start.10 = (f32[8,8,128]{2,1,0:T(8,128)S(1)}, f32[8,8,128]{2,1,0:T(8,128)S(1)}, u32[]{:S(2)}, u32[]{:S(2)}) collective-permute-start(f32[8,8,128]{2,1,0:T(8,128)S(1)} %bitcast.15), channel_id=1, source_target_pairs={{0,1},{1,2},{2,3},{3,4},{4,5},{5,6},{6,7},{8,9},{9,10},{10,11},{11... | collective-permute-start | bytes 98312 | tf_op jit(solution)/shard_map/ppermute | solution.py:716
  100.3 1.0 collective-permute-done.10.before_ref
  101.3 2.1 %shard_map.64 = (f32[8,16,128]{2,1,0:T(8,128)S(1)}, f32[1,128]{1,0:T(1,128)S(1)}) custom-call(f32[25,40,256]{2,1,0:T(8,128)S(1)} %get-tuple-element.43.f0_ref, f32[24,40,256]{2,1,0:T(8,128)S(1)} %get-tuple-element.44.f1_ref, f32[24,40,256]{2,1,0:T(8,128)S(1)} %get-tuple-element.45.f2_ref, f32[24,40,256]{2,1,0:T(8,128)S(1)} %get-tuple-element.46.w_ref, ...), custom_call_target="tpu_custom_call" | custom-call | tf_op jit(solution)/shard_map/pallas_call | solution.py:704
  103.4 18.6 %all_to_all.16.sums_ref = f32[8,1,128]{2,1,0:T(1,128)S(1)} all-to-all(f32[8,1,128]{2,1,0:T(1,128)S(1)} %broadcast_in_dim.9), channel_id=1, replica_groups=mesh['gx'=8,'gy'=8,'gz'=8] {'gz'}, dimensions={0} | all-to-all | bytes 8192 | tf_op jit(solution)/shard_map/all_to_all | solution.py:798
  122.0 0.8 shard_map.65
  (10 shorter events, 0.2 us)
Async XLA Ops:
  1.8 6.8 %collective-permute-start.1 = (bf16[8,16,128]{2,1,0:T(8,128)(2,1)S(1)}, bf16[8,16,128]{2,1,0:T(8,128)(2,1)S(1)}, u32[]{:S(2)}, u32[]{:S(2)}) collective-permute-start(bf16[8,16,128]{2,1,0:T(8,128)(2,1)S(1)} %get-tuple-element.40), channel_id=1, source_target_pairs={{1,0},{2,1},{3,2},{4,3},{5,4},{6,5},{7,6},{9,8},{10,9},{11,10},{12... | collective-permute-start | bytes 98312 | tf_op jit(solution)/shard_map/ppermute | solution.py:716
  3.1 6.5 %collective-permute-start = (bf16[8,16,128]{2,1,0:T(8,128)(2,1)S(1)}, bf16[8,16,128]{2,1,0:T(8,128)(2,1)S(1)}, u32[]{:S(2)}, u32[]{:S(2)}) collective-permute-start(bf16[8,16,128]{2,1,0:T(8,128)(2,1)S(1)} %get-tuple-element.40), channel_id=1, source_target_pairs={{0,1},{1,2},{2,3},{3,4},{4,5},{5,6},{6,7},{8,9},{9,10},{10,11},{11... | collective-permute-start | bytes 98312 | tf_op jit(solution)/shard_map/ppermute | solution.py:716
  9.6 6.4 %collective-permute-start.3 = (bf16[8,6,16,128]{3,2,1,0:T(8,128)(2,1)S(1)}, bf16[8,6,16,128]{3,2,1,0:T(8,128)(2,1)S(1)}, u32[]{:S(2)}, u32[]{:S(2)}) collective-permute-start(bf16[8,6,16,128]{3,2,1,0:T(8,128)(2,1)S(1)} %shard_map.59), channel_id=1, source_target_pairs={{64,0},{128,64},{192,128},{256,192},{320,256},{384,320},{448,384},... | collective-permute-start | bytes 589832 | tf_op jit(solution)/shard_map/ppermute | solution.py:716
  10.9 6.6 %collective-permute-start.2 = (bf16[8,6,16,128]{3,2,1,0:T(8,128)(2,1)S(1)}, bf16[8,6,16,128]{3,2,1,0:T(8,128)(2,1)S(1)}, u32[]{:S(2)}, u32[]{:S(2)}) collective-permute-start(bf16[8,6,16,128]{3,2,1,0:T(8,128)(2,1)S(1)} %shard_map.59), channel_id=1, source_target_pairs={{0,64},{64,128},{128,192},{192,256},{256,320},{320,384},{384,448},... | collective-permute-start | bytes 589832 | tf_op jit(solution)/shard_map/ppermute | solution.py:716
  17.7 11.5 %collective-permute-start.4 = (bf16[15,6,16,128]{3,2,1,0:T(8,128)(2,1)S(1)}, bf16[15,6,16,128]{3,2,1,0:T(8,128)(2,1)S(1)}, u32[]{:S(2)}, u32[]{:S(2)}) collective-permute-start(bf16[15,6,16,128]{3,2,1,0:T(8,128)(2,1)S(1)} %get-tuple-element.41), channel_id=1, source_target_pairs={{8,0},{16,8},{24,16},{32,24},{40,32},{48,40},{56,48},{9,1},{17,9},... | collective-permute-start | bytes 1105928 | tf_op jit(solution)/shard_map/ppermute | solution.py:716
  27.3 6.4 %collective-permute-start.5 = (bf16[15,6,16,128]{3,2,1,0:T(8,128)(2,1)S(1)}, bf16[15,6,16,128]{3,2,1,0:T(8,128)(2,1)S(1)}, u32[]{:S(2)}, u32[]{:S(2)}) collective-permute-start(bf16[15,6,16,128]{3,2,1,0:T(8,128)(2,1)S(1)} %get-tuple-element.42), channel_id=1, source_target_pairs={{0,8},{8,16},{16,24},{24,32},{32,40},{40,48},{48,56},{1,9},{9,17},... | collective-permute-start | bytes 1105928 | tf_op jit(solution)/shard_map/ppermute | solution.py:716
  36.0 22.9 %all-to-all-start = ((f32[64,1,1024]{2,1,0:T(1,128)}), f32[64,1,1024]{2,1,0:T(1,128)S(1)}, u32[]{:S(2)}, u32[]{:S(2)}) async-start(f32[64,1,1024]{2,1,0:T(1,128)} %bitcast), calls=%async_computation | async-start | bytes 524288 | tf_op jit(solution)/shard_map/all_to_all | solution.py:721
  45.7 6.2 %collective-permute-start.6 = (f32[6,24,128]{2,1,0:T(8,128)S(1)}, f32[6,24,128]{2,1,0:T(8,128)S(1)}, u32[]{:S(2)}, u32[]{:S(2)}) collective-permute-start(f32[6,24,128]{2,1,0:T(8,128)S(1)} %get-tuple-element.55), channel_id=1, source_target_pairs={{0,64},{64,128},{128,192},{192,256},{256,320},{320,384},{384,448},... | collective-permute-start | bytes 221192 | tf_op jit(solution)/shard_map/ppermute | solution.py:716
  49.0 5.6 %collective-permute-start.7 = (f32[6,24,128]{2,1,0:T(8,128)S(1)}, f32[6,24,128]{2,1,0:T(8,128)S(1)}, u32[]{:S(2)}, u32[]{:S(2)}) collective-permute-start(f32[6,24,128]{2,1,0:T(8,128)S(1)} %get-tuple-element.56), channel_id=1, source_target_pairs={{64,0},{128,64},{192,128},{256,192},{320,256},{384,320},{448,384},... | collective-permute-start | bytes 221192 | tf_op jit(solution)/shard_map/ppermute | solution.py:716
  58.9 8.5 %collective-permute-start.8 = (f32[32,8,128]{2,1,0:T(8,128)S(1)}, f32[32,8,128]{2,1,0:T(8,128)S(1)}, u32[]{:S(2)}, u32[]{:S(2)}) collective-permute-start(f32[32,8,128]{2,1,0:T(8,128)S(1)} %bitcast.10), channel_id=1, source_target_pairs={{0,1},{1,2},{2,3},{3,4},{4,5},{5,6},{6,7},{8,9},{9,10},{10,11},{11... | collective-permute-start | bytes 393224 | tf_op jit(solution)/shard_map/ppermute | solution.py:716
  62.9 7.4 %collective-permute-start.9 = (f32[32,8,128]{2,1,0:T(8,128)S(1)}, f32[32,8,128]{2,1,0:T(8,128)S(1)}, u32[]{:S(2)}, u32[]{:S(2)}) collective-permute-start(f32[32,8,128]{2,1,0:T(8,128)S(1)} %bitcast.8), channel_id=1, source_target_pairs={{1,0},{2,1},{3,2},{4,3},{5,4},{6,5},{7,6},{9,8},{10,9},{11,10},{12... | collective-permute-start | bytes 393224 | tf_op jit(solution)/shard_map/ppermute | solution.py:716
  93.2 7.1 %collective-permute-start.11 = (f32[8,8,128]{2,1,0:T(8,128)S(1)}, f32[8,8,128]{2,1,0:T(8,128)S(1)}, u32[]{:S(2)}, u32[]{:S(2)}) collective-permute-start(f32[8,8,128]{2,1,0:T(8,128)S(1)} %bitcast.13), channel_id=1, source_target_pairs={{1,0},{2,1},{3,2},{4,3},{5,4},{6,5},{7,6},{9,8},{10,9},{11,10},{12... | collective-permute-start | bytes 98312 | tf_op jit(solution)/shard_map/ppermute | solution.py:716
  94.5 6.9 %collective-permute-start.10 = (f32[8,8,128]{2,1,0:T(8,128)S(1)}, f32[8,8,128]{2,1,0:T(8,128)S(1)}, u32[]{:S(2)}, u32[]{:S(2)}) collective-permute-start(f32[8,8,128]{2,1,0:T(8,128)S(1)} %bitcast.15), channel_id=1, source_target_pairs={{0,1},{1,2},{2,3},{3,4},{4,5},{5,6},{6,7},{8,9},{9,10},{10,11},{11... | collective-permute-start | bytes 98312 | tf_op jit(solution)/shard_map/ppermute | solution.py:716
  101.3 20.7 %copy-start = (f32[8,16,128]{2,1,0:T(8,128)S(1)}, f32[8,16,128]{2,1,0:T(8,128)}, u32[]{:S(2)}) copy-start(f32[8,16,128]{2,1,0:T(8,128)} %s_ref.1) | copy-start | bytes 196612

commit v9 on v8

--- a/solution.py
+++ b/solution.py
@@ -322,10 +322,8 @@
     sm1_ref, t1_ref, u_ref,
 ):
     for target, start in ((up_ref, 5), (down_ref, 9)):
-        target[...] = jnp.zeros_like(target)
-        for i, ref in enumerate((s1_ref, w1_ref, f10_ref)):
-            for k in range(2):
-                target[2 * i + k, pl.ds(4, 12), :] = ref[start + k, pl.ds(0, 12), :]
+        for i, (ref, k) in enumerate(((s1_ref, 0), (s1_ref, 1), (w1_ref, 0), (w1_ref, 1), (f10_ref, 1))):
+            target[i] = ref[start + k]
     for p in range(5, 11):
         sm1_ref[p] = w1_ref[p] * s1_ref[p]
 
@@ -452,11 +450,11 @@
 def second_kernel(
     s_ref, f0_ref, f1_ref, f2_ref, w_ref, d_ref,
     s1_ref, f10_ref, f11_ref, f12_ref, w1_ref,
-    low_ref, high_ref, before_ref, own0_ref, own1_ref, after_ref,
+    low_in, high_in, before_ref, own0_ref, own1_ref, after_ref,
     fp_out, im_out, im_ref, t1s_ref, f20_ref, f21_ref, f22_ref, w2_ref,
     f30_ref, f31_ref, f32_ref, w3_ref, pay_ref,
     v_ref, t3_ref, e_ref, m2_ref, pick_ref, corr1_ref, m1_ref, wide_ref, t_ref,
-    corr_ref, fp_ref, sm_ref, rs_ref, sm1_ref, tq_ref,
+    corr_ref, fp_ref, sm_ref, rs_ref, sm1_ref, tq_ref, low_ref, high_ref,
 ):
     nx2, ny2 = f20_ref.shape[:2]
     lane8 = iota((8, 128), 1)
@@ -493,6 +491,9 @@
         corr1_ref[p] = w1_ref[p] * s1_ref[p] + pick_ref[lax.shift_right_logical(p, 1)]
         return carry
 
+    for target, source in ((low_ref, low_in), (high_ref, high_in)):
+        target[...] = jnp.zeros_like(target)
+        target[:, pl.ds(4, 12), :] = source[:, pl.ds(0, 12), :]
     lax.fori_loop(3, 13, correct_1, 0, unroll=10)
     for k in range(2):
         corr1_ref[1 + k] = low_ref[2 + k] * low_ref[k] + pick_ref[(1 + k) // 2]
@@ -506,8 +507,8 @@
 
     lax.fori_loop(3, 13, relax_1, 0, unroll=10)
     for p, source, w, face, next_face in (
-        (2, low_ref[1], low_ref[3], low_ref[5], f10_ref[3]),
-        (13, high_ref[0], high_ref[2], f10_ref[13], high_ref[5]),
+        (2, low_ref[1], low_ref[3], low_ref[4], f10_ref[3]),
+        (13, high_ref[0], high_ref[2], f10_ref[13], high_ref[4]),
     ):
         m1_ref[p] = KEEP * corr1_ref[p] + w * (
             source + face * corr1_ref[p - 1] + next_face * corr1_ref[p + 1]
@@ -744,7 +745,7 @@
 
     fine, fine_up = (24, 40, 256), (25, 40, 256)
     mid, mid_up = (16, 24, 128), (17, 24, 128)
-    rows, wide, edge = (12, 24, 256), (16, 24, 256), (6, 24, 128)
+    rows, wide, edge = (12, 24, 256), (16, 24, 256), (5, 16, 128)
     slim, slim_up, slim_mid, slim_mid_up, slim_rows = (
         (20, 24, 256), (21, 24, 256), (16, 16, 128), (17, 16, 128), (12, 16, 256)
     )
@@ -778,7 +779,7 @@
         [((8, 16, 128), F32)] * 2
         + [(shape, F32) for shape in (fine, mid, *[level_2] * 4, *[level_3] * 4, (nx2 * ny2 // 8, 4, 128))],
         [(4,) + level_2, half, half, window, (8, 24, 128), mid, mid, wide, (2, 40, 128),
-         fine, fine, fine, (8, 24, 256), mid, (32, 128)],
+         fine, fine, fine, (8, 24, 256), mid, (32, 128), (5, 24, 128), (5, 24, 128)],
         keep_in=range(11),
         keep_out=range(2, 12),
     )

time: 124 us -> 124 us (level)
  no operation moved by 1% of the time
where the time goes in v9:
time: 124 us; the launch traced here: 122 us
  starting transfers between devices  50.3 us (41%)
  blocking collectives  36.3 us (29%)
  waiting for transfers between devices  20.4 us (16%)
  Pallas kernels  14.4 us (12%)
    ppermute x12, starting transfers between devices, shift_along(): lax.ppermute(value, axis, [(i, i + by) for i in range(size) if 0 <= i + b...  40.6 us
    all_to_all x1, blocking collectives, local(): lax.all_to_all(jnp.broadcast_to(sums[None], (peers, 1, 128)), 'gz', 0, 0,...  18.6 us
    all_to_all x1, blocking collectives, gather_plane(): return lax.all_to_all(copies, ('gx', 'gy'), 0, 0, tiled=True)  17.8 us
    ppermute x12, waiting for transfers between devices, shift_along(): lax.ppermute(value, axis, [(i, i + by) for i in range(size) if 0 <= i + b...  15.8 us
    pallas_call x8, Pallas kernels, call(): pl.pallas_call(kernel, out_shape=shapes, in_specs=[pl.BlockSpec(memory_sp...  14.4 us
    all_to_all x1, starting transfers between devices, gather_plane(): return lax.all_to_all(copies, ('gx', 'gy'), 0, 0, tiled=True)  9.7 us
    all_to_all x1, waiting for transfers between devices, gather_plane(): return lax.all_to_all(copies, ('gx', 'gy'), 0, 0, tiled=True)  4.63 us
  transfers between devices with their start and end apart: 13, of which 9 were waited for; matrix products, arithmetic and copies ran while one was open for 0% of the time, Pallas kernels for 3%

profile of v9, /device:TPU:1, one launch (start us, length us, event | category | flops | bytes accessed | tf_op | source)
XLA Modules:
  0.0 122.4 jit_solution(3692472082320430023)
XLA Ops:
  0.6 1.2 shard_map.58
  1.8 1.3 %collective-permute-start.1 = (bf16[8,16,128]{2,1,0:T(8,128)(2,1)S(1)}, bf16[8,16,128]{2,1,0:T(8,128)(2,1)S(1)}, u32[]{:S(2)}, u32[]{:S(2)}) collective-permute-start(bf16[8,16,128]{2,1,0:T(8,128)(2,1)S(1)} %get-tuple-element.40), channel_id=1, source_target_pairs={{1,0},{2,1},{3,2},{4,3},{5,4},{6,5},{7,6},{9,8},{10,9},{11,10},{12... | collective-permute-start | bytes 98312 | tf_op jit(solution)/shard_map/ppermute | solution.py:717
  3.1 5.5 %collective-permute-start = (bf16[8,16,128]{2,1,0:T(8,128)(2,1)S(1)}, bf16[8,16,128]{2,1,0:T(8,128)(2,1)S(1)}, u32[]{:S(2)}, u32[]{:S(2)}) collective-permute-start(bf16[8,16,128]{2,1,0:T(8,128)(2,1)S(1)} %get-tuple-element.40), channel_id=1, source_target_pairs={{0,1},{1,2},{2,3},{3,4},{4,5},{5,6},{6,7},{8,9},{9,10},{10,11},{11... | collective-permute-start | bytes 98312 | tf_op jit(solution)/shard_map/ppermute | solution.py:717
  8.6 1.0 collective-permute-done.before_ref
  9.6 1.3 %collective-permute-start.3 = (bf16[8,6,16,128]{3,2,1,0:T(8,128)(2,1)S(1)}, bf16[8,6,16,128]{3,2,1,0:T(8,128)(2,1)S(1)}, u32[]{:S(2)}, u32[]{:S(2)}) collective-permute-start(bf16[8,6,16,128]{3,2,1,0:T(8,128)(2,1)S(1)} %shard_map.59), channel_id=1, source_target_pairs={{64,0},{128,64},{192,128},{256,192},{320,256},{384,320},{448,384},... | collective-permute-start | bytes 589832 | tf_op jit(solution)/shard_map/ppermute | solution.py:717
  10.9 4.0 %collective-permute-start.2 = (bf16[8,6,16,128]{3,2,1,0:T(8,128)(2,1)S(1)}, bf16[8,6,16,128]{3,2,1,0:T(8,128)(2,1)S(1)}, u32[]{:S(2)}, u32[]{:S(2)}) collective-permute-start(bf16[8,6,16,128]{3,2,1,0:T(8,128)(2,1)S(1)} %shard_map.59), channel_id=1, source_target_pairs={{0,64},{64,128},{128,192},{192,256},{256,320},{320,384},{384,448},... | collective-permute-start | bytes 589832 | tf_op jit(solution)/shard_map/ppermute | solution.py:717
  14.9 1.1 collective-permute-done.3
  16.0 1.5 %collective-permute-done.2 = bf16[8,6,16,128]{3,2,1,0:T(8,128)(2,1)S(1)} collective-permute-done((bf16[8,6,16,128]{3,2,1,0:T(8,128)(2,1)S(1)}, bf16[8,6,16,128]{3,2,1,0:T(8,128)(2,1)S(1)}, u32[]{:S(2)}, u32[]{:S(2)}) %collective-permute-start.2) | collective-permute-done | bytes 196640 | tf_op jit(solution)/shard_map/ppermute | solution.py:717
  17.6 0.1 shard_map.60
  17.7 9.6 %collective-permute-start.4 = (bf16[15,6,16,128]{3,2,1,0:T(8,128)(2,1)S(1)}, bf16[15,6,16,128]{3,2,1,0:T(8,128)(2,1)S(1)}, u32[]{:S(2)}, u32[]{:S(2)}) collective-permute-start(bf16[15,6,16,128]{3,2,1,0:T(8,128)(2,1)S(1)} %get-tuple-element.41), channel_id=1, source_target_pairs={{8,0},{16,8},{24,16},{32,24},{40,32},{48,40},{56,48},{9,1},{17,9},... | collective-permute-start | bytes 1105928 | tf_op jit(solution)/shard_map/ppermute | solution.py:717
  27.3 1.9 %collective-permute-start.5 = (bf16[15,6,16,128]{3,2,1,0:T(8,128)(2,1)S(1)}, bf16[15,6,16,128]{3,2,1,0:T(8,128)(2,1)S(1)}, u32[]{:S(2)}, u32[]{:S(2)}) collective-permute-start(bf16[15,6,16,128]{3,2,1,0:T(8,128)(2,1)S(1)} %get-tuple-element.42), channel_id=1, source_target_pairs={{0,8},{8,16},{16,24},{24,32},{32,40},{40,48},{48,56},{1,9},{9,17},... | collective-permute-start | bytes 1105928 | tf_op jit(solution)/shard_map/ppermute | solution.py:717
  29.3 4.4 %collective-permute-done.5.ym_ref = bf16[15,6,16,128]{3,2,1,0:T(8,128)(2,1)S(1)} collective-permute-done((bf16[15,6,16,128]{3,2,1,0:T(8,128)(2,1)S(1)}, bf16[15,6,16,128]{3,2,1,0:T(8,128)(2,1)S(1)}, u32[]{:S(2)}, u32[]{:S(2)}) %collective-permute-start.5) | collective-permute-done | bytes 368672 | tf_op jit(solution)/shard_map/ppermute | solution.py:717
  33.7 2.2 %shard_map.62 = (f32[5,16,128]{2,1,0:T(8,128)S(1)}, f32[5,16,128]{2,1,0:T(8,128)S(1)}, f32[64,8,128]{2,1,0:T(8,128)}) custom-call(bf16[24,6,16,128]{3,2,1,0:T(8,128)(2,1)S(1)} %pad_maximum_fusion.x_ref, bf16[15,6,16,128]{3,2,1,0:T(8,128)(2,1)S(1)} %collective-permute-done.4.yp_ref, bf16[15,6,16,128]{3,2,1,0:T(8,128)(2,1)S(1)} %collective-permute-done.5.ym_ref), custom_call_target="tpu_custom_call" | custom-call | tf_op jit(solution)/shard_map/pallas_call | solution.py:705
  35.9 9.7 %all-to-all-start = ((f32[64,1,1024]{2,1,0:T(1,128)}), f32[64,1,1024]{2,1,0:T(1,128)S(1)}, u32[]{:S(2)}, u32[]{:S(2)}) async-start(f32[64,1,1024]{2,1,0:T(1,128)} %bitcast), calls=%async_computation | async-start | bytes 524288 | tf_op jit(solution)/shard_map/all_to_all | solution.py:722
  45.6 3.3 %collective-permute-start.6 = (f32[5,16,128]{2,1,0:T(8,128)S(1)}, f32[5,16,128]{2,1,0:T(8,128)S(1)}, u32[]{:S(2)}, u32[]{:S(2)}) collective-permute-start(f32[5,16,128]{2,1,0:T(8,128)S(1)} %get-tuple-element.55), channel_id=1, source_target_pairs={{0,64},{64,128},{128,192},{192,256},{256,320},{320,384},{384,448},... | collective-permute-start | bytes 122888 | tf_op jit(solution)/shard_map/ppermute | solution.py:717
  48.9 1.3 %collective-permute-start.7 = (f32[5,16,128]{2,1,0:T(8,128)S(1)}, f32[5,16,128]{2,1,0:T(8,128)S(1)}, u32[]{:S(2)}, u32[]{:S(2)}) collective-permute-start(f32[5,16,128]{2,1,0:T(8,128)S(1)} %get-tuple-element.56), channel_id=1, source_target_pairs={{64,0},{128,64},{192,128},{256,192},{320,256},{384,320},{448,384},... | collective-permute-start | bytes 122888 | tf_op jit(solution)/shard_map/ppermute | solution.py:717
  50.2 0.2 collective-permute-done.6.low_in
  50.4 3.7 %collective-permute-done.7.high_in = f32[5,16,128]{2,1,0:T(8,128)S(1)} collective-permute-done((f32[5,16,128]{2,1,0:T(8,128)S(1)}, f32[5,16,128]{2,1,0:T(8,128)S(1)}, u32[]{:S(2)}, u32[]{:S(2)}) %collective-permute-start.7) | collective-permute-done | bytes 40992 | tf_op jit(solution)/shard_map/ppermute | solution.py:717
  54.2 4.6 %all-to-all-done = f32[64,1,1024]{2,1,0:T(1,128)S(1)} async-done(((f32[64,1,1024]{2,1,0:T(1,128)}), f32[64,1,1024]{2,1,0:T(1,128)S(1)}, u32[]{:S(2)}, u32[]{:S(2)}) %all-to-all-start) | async-done | bytes 262176 | tf_op jit(solution)/shard_map/all_to_all | solution.py:722
  58.9 4.0 %collective-permute-start.8 = (f32[32,8,128]{2,1,0:T(8,128)S(1)}, f32[32,8,128]{2,1,0:T(8,128)S(1)}, u32[]{:S(2)}, u32[]{:S(2)}) collective-permute-start(f32[32,8,128]{2,1,0:T(8,128)S(1)} %bitcast.10), channel_id=1, source_target_pairs={{0,1},{1,2},{2,3},{3,4},{4,5},{5,6},{6,7},{8,9},{9,10},{10,11},{11... | collective-permute-start | bytes 393224 | tf_op jit(solution)/shard_map/ppermute | solution.py:717
  62.9 1.3 %collective-permute-start.9 = (f32[32,8,128]{2,1,0:T(8,128)S(1)}, f32[32,8,128]{2,1,0:T(8,128)S(1)}, u32[]{:S(2)}, u32[]{:S(2)}) collective-permute-start(f32[32,8,128]{2,1,0:T(8,128)S(1)} %bitcast.8), channel_id=1, source_target_pairs={{1,0},{2,1},{3,2},{4,3},{5,4},{6,5},{7,6},{9,8},{10,9},{11,10},{12... | collective-permute-start | bytes 393224 | tf_op jit(solution)/shard_map/ppermute | solution.py:717
  64.2 3.2 %shard_map.61 = (f32[24,40,256]{2,1,0:T(8,128)S(1)}, f32[25,40,256]{2,1,0:T(8,128)S(1)}, f32[24,40,256]{2,1,0:T(8,128)S(1)}, f32[24,40,256]{2,1,0:T(8,128)S(1)},...) custom-call(bf16[24,6,16,128]{3,2,1,0:T(8,128)(2,1)S(1)} %pad_maximu, ...), custom_call_target="tpu_custom_call" | custom-call | tf_op jit(solution)/shard_map/pallas_call | solution.py:705
  67.4 2.9 %collective-permute-done.9.after_ref = f32[32,8,128]{2,1,0:T(8,128)S(1)} collective-permute-done((f32[32,8,128]{2,1,0:T(8,128)S(1)}, f32[32,8,128]{2,1,0:T(8,128)S(1)}, u32[]{:S(2)}, u32[]{:S(2)}) %collective-permute-start.9) | collective-permute-done | bytes 131104 | tf_op jit(solution)/shard_map/ppermute | solution.py:717
  70.2 4.7 %shard_map.63 = (f32[8,16,128]{2,1,0:T(8,128)S(1)}, f32[8,16,128]{2,1,0:T(8,128)S(1)}, f32[24,40,256]{2,1,0:T(8,128)S(1)}, f32[16,24,128]{2,1,0:T(8,128)S(1)}, f...) custom-call(f32[24,40,256]{2,1,0:T(8,128)S(1)} %get-tuple-element.51, ...), custom_call_target="tpu_custom_call" | custom-call | tf_op jit(solution)/shard_map/pallas_call | solution.py:705
  74.9 17.8 %all_to_all.15 = f32[64,1,512]{2,1,0:T(1,128)S(1)} all-to-all(f32[64,1,512]{2,1,0:T(1,128)S(1)} %bitcast.17), channel_id=1, replica_groups=mesh['gx'=8,'gy'=8,'gz'=8] {'gx','gy'}, dimensions={0} | all-to-all | bytes 262144 | tf_op jit(solution)/shard_map/all_to_all | solution.py:722
  92.7 0.1 fusion.1
  92.8 1.3 %collective-permute-start.11 = (f32[8,8,128]{2,1,0:T(8,128)S(1)}, f32[8,8,128]{2,1,0:T(8,128)S(1)}, u32[]{:S(2)}, u32[]{:S(2)}) collective-permute-start(f32[8,8,128]{2,1,0:T(8,128)S(1)} %bitcast.13), channel_id=1, source_target_pairs={{1,0},{2,1},{3,2},{4,3},{5,4},{6,5},{7,6},{9,8},{10,9},{11,10},{12... | collective-permute-start | bytes 98312 | tf_op jit(solution)/shard_map/ppermute | solution.py:717
  94.1 5.8 %collective-permute-start.10 = (f32[8,8,128]{2,1,0:T(8,128)S(1)}, f32[8,8,128]{2,1,0:T(8,128)S(1)}, u32[]{:S(2)}, u32[]{:S(2)}) collective-permute-start(f32[8,8,128]{2,1,0:T(8,128)S(1)} %bitcast.15), channel_id=1, source_target_pairs={{0,1},{1,2},{2,3},{3,4},{4,5},{5,6},{6,7},{8,9},{9,10},{10,11},{11... | collective-permute-start | bytes 98312 | tf_op jit(solution)/shard_map/ppermute | solution.py:717
  99.9 1.0 collective-permute-done.10.before_ref
  100.9 2.1 %shard_map.64 = (f32[8,16,128]{2,1,0:T(8,128)S(1)}, f32[1,128]{1,0:T(1,128)S(1)}) custom-call(f32[25,40,256]{2,1,0:T(8,128)S(1)} %get-tuple-element.43.f0_ref, f32[24,40,256]{2,1,0:T(8,128)S(1)} %get-tuple-element.44.f1_ref, f32[24,40,256]{2,1,0:T(8,128)S(1)} %get-tuple-element.45.f2_ref, f32[24,40,256]{2,1,0:T(8,128)S(1)} %get-tuple-element.46.w_ref, ...), custom_call_target="tpu_custom_call" | custom-call | tf_op jit(solution)/shard_map/pallas_call | solution.py:705
  103.0 18.6 %all_to_all.16.sums_ref = f32[8,1,128]{2,1,0:T(1,128)S(1)} all-to-all(f32[8,1,128]{2,1,0:T(1,128)S(1)} %broadcast_in_dim.9), channel_id=1, replica_groups=mesh['gx'=8,'gy'=8,'gz'=8] {'gz'}, dimensions={0} | all-to-all | bytes 8192 | tf_op jit(solution)/shard_map/all_to_all | solution.py:799
  121.6 0.8 shard_map.65
  (10 shorter events, 0.2 us)
Async XLA Ops:
  1.8 6.8 %collective-permute-start.1 = (bf16[8,16,128]{2,1,0:T(8,128)(2,1)S(1)}, bf16[8,16,128]{2,1,0:T(8,128)(2,1)S(1)}, u32[]{:S(2)}, u32[]{:S(2)}) collective-permute-start(bf16[8,16,128]{2,1,0:T(8,128)(2,1)S(1)} %get-tuple-element.40), channel_id=1, source_target_pairs={{1,0},{2,1},{3,2},{4,3},{5,4},{6,5},{7,6},{9,8},{10,9},{11,10},{12... | collective-permute-start | bytes 98312 | tf_op jit(solution)/shard_map/ppermute | solution.py:717
  3.1 6.5 %collective-permute-start = (bf16[8,16,128]{2,1,0:T(8,128)(2,1)S(1)}, bf16[8,16,128]{2,1,0:T(8,128)(2,1)S(1)}, u32[]{:S(2)}, u32[]{:S(2)}) collective-permute-start(bf16[8,16,128]{2,1,0:T(8,128)(2,1)S(1)} %get-tuple-element.40), channel_id=1, source_target_pairs={{0,1},{1,2},{2,3},{3,4},{4,5},{5,6},{6,7},{8,9},{9,10},{10,11},{11... | collective-permute-start | bytes 98312 | tf_op jit(solution)/shard_map/ppermute | solution.py:717
  9.6 6.4 %collective-permute-start.3 = (bf16[8,6,16,128]{3,2,1,0:T(8,128)(2,1)S(1)}, bf16[8,6,16,128]{3,2,1,0:T(8,128)(2,1)S(1)}, u32[]{:S(2)}, u32[]{:S(2)}) collective-permute-start(bf16[8,6,16,128]{3,2,1,0:T(8,128)(2,1)S(1)} %shard_map.59), channel_id=1, source_target_pairs={{64,0},{128,64},{192,128},{256,192},{320,256},{384,320},{448,384},... | collective-permute-start | bytes 589832 | tf_op jit(solution)/shard_map/ppermute | solution.py:717
  10.9 6.6 %collective-permute-start.2 = (bf16[8,6,16,128]{3,2,1,0:T(8,128)(2,1)S(1)}, bf16[8,6,16,128]{3,2,1,0:T(8,128)(2,1)S(1)}, u32[]{:S(2)}, u32[]{:S(2)}) collective-permute-start(bf16[8,6,16,128]{3,2,1,0:T(8,128)(2,1)S(1)} %shard_map.59), channel_id=1, source_target_pairs={{0,64},{64,128},{128,192},{192,256},{256,320},{320,384},{384,448},... | collective-permute-start | bytes 589832 | tf_op jit(solution)/shard_map/ppermute | solution.py:717
  17.7 11.5 %collective-permute-start.4 = (bf16[15,6,16,128]{3,2,1,0:T(8,128)(2,1)S(1)}, bf16[15,6,16,128]{3,2,1,0:T(8,128)(2,1)S(1)}, u32[]{:S(2)}, u32[]{:S(2)}) collective-permute-start(bf16[15,6,16,128]{3,2,1,0:T(8,128)(2,1)S(1)} %get-tuple-element.41), channel_id=1, source_target_pairs={{8,0},{16,8},{24,16},{32,24},{40,32},{48,40},{56,48},{9,1},{17,9},... | collective-permute-start | bytes 1105928 | tf_op jit(solution)/shard_map/ppermute | solution.py:717
  27.3 6.4 %collective-permute-start.5 = (bf16[15,6,16,128]{3,2,1,0:T(8,128)(2,1)S(1)}, bf16[15,6,16,128]{3,2,1,0:T(8,128)(2,1)S(1)}, u32[]{:S(2)}, u32[]{:S(2)}) collective-permute-start(bf16[15,6,16,128]{3,2,1,0:T(8,128)(2,1)S(1)} %get-tuple-element.42), channel_id=1, source_target_pairs={{0,8},{8,16},{16,24},{24,32},{32,40},{40,48},{48,56},{1,9},{9,17},... | collective-permute-start | bytes 1105928 | tf_op jit(solution)/shard_map/ppermute | solution.py:717
  35.9 22.9 %all-to-all-start = ((f32[64,1,1024]{2,1,0:T(1,128)}), f32[64,1,1024]{2,1,0:T(1,128)S(1)}, u32[]{:S(2)}, u32[]{:S(2)}) async-start(f32[64,1,1024]{2,1,0:T(1,128)} %bitcast), calls=%async_computation | async-start | bytes 524288 | tf_op jit(solution)/shard_map/all_to_all | solution.py:722
  45.6 4.8 %collective-permute-start.6 = (f32[5,16,128]{2,1,0:T(8,128)S(1)}, f32[5,16,128]{2,1,0:T(8,128)S(1)}, u32[]{:S(2)}, u32[]{:S(2)}) collective-permute-start(f32[5,16,128]{2,1,0:T(8,128)S(1)} %get-tuple-element.55), channel_id=1, source_target_pairs={{0,64},{64,128},{128,192},{192,256},{256,320},{320,384},{384,448},... | collective-permute-start | bytes 122888 | tf_op jit(solution)/shard_map/ppermute | solution.py:717
  48.9 5.2 %collective-permute-start.7 = (f32[5,16,128]{2,1,0:T(8,128)S(1)}, f32[5,16,128]{2,1,0:T(8,128)S(1)}, u32[]{:S(2)}, u32[]{:S(2)}) collective-permute-start(f32[5,16,128]{2,1,0:T(8,128)S(1)} %get-tuple-element.56), channel_id=1, source_target_pairs={{64,0},{128,64},{192,128},{256,192},{320,256},{384,320},{448,384},... | collective-permute-start | bytes 122888 | tf_op jit(solution)/shard_map/ppermute | solution.py:717
  58.9 8.5 %collective-permute-start.8 = (f32[32,8,128]{2,1,0:T(8,128)S(1)}, f32[32,8,128]{2,1,0:T(8,128)S(1)}, u32[]{:S(2)}, u32[]{:S(2)}) collective-permute-start(f32[32,8,128]{2,1,0:T(8,128)S(1)} %bitcast.10), channel_id=1, source_target_pairs={{0,1},{1,2},{2,3},{3,4},{4,5},{5,6},{6,7},{8,9},{9,10},{10,11},{11... | collective-permute-start | bytes 393224 | tf_op jit(solution)/shard_map/ppermute | solution.py:717
  62.9 7.4 %collective-permute-start.9 = (f32[32,8,128]{2,1,0:T(8,128)S(1)}, f32[32,8,128]{2,1,0:T(8,128)S(1)}, u32[]{:S(2)}, u32[]{:S(2)}) collective-permute-start(f32[32,8,128]{2,1,0:T(8,128)S(1)} %bitcast.8), channel_id=1, source_target_pairs={{1,0},{2,1},{3,2},{4,3},{5,4},{6,5},{7,6},{9,8},{10,9},{11,10},{12... | collective-permute-start | bytes 393224 | tf_op jit(solution)/shard_map/ppermute | solution.py:717
  92.8 7.1 %collective-permute-start.11 = (f32[8,8,128]{2,1,0:T(8,128)S(1)}, f32[8,8,128]{2,1,0:T(8,128)S(1)}, u32[]{:S(2)}, u32[]{:S(2)}) collective-permute-start(f32[8,8,128]{2,1,0:T(8,128)S(1)} %bitcast.13), channel_id=1, source_target_pairs={{1,0},{2,1},{3,2},{4,3},{5,4},{6,5},{7,6},{9,8},{10,9},{11,10},{12... | collective-permute-start | bytes 98312 | tf_op jit(solution)/shard_map/ppermute | solution.py:717
  94.1 6.8 %collective-permute-start.10 = (f32[8,8,128]{2,1,0:T(8,128)S(1)}, f32[8,8,128]{2,1,0:T(8,128)S(1)}, u32[]{:S(2)}, u32[]{:S(2)}) collective-permute-start(f32[8,8,128]{2,1,0:T(8,128)S(1)} %bitcast.15), channel_id=1, source_target_pairs={{0,1},{1,2},{2,3},{3,4},{4,5},{5,6},{6,7},{8,9},{9,10},{10,11},{11... | collective-permute-start | bytes 98312 | tf_op jit(solution)/shard_map/ppermute | solution.py:717
  100.9 20.7 %copy-start = (f32[8,16,128]{2,1,0:T(8,128)S(1)}, f32[8,16,128]{2,1,0:T(8,128)}, u32[]{:S(2)}) copy-start(f32[8,16,128]{2,1,0:T(8,128)} %s_ref.1) | copy-start | bytes 196612
